TPU v7x, 32 devices: a whole 2x2x4 slice. The times are simulated.
32 devices in a mesh: group: 2 (over y), expert: 4 (over z), dp: 4 (over x, core).
Axes of the slice: x: 2, y: 2, z: 4, core: 2. Of those that a mesh axis runs over, the one named last changes fastest.
Arguments:
- tokens: bfloat16 [1024, 3072], P(('group', 'expert'), 'dp'), parts along dimension 0, may hold values from -6 to 6
- cotangent: bfloat16 [1024, 3072], P(('group', 'expert'), 'dp'), parts along dimension 0, may hold values from -6 to 6
- routes: int32 [1024, 2], P(('group', 'expert')), parts along dimension 0, may hold values from 0 to 3, all different within a row; in each aligned block of 128 rows (0 to 127, 128 to 255, ...) at most 74 rows name the same one
- route_gates: float32 [1024, 2], P(('group', 'expert')), parts along dimension 0, may hold values from 0.1 to 1
- gate_weight: bfloat16 [4, 3072, 768], P('expert', 'dp'), may hold values from -0.109375 to 0.109375
- up_weight: bfloat16 [4, 3072, 768], P('expert', 'dp'), may hold values from -0.109375 to 0.109375
- down_weight: bfloat16 [4, 768, 3072], P('expert', None, 'dp'), may hold values from -0.21875 to 0.21875
Outputs:
- mixed: bfloat16 [1024, 3072], P(('group', 'expert'), 'dp'), parts along dimension 0
- grad_tokens: bfloat16 [1024, 3072], P(('group', 'expert'), 'dp'), parts along dimension 0
- grad_gates: float32 [1024, 2], P(('group', 'expert')), parts along dimension 0
- grad_gate_weight: bfloat16 [8, 3072, 768], P(('group', 'expert'), 'dp'), parts along dimension 0
- grad_up_weight: bfloat16 [8, 3072, 768], P(('group', 'expert'), 'dp'), parts along dimension 0
- grad_down_weight: bfloat16 [8, 768, 3072], P(('group', 'expert'), None, 'dp'), parts along dimension 0
There are 2 independent parts, one for each index of `group`. A program takes and returns all parts, laid end to end along the dimension named above; an argument that names none is the same for every part. Nothing has to cross between parts.
Inputs may be any that keep to these rules, and one draw needn't show every extreme that they name: `routes`: each row names 2 different experts. Among the 128 tokens of one index of expert no expert is named more than 74 times, and in some such block of tokens some expert is named exactly 74 times.
All inputs are finite; a program needn't handle non-finite values.
Results may differ from a plain program's by a relative error of at most 0.019.
Values may be sent and summed in bfloat16 or wider, within the bound.
No kernel may reach another device: no remote copies, remote signals or barrier semaphores. Data moves between devices by JAX's collectives and lax.ppermute only.
A program may use at most 64 MiB of HBM per device.

v0:
```python
import jax
import jax.numpy as jnp
from jax import lax
from jax.sharding import PartitionSpec as P


def swapped(block, axis, bit):
    count = lax.axis_size(axis)
    route = []
    for low in range(count):
        high = low | 1 << bit
        if high != low and high < count:
            route += [(low, high), (high, low)]
    return lax.ppermute(block, axis, route)


def slot_places(routes, expert_total, capacity):
    flat_routes = routes.reshape(-1)
    onehot = (flat_routes[:, None] == jnp.arange(expert_total, dtype=jnp.int32)[None, :]).astype(
        jnp.int32
    )
    before = jnp.cumsum(onehot, axis=0) - onehot
    slot_rank = jnp.sum(before * onehot, axis=1)
    return flat_routes * capacity + slot_rank


def xor_route(buffer, levels, sender):
    position = lax.axis_index("expert")
    for level in range(levels):
        stride = 1 << level
        layout = buffer.shape
        halves = buffer.reshape((layout[0] // (2 * stride), 2, stride) + layout[1:])
        upper_side = position >> level & 1
        other_side = 1 - upper_side
        leaving = lax.dynamic_slice_in_dim(halves, other_side, 1, 1)
        arrived = sender(leaving, level)
        zero_index = jnp.zeros_like(other_side)
        starts = (zero_index, other_side) + tuple((zero_index for extra in range(halves.ndim - 2)))
        halves = lax.dynamic_update_slice(halves, arrived, starts)
        buffer = halves.reshape(layout)
    return buffer


def activate(summed, hidden_width):
    gate_sum = summed[..., :hidden_width]
    up_sum = summed[..., hidden_width:]
    sigma = jax.nn.sigmoid(gate_sum)
    return (gate_sum * sigma * up_sum).astype(jnp.bfloat16)


def derive(summed, dhidden, hidden_width):
    gate_sum = summed[..., :hidden_width]
    up_sum = summed[..., hidden_width:]
    sigma = jax.nn.sigmoid(gate_sum)
    silu_value = gate_sum * sigma
    dgate = (dhidden * up_sum * sigma * (1.0 + gate_sum * (1.0 - sigma))).astype(jnp.bfloat16)
    dup = (dhidden * silu_value).astype(jnp.bfloat16)
    return (dgate, dup)


def shards(tokens, cotangent, routes, route_gates, gate_weight, up_weight, down_weight):
    expert_count = lax.axis_size("expert")
    levels = expert_count.bit_length() - 1
    tok_count, top_count = routes.shape
    local_experts, block_width, hidden_width = gate_weight.shape
    expert_total = local_experts * expert_count
    capacity = 7 * tok_count * top_count // (6 * expert_total)
    places = slot_places(routes, expert_total, capacity)
    owners = jnp.arange(tok_count * top_count, dtype=jnp.int32) // top_count
    scaled = (route_gates.reshape(-1)[:, None] * cotangent[owners].astype(jnp.float32)).astype(
        jnp.bfloat16
    )
    route_rows = jnp.concatenate([tokens[owners], scaled], axis=1)
    outbound = (
        jnp.zeros((expert_total * capacity, 2 * block_width), jnp.bfloat16)
        .at[places]
        .set(route_rows)
    )
    outbound = outbound.reshape(expert_count, local_experts * capacity, 2 * block_width)
    inbound = xor_route(outbound, levels, lambda portion, level: swapped(portion, "expert", level))
    inbound = inbound.reshape(expert_count, local_experts, capacity, 2 * block_width)
    expert_in = inbound[..., :block_width]
    expert_cot = inbound[..., block_width:]
    joint_weight = jnp.concatenate([gate_weight, up_weight], axis=2)
    summed = lax.psum(
        jnp.einsum(
            "sjcd,jdf->sjcf", expert_in, joint_weight, preferred_element_type=jnp.float32
        ).astype(jnp.bfloat16),
        "dp",
    ).astype(jnp.float32)
    hidden = activate(summed, hidden_width)
    dhidden = lax.psum(
        jnp.einsum(
            "sjcd,jfd->sjcf", expert_cot, down_weight, preferred_element_type=jnp.float32
        ).astype(jnp.bfloat16),
        "dp",
    ).astype(jnp.float32)
    dgate, dup = derive(summed, dhidden, hidden_width)
    expert_out = jnp.einsum(
        "sjcf,jfd->sjcd", hidden, down_weight, preferred_element_type=jnp.float32
    ).astype(jnp.bfloat16)
    grad_down = jnp.einsum(
        "sjcf,sjcd->jfd", hidden, expert_cot, preferred_element_type=jnp.float32
    ).astype(jnp.bfloat16)
    grad_gate = jnp.einsum(
        "sjcd,sjcf->jdf", expert_in, dgate, preferred_element_type=jnp.float32
    ).astype(jnp.bfloat16)
    grad_up = jnp.einsum(
        "sjcd,sjcf->jdf", expert_in, dup, preferred_element_type=jnp.float32
    ).astype(jnp.bfloat16)
    expert_dx = (
        jnp.einsum("sjcf,jdf->sjcd", dgate, gate_weight, preferred_element_type=jnp.float32)
        + jnp.einsum("sjcf,jdf->sjcd", dup, up_weight, preferred_element_type=jnp.float32)
    ).astype(jnp.bfloat16)
    returning = jnp.concatenate([expert_out, expert_dx], axis=3).reshape(
        expert_count, local_experts * capacity, 2 * block_width
    )
    returned = xor_route(
        returning, levels, lambda portion, level: swapped(portion, "expert", level)
    )
    gathered = returned.reshape(expert_total * capacity, 2 * block_width)[places]
    back_out = (
        gathered[:, :block_width].astype(jnp.float32).reshape(tok_count, top_count, block_width)
    )
    back_dx = (
        gathered[:, block_width:].astype(jnp.float32).reshape(tok_count, top_count, block_width)
    )
    mixed = jnp.sum(route_gates[:, :, None] * back_out, axis=1).astype(jnp.bfloat16)
    grad_tokens = jnp.sum(back_dx, axis=1).astype(jnp.bfloat16)
    partial_dots = jnp.sum(back_out * cotangent.astype(jnp.float32)[:, None, :], axis=2)
    grad_gates = lax.psum(partial_dots, "dp")
    return (mixed, grad_tokens, grad_gates, grad_gate, grad_up, grad_down)


def solution(mesh):
    in_specs = (
        P(("group", "expert"), "dp"),
        P(("group", "expert"), "dp"),
        P(("group", "expert"), None),
        P(("group", "expert"), None),
        P("expert", "dp", None),
        P("expert", "dp", None),
        P("expert", None, "dp"),
    )
    out_specs = (
        P(("group", "expert"), "dp"),
        P(("group", "expert"), "dp"),
        P(("group", "expert"), None),
        P(("group", "expert"), "dp", None),
        P(("group", "expert"), "dp", None),
        P(("group", "expert"), None, "dp"),
    )
    return jax.shard_map(shards, mesh=mesh, in_specs=in_specs, out_specs=out_specs, check_vma=False)
```

profile of v0, /device:TPU:0, one launch (start us, length us, event | category | flops | bytes accessed | tf_op | source)
XLA Modules:
  0.0 178.2 jit_solution(3588632078811233861)
XLA Ops:
  7.2 0.9 copy.19
  8.4 0.7 broadcast_multiply_fusion
  9.1 1.2 reduce-window.6
  11.0 0.8 copy.17
  11.8 0.6 copy-done.10
  12.6 1.2 gather_fusion.1
  13.8 1.9 %gather_fusion = bf16[256,768]{1,0:T(8,128)(2,1)} fusion(bf16[128,768]{1,0:T(8,128)(2,1)S(1)} %copy-done.2, s32[1024]{0:T(1024)S(1)} %pad_clamp_fusion.1), kind=kCustom, calls=%fused_computation | custom fusion | bytes 787456 | tf_op jit(solution)/shard_map/gather | solution.py:73
  15.9 2.7 %scatter_custom_fusion = bf16[296,1536]{1,0:T(8,128)(2,1)S(1)} fusion(s32[256]{0:T(256)S(1)} %bitcast.121, bf16[256,768]{1,0:T(8,128)(2,1)S(1)} %multiply_convert_fusion.1, bf16[]{:T(256)} %constant.49, bf16[256,768]{1,0:T(8,128)(2,1)} %gather_fusion, bf16[]{:T(256)} %constant.33.clone.1), kind=kCustom, calls=%fused_computation.37 | custom fusion | flops 1572864 | bytes 1695748 | tf_op jit(solution)/shard_map/scatter | solution.py:77
  18.6 0.2 reshape_reshape.23
  18.8 0.8 dynamic-slice_bitcast_fusion.1
  19.7 3.0 %collective-permute-start = (bf16[2,1,1,74,1536]{4,3,0,2,1:T(8,128)(2,1)}, bf16[2,1,1,74,1536]{4,3,0,2,1:T(8,128)(2,1)}, u32[]{:S(2)}, u32[]{:S(2)}) collective-permute-start(bf16[2,1,1,74,1536]{4,3,0,2,1:T(8,128)(2,1)} %dynamic-slice_bitcast_fusion.1), channel_id=1, source_target_pairs={{0,4},{4,0},{8,12},{12,8},{1,5},{5,1},{9,13},{13,9},{2,6},{6,2},{1... | collective-permute-start | bytes 1363976 | tf_op jit(solution)/shard_map/ppermute | solution.py:14
  22.7 0.2 reshape_reshape.22
  22.9 11.3 %collective-permute-done = bf16[2,1,1,74,1536]{4,3,0,2,1:T(8,128)(2,1)} collective-permute-done((bf16[2,1,1,74,1536]{4,3,0,2,1:T(8,128)(2,1)}, bf16[2,1,1,74,1536]{4,3,0,2,1:T(8,128)(2,1)}, u32[]{:S(2)}, u32[]{:S(2)}) %collective-permute-start) | collective-permute-done | bytes 454688 | tf_op jit(solution)/shard_map/ppermute | solution.py:14
  34.2 1.1 bitcast_dynamic-update-slice_fusion.1
  35.3 2.8 %collective-permute-start.1 = (bf16[1,1,2,74,1536]{4,3,2,1,0:T(8,128)(2,1)S(1)}, bf16[1,1,2,74,1536]{4,3,2,1,0:T(8,128)(2,1)S(1)}, u32[]{:S(2)}, u32[]{:S(2)}) collective-permute-start(bf16[1,1,2,74,1536]{4,3,2,1,0:T(8,128)(2,1)S(1)} %constant_dynamic-slice_fusion.1), channel_id=1, source_target_pairs={{0,8},{8,0},{4,12},{12,4},{1,9},{9,1},{5,13},{13,5},{2,10},{10,2},... | collective-permute-start | bytes 1363976 | tf_op jit(solution)/shard_map/ppermute | solution.py:14
  38.2 21.1 %collective-permute-done.1 = bf16[1,1,2,74,1536]{4,3,2,1,0:T(8,128)(2,1)S(1)} collective-permute-done((bf16[1,1,2,74,1536]{4,3,2,1,0:T(8,128)(2,1)S(1)}, bf16[1,1,2,74,1536]{4,3,2,1,0:T(8,128)(2,1)S(1)}, u32[]{:S(2)}, u32[]{:S(2)}) %collective-permute-start.1) | collective-permute-done | bytes 454688 | tf_op jit(solution)/shard_map/ppermute | solution.py:14
  59.3 1.4 fusion.8
  60.7 0.3 copy-done.16
  61.0 0.4 copy-done.9
  61.4 1.9 %fusion = bf16[4,1,74,1536]{3,2,0,1:T(8,128)(2,1)} fusion(bf16[1,768,768]{2,1,0:T(8,128)(2,1)S(1)} %copy-done.16, bf16[1,768,768]{2,1,0:T(8,128)(2,1)S(1)} %copy-done.9, bf16[4,1,74,1536]{3,2,0,1:T(8,128)(2,1)S(1)} %bitcast.116), kind=kOutput, calls=%fused_computation.5 | convolution fusion | flops 703524864 | bytes 3760128 | tf_op jit(solution)/shard_map/sjcd,jdf->sjcf/dot_general | solution.py:86
  63.3 42.6 %all-reduce.3.cloned.1.call-done = (bf16[4,1,74,768]{3,2,0,1:T(8,128)(2,1)}, bf16[4,1,74,1536]{3,2,0,1:T(8,128)(2,1)}) async-done(((bf16[4,1,74,768]{3,2,0,1:T(8,128)(2,1)}, bf16[4,1,74,1536]{3,2,0,1:T(8,128)(2,1)}), (bf16[4,1,74,768]{3,2,0,1:T(8,128)(2,1)}, bf16[4,1,74,1536]{3,2,0,1:T(8,128)(2,1)})) %all-reduce.3.cloned.1.call-update) | async-done | bytes 1363984 | tf_op jit(solution)/shard_map/psum | solution.py:92
  105.9 1.5 convert_element_type.111
  107.4 0.5 fusion.24
  107.9 0.9 copy-done.8
  108.8 0.6 fusion.11
  109.4 0.7 copy-done.17
  110.1 0.7 fusion.9
  110.8 0.6 fusion.7
  111.4 0.8 dynamic-slice_bitcast_fusion
  112.2 1.5 collective-permute-start.2
  113.7 0.2 mul.86
  113.9 1.4 mul.87
  115.4 3.0 %fusion.3 = bf16[1,768,768]{2,1,0:T(8,128)(2,1)} fusion(bf16[4,1,74,768]{3,2,0,1:T(8,128)(2,1)} %copy-done.8, bf16[4,1,74,1536]{3,2,0,1:T(8,128)(2,1)} %bitcast.117), kind=kOutput, calls=%fused_computation.12 | convolution fusion | flops 349765632 | bytes 2162688 | tf_op jit(solution)/shard_map/sjcd,sjcf->jdf/dot_general | solution.py:105
  118.4 7.2 %collective-permute-done.2 = bf16[2,1,1,74,1536]{4,3,0,2,1:T(8,128)(2,1)} collective-permute-done((bf16[2,1,1,74,1536]{4,3,0,2,1:T(8,128)(2,1)}, bf16[2,1,1,74,1536]{4,3,0,2,1:T(8,128)(2,1)}, u32[]{:S(2)}, u32[]{:S(2)}) %collective-permute-start.2) | collective-permute-done | bytes 454688 | tf_op jit(solution)/shard_map/ppermute | solution.py:14
  125.6 1.1 bitcast_dynamic-update-slice_fusion
  126.7 2.5 %collective-permute-start.3 = (bf16[1,1,2,74,1536]{4,3,2,1,0:T(8,128)(2,1)S(1)}, bf16[1,1,2,74,1536]{4,3,2,1,0:T(8,128)(2,1)S(1)}, u32[]{:S(2)}, u32[]{:S(2)}) collective-permute-start(bf16[1,1,2,74,1536]{4,3,2,1,0:T(8,128)(2,1)S(1)} %constant_dynamic-slice_fusion), channel_id=1, source_target_pairs={{0,8},{8,0},{4,12},{12,4},{1,9},{9,1},{5,13},{13,5},{2,10},{10,2},... | collective-permute-start | bytes 1363976 | tf_op jit(solution)/shard_map/ppermute | solution.py:14
  129.2 1.8 %fusion.5 = bf16[1,768,768]{2,1,0:T(8,128)(2,1)} fusion(bf16[4,74,768]{2,1,0:T(8,128)(2,1)S(1)} %copy-done.15, bf16[4,1,74,1536]{3,2,0,1:T(8,128)(2,1)S(1)} %bitcast.118), kind=kOutput, calls=%fused_computation.14 | convolution fusion | flops 349765632 | bytes 2162688 | tf_op jit(solution)/shard_map/sjcf,sjcd->jfd/dot_general | solution.py:102
  131.0 1.9 %fusion.4 = bf16[1,768,768]{2,1,0:T(8,128)(2,1)} fusion(bf16[4,1,74,1536]{3,2,0,1:T(8,128)(2,1)S(1)} %bitcast.119, bf16[4,1,74,768]{3,2,0,1:T(8,128)(2,1)S(1)} %copy-done.13, f32[4,1,74,1536]{3,2,0,1:T(8,128)S(1)} %copy-done.4), kind=kOutput, calls=%fused_computation.13 | convolution fusion | flops 351356928 | bytes 3145728 | tf_op jit(solution)/shard_map/sjcd,sjcf->jdf/dot_general | solution.py:108
  133.0 17.4 %collective-permute-done.3 = bf16[1,1,2,74,1536]{4,3,2,1,0:T(8,128)(2,1)S(1)} collective-permute-done((bf16[1,1,2,74,1536]{4,3,2,1,0:T(8,128)(2,1)S(1)}, bf16[1,1,2,74,1536]{4,3,2,1,0:T(8,128)(2,1)S(1)}, u32[]{:S(2)}, u32[]{:S(2)}) %collective-permute-start.3) | collective-permute-done | bytes 454688 | tf_op jit(solution)/shard_map/ppermute | solution.py:14
  150.4 0.3 reshape_reshape.29
  150.7 1.3 gather_fusion.2
  151.9 1.1 fusion.35
  153.0 1.6 reshape.181
  154.7 1.7 multiply_reduce_fusion.1
  156.4 1.2 reshape.182
  157.6 1.7 reduce.1
  159.6 11.1 %psum.23 = f32[128,2]{1,0:T(8,128)S(1)} all-reduce(f32[128,2]{1,0:T(8,128)S(1)} %reduce_sum.45), channel_id=1, replica_groups=mesh['group'=2,'expert'=4,'dp'=4] {'dp'}, use_global_device_ids=true, to_apply=%region_9.10 | all-reduce | flops 256 | bytes 2048 | tf_op jit(solution)/shard_map/psum | solution.py:131
  170.7 0.6 copy.26
  (57 shorter events, 1.9 us)
Async XLA Ops:
  7.2 52.1 %copy-start = (bf16[1,768,768]{2,1,0:T(8,128)(2,1)S(1)}, bf16[1,768,768]{2,1,0:T(8,128)(2,1)}, u32[]{:S(2)}) copy-start(bf16[1,768,768]{2,1,0:T(8,128)(2,1)} %param.13) | copy-start | bytes 3538948
  7.2 5.4 %copy-start.1 = (bf16[128,768]{1,0:T(8,128)(2,1)S(1)}, bf16[128,768]{1,0:T(8,128)(2,1)}, u32[]{:S(2)}) copy-start(bf16[128,768]{1,0:T(8,128)(2,1)} %param.8) | copy-start | bytes 589828
  7.2 98.7 %all-reduce.3.cloned.1.call-start = ((), (), s32[]{:S(2)}) async-start(), calls=%async_computation | async-start | bytes 2949120 | tf_op jit(solution)/shard_map/psum | solution.py:92
  11.8 0.6 copy-start.10
  12.6 1.2 copy-start.2
  19.7 14.6 %collective-permute-start = (bf16[2,1,1,74,1536]{4,3,0,2,1:T(8,128)(2,1)}, bf16[2,1,1,74,1536]{4,3,0,2,1:T(8,128)(2,1)}, u32[]{:S(2)}, u32[]{:S(2)}) collective-permute-start(bf16[2,1,1,74,1536]{4,3,0,2,1:T(8,128)(2,1)} %dynamic-slice_bitcast_fusion.1), channel_id=1, source_target_pairs={{0,4},{4,0},{8,12},{12,8},{1,5},{5,1},{9,13},{13,9},{2,6},{6,2},{1... | collective-permute-start | bytes 1363976 | tf_op jit(solution)/shard_map/ppermute | solution.py:14
  35.3 23.9 %collective-permute-start.1 = (bf16[1,1,2,74,1536]{4,3,2,1,0:T(8,128)(2,1)S(1)}, bf16[1,1,2,74,1536]{4,3,2,1,0:T(8,128)(2,1)S(1)}, u32[]{:S(2)}, u32[]{:S(2)}) collective-permute-start(bf16[1,1,2,74,1536]{4,3,2,1,0:T(8,128)(2,1)S(1)} %constant_dynamic-slice_fusion.1), channel_id=1, source_target_pairs={{0,8},{8,0},{4,12},{12,4},{1,9},{9,1},{5,13},{13,5},{2,10},{10,2},... | collective-permute-start | bytes 1363976 | tf_op jit(solution)/shard_map/ppermute | solution.py:14
  59.2 1.7 copy-start.16
  59.3 4.0 %copy-start.6 = (bf16[1,2,2,74,1536]{4,3,2,1,0:T(8,128)(2,1)}, bf16[1,2,2,74,1536]{4,3,2,1,0:T(8,128)(2,1)S(1)}, u32[]{:S(2)}) copy-start(bf16[1,2,2,74,1536]{4,3,2,1,0:T(8,128)(2,1)S(1)} %constant_dynamic-update-slice_fusion) | copy-start | bytes 2727940
  59.3 2.1 %copy-start.9 = (bf16[1,768,768]{2,1,0:T(8,128)(2,1)S(1)}, bf16[1,768,768]{2,1,0:T(8,128)(2,1)}, u32[]{:S(2)}) copy-start(bf16[1,768,768]{2,1,0:T(8,128)(2,1)} %param.11) | copy-start | bytes 3538948
  105.9 1.5 copy-start.12
  107.4 2.0 %copy-start.3 = (f32[4,1,74,1536]{3,2,0,1:T(8,128)}, f32[4,1,74,1536]{3,2,0,1:T(8,128)S(1)}, u32[]{:S(2)}) copy-start(f32[4,1,74,1536]{3,2,0,1:T(8,128)S(1)} %convert_element_type.111) | copy-start | bytes 5455876
  107.9 0.9 copy-start.8
  107.9 2.8 %copy-start.14 = (bf16[4,74,768]{2,1,0:T(8,128)(2,1)}, bf16[4,74,768]{2,1,0:T(8,128)(2,1)S(1)}, u32[]{:S(2)}) copy-start(bf16[4,74,768]{2,1,0:T(8,128)(2,1)S(1)} %get-tuple-element.14) | copy-start | bytes 1363972
  108.8 1.3 copy-start.17
  112.2 13.3 %collective-permute-start.2 = (bf16[2,1,1,74,1536]{4,3,0,2,1:T(8,128)(2,1)}, bf16[2,1,1,74,1536]{4,3,0,2,1:T(8,128)(2,1)}, u32[]{:S(2)}, u32[]{:S(2)}) collective-permute-start(bf16[2,1,1,74,1536]{4,3,0,2,1:T(8,128)(2,1)} %dynamic-slice_bitcast_fusion), channel_id=1, source_target_pairs={{0,4},{4,0},{8,12},{12,8},{1,5},{5,1},{9,13},{13,9},{2,6},{6,2},{1... | collective-permute-start | bytes 1363976 | tf_op jit(solution)/shard_map/ppermute | solution.py:14
  118.4 10.8 %copy-start.7 = (bf16[1,2,2,74,1536]{4,3,2,1,0:T(8,128)(2,1)S(1)}, bf16[1,2,2,74,1536]{4,3,2,1,0:T(8,128)(2,1)}, u32[]{:S(2)}) copy-start(bf16[1,2,2,74,1536]{4,3,2,1,0:T(8,128)(2,1)} %copy-done.6) | copy-start | bytes 2727940
  118.4 10.8 %copy-start.15 = (bf16[4,74,768]{2,1,0:T(8,128)(2,1)S(1)}, bf16[4,74,768]{2,1,0:T(8,128)(2,1)}, u32[]{:S(2)}) copy-start(bf16[4,74,768]{2,1,0:T(8,128)(2,1)} %copy-done.14) | copy-start | bytes 1363972
  126.7 4.3 %copy-start.4 = (f32[4,1,74,1536]{3,2,0,1:T(8,128)S(1)}, f32[4,1,74,1536]{3,2,0,1:T(8,128)}, u32[]{:S(2)}) copy-start(f32[4,1,74,1536]{3,2,0,1:T(8,128)} %copy-done.3) | copy-start | bytes 5455876
  126.7 4.3 %copy-start.13 = (bf16[4,1,74,768]{3,2,0,1:T(8,128)(2,1)S(1)}, bf16[4,1,74,768]{3,2,0,1:T(8,128)(2,1)}, u32[]{:S(2)}) copy-start(bf16[4,1,74,768]{3,2,0,1:T(8,128)(2,1)} %get-tuple-element.12) | copy-start | bytes 1363972
  126.7 23.6 %collective-permute-start.3 = (bf16[1,1,2,74,1536]{4,3,2,1,0:T(8,128)(2,1)S(1)}, bf16[1,1,2,74,1536]{4,3,2,1,0:T(8,128)(2,1)S(1)}, u32[]{:S(2)}, u32[]{:S(2)}) collective-permute-start(bf16[1,1,2,74,1536]{4,3,2,1,0:T(8,128)(2,1)S(1)} %constant_dynamic-slice_fusion), channel_id=1, source_target_pairs={{0,8},{8,0},{4,12},{12,4},{1,9},{9,1},{5,13},{13,5},{2,10},{10,2},... | collective-permute-start | bytes 1363976 | tf_op jit(solution)/shard_map/ppermute | solution.py:14
  153.0 1.6 copy-start.11
  156.4 2.9 %copy-start.5 = (f32[256,768]{1,0:T(8,128)S(1)}, f32[256,768]{1,0:T(8,128)}, u32[]{:S(2)}) copy-start(f32[256,768]{1,0:T(8,128)} %mul.87) | copy-start | bytes 2359300
Sparse Core Ops, SparseCore 0:
  63.4 42.3 all-reduce.2
where the time goes:
time: 179 us; the launch traced here: 178 us
  waiting for transfers between devices  99.5 us (56%)
  local copies, waits for them, and re-layouts  19.9 us (11%)
  between operations  14.4 us (8%)
  matrix products  11.8 us (7%)
  other arithmetic  11.6 us (6%)
  blocking collectives  11.1 us (6%)
  starting transfers between devices  9.84 us (5%)
    ppermute x4, waiting for transfers between devices, swapped(): return lax.ppermute(block, axis, route)  57 us
    psum x1, waiting for transfers between devices, shards(): lax.psum(jnp.einsum('sjcd,jfd->sjcf', expert_cot, down_weight, preferred_...  42.6 us
    psum x1, blocking collectives, shards(): grad_gates = lax.psum(partial_dots, 'dp')  11.1 us
    ppermute x4, starting transfers between devices, swapped(): return lax.ppermute(block, axis, route)  9.8 us
    unnamed x41, local copies, waits for them, and re-layouts  6.92 us
  transfers between devices with their start and end apart: 5, of which 5 were waited for; matrix products, arithmetic and copies ran while one was open for 5% of the time, Pallas kernels for 0%

commit v1 on v0

v1 whole, which is shorter than its diff:
```python
import functools

import jax
import jax.numpy as jnp
from jax import lax
from jax.experimental import pallas as pl
from jax.experimental.pallas import tpu as pltpu
from jax.sharding import PartitionSpec as P

BF = jnp.bfloat16
F32 = jnp.float32
VMEM_BYTES = 40 * 1024 * 1024


def swap(block, axis, offset):
    count = lax.axis_size(axis)
    return lax.ppermute(block, axis, [(i, i ^ offset) for i in range(count)])


def dot(a, b):
    return lax.dot_general(a, b, (((1,), (0,)), ((), ())), preferred_element_type=F32)


def dot_nt(a, b):
    return lax.dot_general(a, b, (((1,), (1,)), ((), ())), preferred_element_type=F32)


def dot_tn(a, b):
    return lax.dot_general(a, b, (((0,), (0,)), ((), ())), preferred_element_type=F32)


def call(kernel, name, outs, args, scalars=1, scratch=(), flops=0):
    smem = pl.BlockSpec(memory_space=pltpu.SMEM)
    vmem = pl.BlockSpec(memory_space=pltpu.VMEM)
    moved = sum(a.size * a.dtype.itemsize for a in args) + sum(
        o.size * o.dtype.itemsize for o in outs
    )
    return pl.pallas_call(
        kernel,
        name=name,
        out_shape=outs,
        in_specs=[smem] * scalars + [vmem] * (len(args) - scalars),
        out_specs=[vmem] * len(outs),
        scratch_shapes=list(scratch),
        compiler_params=pltpu.CompilerParams(vmem_limit_bytes=VMEM_BYTES),
        cost_estimate=pl.CostEstimate(flops=flops, bytes_accessed=moved, transcendentals=0),
    )(*args)


def chosen(routes, gates, expert):
    hit = routes == expert
    taken = jnp.sum(hit.astype(F32), axis=0, keepdims=True)
    gate = jnp.sum(jnp.where(hit, gates, 0.0), axis=0, keepdims=True)
    return taken, gate


def pack_kernel(peers, me_ref, routes_ref, gates_ref, tokens_ref, cot_ref, *out_refs):
    x_refs, c_refs, place_ref = out_refs[:peers], out_refs[peers : 2 * peers], out_refs[2 * peers]
    me = me_ref[0]
    routes, gates = routes_ref[...], gates_ref[...]
    count = routes.shape[1]
    rows = x_refs[0].shape[0]
    earlier = (
        lax.broadcasted_iota(jnp.int32, (count, count), 0)
        < lax.broadcasted_iota(jnp.int32, (count, count), 1)
    ).astype(BF)
    pairs = [chosen(routes, gates, me ^ j) for j in range(peers)]
    taken = jnp.concatenate([p[0] for p in pairs], axis=0)
    rank = dot(taken.astype(BF), earlier)
    rank = jnp.where(taken > 0.0, rank, -1.0).astype(jnp.int32)
    slot = lax.broadcasted_iota(jnp.int32, (rows, count), 0)
    for j in range(peers):
        place_ref[j * rows : (j + 1) * rows, :] = (slot == rank[j : j + 1]).astype(F32).astype(BF)
    tokens = tokens_ref[...]
    for j in range(peers):
        x_refs[j][...] = dot(place_ref[j * rows : (j + 1) * rows, :], tokens).astype(BF)
    cot = cot_ref[...]
    for j in range(peers):
        place = place_ref[j * rows : (j + 1) * rows, :]
        scale = jnp.sum(place.astype(F32) * pairs[j][1], axis=1, keepdims=True)
        c_refs[j][...] = (dot(place, cot) * scale).astype(BF)


def up_kernel(peers, half_ref, *refs):
    x_refs, (gate_ref, up_ref, keep_ref, send_ref) = refs[:peers], refs[peers:]
    half = half_ref[0]
    width = gate_ref.shape[1]
    x = jnp.concatenate([r[...] for r in x_refs], axis=0)
    rows = x.shape[0] // 2
    for i, w_ref in enumerate((gate_ref, up_ref)):
        y = dot(x, w_ref[...]).astype(BF)
        lanes = slice(i * width, (i + 1) * width)

        @pl.when(half == 0)
        def _():
            keep_ref[:, lanes] = y[:rows]
            send_ref[:, lanes] = y[rows:]

        @pl.when(half == 1)
        def _():
            keep_ref[:, lanes] = y[rows:]
            send_ref[:, lanes] = y[:rows]


def back_kernel(peers, half_ref, *refs):
    c_refs, (down_ref, keep_ref, send_ref) = refs[:peers], refs[peers:]
    half = half_ref[0]
    c = jnp.concatenate([r[...] for r in c_refs], axis=0)
    rows = c.shape[0] // 2
    y = dot_nt(c, down_ref[...]).astype(BF)

    @pl.when(half == 0)
    def _():
        keep_ref[...] = y[:rows]
        send_ref[...] = y[rows:]

    @pl.when(half == 1)
    def _():
        keep_ref[...] = y[rows:]
        send_ref[...] = y[:rows]


def out_kernel(peers, half_ref, mine_ref, other_ref, down_ref, *refs):
    out_refs, (hidden_ref, sums_ref) = refs[:peers], refs[peers:]
    half = half_ref[0]
    width = down_ref.shape[0]
    sums_ref[half] = mine_ref[...]
    sums_ref[1 - half] = other_ref[...]
    rows = mine_ref.shape[0]
    for h in range(2):
        g = sums_ref[h, :, :width].astype(F32)
        u = sums_ref[h, :, width:].astype(F32)
        hidden_ref[h * rows : (h + 1) * rows, :] = (g * jax.nn.sigmoid(g) * u).astype(BF)
    out = dot(hidden_ref[...], down_ref[...]).astype(BF)
    cp = out_refs[0].shape[0]
    for j in range(peers):
        out_refs[j][...] = out[j * cp : (j + 1) * cp]


def dx_kernel(peers, cap, half_ref, sums_ref, hidden_ref, mine_ref, other_ref, gate_ref, up_ref, *refs):
    dx_refs, (dgate_ref, dup_ref, dh_ref, dot_ref) = refs[:peers], refs[peers:]
    half = half_ref[0]
    width = gate_ref.shape[1]
    dh_ref[half] = mine_ref[...]
    dh_ref[1 - half] = other_ref[...]
    rows = mine_ref.shape[0]
    for h in range(2):
        part = slice(h * rows, (h + 1) * rows)
        g = sums_ref[h, :, :width].astype(F32)
        u = sums_ref[h, :, width:].astype(F32)
        dh = dh_ref[h].astype(F32)
        s = jax.nn.sigmoid(g)
        dgate_ref[part, :] = (dh * u * s * (1.0 + g * (1.0 - s))).astype(BF)
        dup_ref[part, :] = (dh * (g * s)).astype(BF)
        dot_ref[part, :] = jnp.sum(hidden_ref[part, :].astype(F32) * dh, axis=1, keepdims=True)
    dx = dot_nt(dgate_ref[...], gate_ref[...]) + dot_nt(dup_ref[...], up_ref[...])
    cp = dx_refs[0].shape[0]
    lanes = 128 * (-(-cp // 128))
    eye = lax.broadcasted_iota(jnp.int32, (cp, lanes), 0) == lax.broadcasted_iota(
        jnp.int32, (cp, lanes), 1
    )
    row = lax.broadcasted_iota(jnp.int32, (cp, lanes), 0)
    for j in range(peers):
        block = dx[j * cp : (j + 1) * cp]
        dx_refs[j][...] = block.astype(BF)
        dots = jnp.sum(jnp.where(eye, dot_ref[j * cp : (j + 1) * cp, :], 0.0), axis=0, keepdims=True)
        high = dots.astype(BF).astype(F32)
        middle = (dots - high).astype(BF).astype(F32)
        low = dots - high - middle
        first = jnp.where(row == cap, high, block[:, :lanes])
        first = jnp.where(row == cap + 1, middle, first)
        first = jnp.where(row == cap + 2, low, first)
        dx_refs[j][:, :lanes] = first.astype(BF)


def grad_kernel(peers, *refs):
    x_refs, c_refs = refs[:peers], refs[peers : 2 * peers]
    hidden_ref, dgate_ref, dup_ref, gg_ref, gu_ref, gd_ref = refs[2 * peers :]
    x = jnp.concatenate([r[...] for r in x_refs], axis=0)
    gg_ref[...] = dot_tn(x, dgate_ref[...]).astype(BF)
    gu_ref[...] = dot_tn(x, dup_ref[...]).astype(BF)
    c = jnp.concatenate([r[...] for r in c_refs], axis=0)
    gd_ref[...] = dot_tn(hidden_ref[...], c).astype(BF)


def merge_kernel(peers, cap, me_ref, routes_ref, gates_ref, place_ref, *refs):
    out_refs, dx_refs = refs[:peers], refs[peers : 2 * peers]
    mixed_ref, grad_ref, gates_out_ref = refs[2 * peers :]
    me = me_ref[0]
    routes, gates = routes_ref[...], gates_ref[...]
    cp = out_refs[0].shape[0]
    highs, lows = [], []
    total = jnp.zeros(gates.shape, F32)
    base = cap // 16 * 16
    for j in range(peers):
        place = place_ref[j * cp : (j + 1) * cp, :]
        _, gate = chosen(routes, gates, me ^ j)
        high = gate.astype(BF).astype(F32)
        highs.append((place.astype(F32) * high).astype(BF))
        lows.append((place.astype(F32) * (gate - high)).astype(BF))
        found = dot(dx_refs[j][base:cp, :cp], place)
        at = cap - base
        value = found[at : at + 1] + found[at + 1 : at + 2] + found[at + 2 : at + 3]
        total = total + jnp.where(routes == (me ^ j), value, 0.0)
    gates_out_ref[...] = total / gates
    out = jnp.concatenate([r[...] for r in out_refs], axis=0)
    mixed = dot_tn(jnp.concatenate(highs, axis=0), out) + dot_tn(jnp.concatenate(lows, axis=0), out)
    mixed_ref[...] = mixed.astype(BF)
    dx = jnp.concatenate([r[...] for r in dx_refs], axis=0)
    grad_ref[...] = dot_tn(place_ref[...], dx).astype(BF)


def added(a, b):
    return (a.astype(F32) + b.astype(F32)).astype(BF)


def reduced(keep, send, dp_count):
    total = added(keep, swap(send, "dp", 1))
    bit = 2
    while bit < dp_count:
        total = added(total, swap(total, "dp", bit))
        bit *= 2
    return total, swap(total, "dp", 1)


def shards(tokens, cotangent, routes, route_gates, gate_weight, up_weight, down_weight):
    peers = lax.axis_size("expert")
    dp_count = lax.axis_size("dp")
    count, top = routes.shape
    width = tokens.shape[1]
    ff = gate_weight.shape[2]
    cap = 7 * count * top // (6 * peers)
    cp = -(-(cap + 3) // 16) * 16
    rows = peers * cp
    gate_w, up_w, down_w = gate_weight[0], up_weight[0], down_weight[0]
    me = lax.axis_index("expert").astype(jnp.int32).reshape(1)
    half = (lax.axis_index("dp").astype(jnp.int32) & 1).reshape(1)
    routes_t, gates_t = routes.T, route_gates.T

    def sds(shape, dtype=BF):
        return jax.ShapeDtypeStruct(shape, dtype)

    part = sds((cp, width))
    packed = call(
        functools.partial(pack_kernel, peers),
        "pack",
        [part] * (2 * peers) + [sds((rows, count))],
        (me, routes_t, gates_t, tokens, cotangent),
        flops=4 * rows * count * width,
    )
    xs, cs, place = packed[:peers], packed[peers : 2 * peers], packed[2 * peers]
    xs = [xs[0]] + [swap(xs[j], "expert", j) for j in range(1, peers)]
    cs = [cs[0]] + [swap(cs[j], "expert", j) for j in range(1, peers)]
    work = 2 * rows * width * ff
    keep, send = call(
        functools.partial(up_kernel, peers),
        "up",
        [sds((rows // 2, 2 * ff))] * 2,
        (half, *xs, gate_w, up_w),
        flops=2 * work,
    )
    sum_mine, sum_other = reduced(keep, send, dp_count)
    keep, send = call(
        functools.partial(back_kernel, peers),
        "back",
        [sds((rows // 2, ff))] * 2,
        (half, *cs, down_w),
        flops=work,
    )
    dh_mine, dh_other = reduced(keep, send, dp_count)
    *outs, hidden, sums = call(
        functools.partial(out_kernel, peers),
        "out",
        [part] * peers + [sds((rows, ff)), sds((2, rows // 2, 2 * ff))],
        (half, sum_mine, sum_other, down_w),
        flops=work,
    )
    outs = [outs[0]] + [swap(outs[j], "expert", j) for j in range(1, peers)]
    *dxs, dgate, dup = call(
        functools.partial(dx_kernel, peers, cap),
        "dx",
        [part] * peers + [sds((rows, ff))] * 2,
        (half, sums, hidden, dh_mine, dh_other, gate_w, up_w),
        scratch=[pltpu.VMEM((2, rows // 2, ff), BF), pltpu.VMEM((rows, 1), F32)],
        flops=2 * work,
    )
    dxs = [dxs[0]] + [swap(dxs[j], "expert", j) for j in range(1, peers)]
    grad_gate, grad_up, grad_down = call(
        functools.partial(grad_kernel, peers),
        "grads",
        [sds((width, ff))] * 2 + [sds((ff, width))],
        (*xs, *cs, hidden, dgate, dup),
        scalars=0,
        flops=3 * work,
    )
    mixed, grad_tokens, gates_grad = call(
        functools.partial(merge_kernel, peers, cap),
        "merge",
        [sds((count, width))] * 2 + [sds((top, count), F32)],
        (me, routes_t, gates_t, place, *outs, *dxs),
        flops=6 * rows * count * width,
    )
    return (mixed, grad_tokens, gates_grad.T, grad_gate[None], grad_up[None], grad_down[None])


def solution(mesh):
    in_specs = (
        P(("group", "expert"), "dp"),
        P(("group", "expert"), "dp"),
        P(("group", "expert"), None),
        P(("group", "expert"), None),
        P("expert", "dp", None),
        P("expert", "dp", None),
        P("expert", None, "dp"),
    )
    out_specs = (
        P(("group", "expert"), "dp"),
        P(("group", "expert"), "dp"),
        P(("group", "expert"), None),
        P(("group", "expert"), "dp", None),
        P(("group", "expert"), "dp", None),
        P(("group", "expert"), None, "dp"),
    )
    return jax.shard_map(shards, mesh=mesh, in_specs=in_specs, out_specs=out_specs, check_vma=False)
```

time: 179 us -> 76.4 us (0.43)
  waiting for transfers between devices: 99.5 us -> 37.4 us
  local copies, waits for them, and re-layouts: 19.9 us -> 5.77 us
  between operations: 14.4 us -> 0.78 us
  starting transfers between devices: 9.84 us -> 22.9 us
  matrix products: 11.8 us -> 0 us
  other arithmetic: 11.6 us -> 0.4 us
  blocking collectives: 11.1 us -> 0 us
  Pallas kernels: 0 us -> 8.87 us
    psum x1 -> x0, waiting for transfers between devices: 42.6 us -> none  [shards(): lax.psum(jnp.einsum('sjcd,jfd->sjcf', expert_cot, down_weight, preferred_...]
    ppermute x4 -> x18, waiting for transfers between devices: 57 us -> 37.4 us  [swap(): return lax.ppermute(block, axis, [(i, i ^ offset) for i in range(count)])]
    ppermute x4 -> x18, starting transfers between devices: 9.8 us -> 22.9 us  [swap(): return lax.ppermute(block, axis, [(i, i ^ offset) for i in range(count)])]
    dot_general x8 -> x0, matrix products: 11.8 us -> none  [the longest x1 3 us: shards(): jnp.einsum('sjcd,sjcf->jdf', expert_in, dgate, preferred_element_type=jnp...]
    psum x1 -> x0, blocking collectives: 11.1 us -> none  [shards(): grad_gates = lax.psum(partial_dots, 'dp')]
    pallas_call x0 -> x7, Pallas kernels: none -> 8.87 us  [call(): pl.pallas_call(kernel, name=name, out_shape=outs, in_specs=[smem] * scala...]
    gather x3 -> x0, local copies, waits for them, and re-layouts: 4.39 us -> none  [the longest x1 1.93 us: shards(): route_rows = jnp.concatenate([tokens[owners], scaled], axis=1)]
    reduce_sum x4 -> x0, other arithmetic: 3.57 us -> none  [the longest x1 1.71 us: shards(): grad_tokens = jnp.sum(back_dx, axis=1).astype(jnp.bfloat16)]
  transfers between devices with their start and end apart: 5 -> 18, of which waited for: 5 -> 8; matrix products, arithmetic and copies ran while one was open for 5% -> 1% of each run, Pallas kernels for 0% -> 7%
where the time goes in v1:
time: 76.4 us; the launch traced here: 76.1 us
  waiting for transfers between devices  37.4 us (49%)
  starting transfers between devices  22.9 us (30%)
  Pallas kernels  8.87 us (12%)
  local copies, waits for them, and re-layouts  5.77 us (8%)
  between operations  0.78 us (1%)
    ppermute x18, waiting for transfers between devices, swap(): return lax.ppermute(block, axis, [(i, i ^ offset) for i in range(count)])  37.4 us
    ppermute x18, starting transfers between devices, swap(): return lax.ppermute(block, axis, [(i, i ^ offset) for i in range(count)])  22.9 us
    pallas_call x7, Pallas kernels, call(): pl.pallas_call(kernel, name=name, out_shape=outs, in_specs=[smem] * scala...  8.87 us
    unnamed x22, local copies, waits for them, and re-layouts  5.77 us
  transfers between devices with their start and end apart: 18, of which 8 were waited for; matrix products, arithmetic and copies ran while one was open for 1% of the time, Pallas kernels for 7%

profile of v1, /device:TPU:0, one launch (start us, length us, event | category | flops | bytes accessed | tf_op | source)
XLA Modules:
  0.0 76.1 jit_solution(11538047530140200389)
XLA Ops:
  0.6 0.0 copy-start.5
  0.6 0.7 copy-done.5
  1.3 0.7 copy-done.7
  2.0 0.9 %copy-done.9 = bf16[128,768]{1,0:T(8,128)(2,1)S(1)} copy-done((bf16[128,768]{1,0:T(8,128)(2,1)S(1)}, bf16[128,768]{1,0:T(8,128)(2,1)}, u32[]{:S(2)}) %copy-start.9) | copy-done | bytes 196632
  2.9 0.9 %copy-done.10 = bf16[128,768]{1,0:T(8,128)(2,1)S(1)} copy-done((bf16[128,768]{1,0:T(8,128)(2,1)S(1)}, bf16[128,768]{1,0:T(8,128)(2,1)}, u32[]{:S(2)}) %copy-start.10) | copy-done | bytes 196632
  3.9 0.6 pack.1
  4.4 3.1 %collective-permute-start = (bf16[80,768]{1,0:T(8,128)(2,1)S(1)}, bf16[80,768]{1,0:T(8,128)(2,1)S(1)}, u32[]{:S(2)}, u32[]{:S(2)}) collective-permute-start(bf16[80,768]{1,0:T(8,128)(2,1)S(1)} %get-tuple-element.39), channel_id=1, source_target_pairs={{0,4},{4,0},{8,12},{12,8},{1,5},{5,1},{9,13},{13,9},{2,6},{6,2},{1... | collective-permute-start | bytes 368648 | tf_op jit(solution)/shard_map/ppermute | solution.py:17
  7.5 2.6 %collective-permute-start.1 = (bf16[80,768]{1,0:T(8,128)(2,1)S(1)}, bf16[80,768]{1,0:T(8,128)(2,1)S(1)}, u32[]{:S(2)}, u32[]{:S(2)}) collective-permute-start(bf16[80,768]{1,0:T(8,128)(2,1)S(1)} %get-tuple-element.40), channel_id=1, source_target_pairs={{0,8},{4,12},{8,0},{12,4},{1,9},{5,13},{9,1},{13,5},{2,10},{6,14},... | collective-permute-start | bytes 368648 | tf_op jit(solution)/shard_map/ppermute | solution.py:17
  10.1 0.0 collective-permute-start.2
  10.1 2.1 %collective-permute-done.refs_1_ = bf16[80,768]{1,0:T(8,128)(2,1)S(1)} collective-permute-done((bf16[80,768]{1,0:T(8,128)(2,1)S(1)}, bf16[80,768]{1,0:T(8,128)(2,1)S(1)}, u32[]{:S(2)}, u32[]{:S(2)}) %collective-permute-start) | collective-permute-done | bytes 122912 | tf_op jit(solution)/shard_map/ppermute | solution.py:17
  12.2 7.7 %collective-permute-done.1.refs_2_ = bf16[80,768]{1,0:T(8,128)(2,1)S(1)} collective-permute-done((bf16[80,768]{1,0:T(8,128)(2,1)S(1)}, bf16[80,768]{1,0:T(8,128)(2,1)S(1)}, u32[]{:S(2)}, u32[]{:S(2)}) %collective-permute-start.1) | collective-permute-done | bytes 122912 | tf_op jit(solution)/shard_map/ppermute | solution.py:17
  19.8 1.3 %copy-done = bf16[1,768,768]{2,1,0:T(8,128)(2,1)S(1)} copy-done((bf16[1,768,768]{2,1,0:T(8,128)(2,1)S(1)}, bf16[1,768,768]{2,1,0:T(8,128)(2,1)}, u32[]{:S(2)}) %copy-start) | copy-done | bytes 1179672
  21.1 1.3 %copy-done.2 = bf16[1,768,768]{2,1,0:T(8,128)(2,1)S(1)} copy-done((bf16[1,768,768]{2,1,0:T(8,128)(2,1)S(1)}, bf16[1,768,768]{2,1,0:T(8,128)(2,1)}, u32[]{:S(2)}) %copy-start.2) | copy-done | bytes 1179672
  22.4 1.4 %up.1 = (bf16[160,1536]{1,0:T(8,128)(2,1)S(1)}, bf16[160,1536]{1,0:T(8,128)(2,1)S(1)}) custom-call(s32[1]{0:T(128)} %bitcast.3.half_ref, bf16[80,768]{1,0:T(8,128)(2,1)S(1)} %get-tuple-element.38.refs_0_, bf16[80,768]{1,0:T(8,128)(2,1)S(1)} %collective-permute-done.refs_1_, bf16[80,768]{1,0:T(8,128)(2,1)S(1)} %collective-permute-done.1.refs_2_, ...), custom_call_target="tpu_custom_call" | custom-call | flops 754974720 | bytes 3833860 | tf_op jit(solution)/shard_map/up/pallas_call | solution.py:38
  23.8 0.0 copy-start.4
  23.8 0.1 collective-permute-start.3
  23.9 1.9 %collective-permute-start.9 = (bf16[80,768]{1,0:T(8,128)(2,1)S(1)}, bf16[80,768]{1,0:T(8,128)(2,1)S(1)}, u32[]{:S(2)}, u32[]{:S(2)}) collective-permute-start(bf16[80,768]{1,0:T(8,128)(2,1)S(1)} %get-tuple-element.51), channel_id=1, source_target_pairs={{0,4},{4,0},{8,12},{12,8},{1,5},{5,1},{9,13},{13,9},{2,6},{6,2},{1... | collective-permute-start | bytes 368648 | tf_op jit(solution)/shard_map/ppermute | solution.py:17
  25.8 1.1 %collective-permute-start.10 = (bf16[80,768]{1,0:T(8,128)(2,1)S(1)}, bf16[80,768]{1,0:T(8,128)(2,1)S(1)}, u32[]{:S(2)}, u32[]{:S(2)}) collective-permute-start(bf16[80,768]{1,0:T(8,128)(2,1)S(1)} %get-tuple-element.52), channel_id=1, source_target_pairs={{0,8},{4,12},{8,0},{12,4},{1,9},{5,13},{9,1},{13,5},{2,10},{6,14},... | collective-permute-start | bytes 368648 | tf_op jit(solution)/shard_map/ppermute | solution.py:17
  26.9 1.4 %collective-permute-start.11 = (bf16[80,768]{1,0:T(8,128)(2,1)S(1)}, bf16[80,768]{1,0:T(8,128)(2,1)S(1)}, u32[]{:S(2)}, u32[]{:S(2)}) collective-permute-start(bf16[80,768]{1,0:T(8,128)(2,1)S(1)} %get-tuple-element.53), channel_id=1, source_target_pairs={{0,12},{4,8},{8,4},{12,0},{1,13},{5,9},{9,5},{13,1},{2,14},{6,10},... | collective-permute-start | bytes 368648 | tf_op jit(solution)/shard_map/ppermute | solution.py:17
  28.3 0.0 collective-permute-done.3
  28.3 0.1 add_convert_fusion.1
  28.5 1.6 %collective-permute-start.4 = (bf16[160,1536]{1,0:T(8,128)(2,1)S(1)}, bf16[160,1536]{1,0:T(8,128)(2,1)S(1)}, u32[]{:S(2)}, u32[]{:S(2)}) collective-permute-start(bf16[160,1536]{1,0:T(8,128)(2,1)S(1)} %add_convert_fusion.1), channel_id=1, source_target_pairs={{0,2},{1,3},{2,0},{3,1},{4,6},{5,7},{6,4},{7,5},{8,10},{9,11},{10,... | collective-permute-start | bytes 1474568 | tf_op jit(solution)/shard_map/ppermute | solution.py:17
  30.0 1.7 %collective-permute-done.9.refs_1_.refs_5_ = bf16[80,768]{1,0:T(8,128)(2,1)S(1)} collective-permute-done((bf16[80,768]{1,0:T(8,128)(2,1)S(1)}, bf16[80,768]{1,0:T(8,128)(2,1)S(1)}, u32[]{:S(2)}, u32[]{:S(2)}) %collective-permute-start.9) | collective-permute-done | bytes 122912 | tf_op jit(solution)/shard_map/ppermute | solution.py:17
  31.7 6.5 %collective-permute-done.10.refs_2_.refs_6_ = bf16[80,768]{1,0:T(8,128)(2,1)S(1)} collective-permute-done((bf16[80,768]{1,0:T(8,128)(2,1)S(1)}, bf16[80,768]{1,0:T(8,128)(2,1)S(1)}, u32[]{:S(2)}, u32[]{:S(2)}) %collective-permute-start.10) | collective-permute-done | bytes 122912 | tf_op jit(solution)/shard_map/ppermute | solution.py:17
  38.2 0.0 collective-permute-done.11.refs_3_.refs_7_
  38.2 0.6 back.1
  38.8 0.1 collective-permute-start.12
  38.9 1.5 %collective-permute-done.12 = bf16[160,768]{1,0:T(8,128)(2,1)S(1)} collective-permute-done((bf16[160,768]{1,0:T(8,128)(2,1)S(1)}, bf16[160,768]{1,0:T(8,128)(2,1)S(1)}, u32[]{:S(2)}, u32[]{:S(2)}) %collective-permute-start.12) | collective-permute-done | bytes 245792 | tf_op jit(solution)/shard_map/ppermute | solution.py:17
  40.4 0.1 add_convert_fusion.3
  40.5 1.6 %collective-permute-start.13 = (bf16[160,768]{1,0:T(8,128)(2,1)S(1)}, bf16[160,768]{1,0:T(8,128)(2,1)S(1)}, u32[]{:S(2)}, u32[]{:S(2)}) collective-permute-start(bf16[160,768]{1,0:T(8,128)(2,1)S(1)} %add_convert_fusion.3), channel_id=1, source_target_pairs={{0,2},{1,3},{2,0},{3,1},{4,6},{5,7},{6,4},{7,5},{8,10},{9,11},{10,... | collective-permute-start | bytes 737288 | tf_op jit(solution)/shard_map/ppermute | solution.py:17
  42.1 0.1 add_convert_fusion.mine_ref
  42.2 0.1 collective-permute-start.5
  42.3 6.3 %collective-permute-done.13 = bf16[160,768]{1,0:T(8,128)(2,1)S(1)} collective-permute-done((bf16[160,768]{1,0:T(8,128)(2,1)S(1)}, bf16[160,768]{1,0:T(8,128)(2,1)S(1)}, u32[]{:S(2)}, u32[]{:S(2)}) %collective-permute-start.13) | collective-permute-done | bytes 245792 | tf_op jit(solution)/shard_map/ppermute | solution.py:17
  48.5 0.1 add_convert_fusion.2.mine_ref
  48.6 0.0 copy-start.1
  48.6 0.1 collective-permute-start.14
  48.7 0.7 out.1
  49.5 2.5 %collective-permute-start.6 = (bf16[80,768]{1,0:T(8,128)(2,1)S(1)}, bf16[80,768]{1,0:T(8,128)(2,1)S(1)}, u32[]{:S(2)}, u32[]{:S(2)}) collective-permute-start(bf16[80,768]{1,0:T(8,128)(2,1)S(1)} %get-tuple-element.45), channel_id=1, source_target_pairs={{0,4},{4,0},{8,12},{12,8},{1,5},{5,1},{9,13},{13,9},{2,6},{6,2},{1... | collective-permute-start | bytes 368648 | tf_op jit(solution)/shard_map/ppermute | solution.py:17
  52.0 1.1 %collective-permute-start.7 = (bf16[80,768]{1,0:T(8,128)(2,1)S(1)}, bf16[80,768]{1,0:T(8,128)(2,1)S(1)}, u32[]{:S(2)}, u32[]{:S(2)}) collective-permute-start(bf16[80,768]{1,0:T(8,128)(2,1)S(1)} %get-tuple-element.46), channel_id=1, source_target_pairs={{0,8},{4,12},{8,0},{12,4},{1,9},{5,13},{9,1},{13,5},{2,10},{6,14},... | collective-permute-start | bytes 368648 | tf_op jit(solution)/shard_map/ppermute | solution.py:17
  53.0 1.4 %collective-permute-start.8 = (bf16[80,768]{1,0:T(8,128)(2,1)S(1)}, bf16[80,768]{1,0:T(8,128)(2,1)S(1)}, u32[]{:S(2)}, u32[]{:S(2)}) collective-permute-start(bf16[80,768]{1,0:T(8,128)(2,1)S(1)} %get-tuple-element.47), channel_id=1, source_target_pairs={{0,12},{4,8},{8,4},{12,0},{1,13},{5,9},{9,5},{13,1},{2,14},{6,10},... | collective-permute-start | bytes 368648 | tf_op jit(solution)/shard_map/ppermute | solution.py:17
  54.4 1.2 %dx.1 = (bf16[80,768]{1,0:T(8,128)(2,1)S(1)}, bf16[80,768]{1,0:T(8,128)(2,1)S(1)}, bf16[80,768]{1,0:T(8,128)(2,1)S(1)}, bf16[80,768]{1,0:T(8,128)(2,1)S(1)}, bf1...) custom-call(s32[1]{0:T(128)} %bitcast.3.half_ref, bf16[2,160,1536]{2,1,0:T(8,128)(2,1)S(1)} %get-tuple-element.48.sums_ref, ...), custom_call_target="tpu_custom_call" | custom-call | flops 754974720 | bytes 5799940 | tf_op jit(solution)/shard_map/dx/pallas_call | solution.py:38
  55.6 1.1 %collective-permute-start.15 = (bf16[80,768]{1,0:T(8,128)(2,1)S(1)}, bf16[80,768]{1,0:T(8,128)(2,1)S(1)}, u32[]{:S(2)}, u32[]{:S(2)}) collective-permute-start(bf16[80,768]{1,0:T(8,128)(2,1)S(1)} %get-tuple-element.57), channel_id=1, source_target_pairs={{0,4},{4,0},{8,12},{12,8},{1,5},{5,1},{9,13},{13,9},{2,6},{6,2},{1... | collective-permute-start | bytes 368648 | tf_op jit(solution)/shard_map/ppermute | solution.py:17
  56.8 1.9 %collective-permute-start.16 = (bf16[80,768]{1,0:T(8,128)(2,1)S(1)}, bf16[80,768]{1,0:T(8,128)(2,1)S(1)}, u32[]{:S(2)}, u32[]{:S(2)}) collective-permute-start(bf16[80,768]{1,0:T(8,128)(2,1)S(1)} %get-tuple-element.58), channel_id=1, source_target_pairs={{0,8},{4,12},{8,0},{12,4},{1,9},{5,13},{9,1},{13,5},{2,10},{6,14},... | collective-permute-start | bytes 368648 | tf_op jit(solution)/shard_map/ppermute | solution.py:17
  58.7 1.4 %collective-permute-start.17 = (bf16[80,768]{1,0:T(8,128)(2,1)S(1)}, bf16[80,768]{1,0:T(8,128)(2,1)S(1)}, u32[]{:S(2)}, u32[]{:S(2)}) collective-permute-start(bf16[80,768]{1,0:T(8,128)(2,1)S(1)} %get-tuple-element.59), channel_id=1, source_target_pairs={{0,12},{4,8},{8,4},{12,0},{1,13},{5,9},{9,5},{13,1},{2,14},{6,10},... | collective-permute-start | bytes 368648 | tf_op jit(solution)/shard_map/ppermute | solution.py:17
  60.1 3.1 %grads.1 = (bf16[768,768]{1,0:T(8,128)(2,1)}, bf16[768,768]{1,0:T(8,128)(2,1)}, bf16[768,768]{1,0:T(8,128)(2,1)}) custom-call(bf16[80,768]{1,0:T(8,128)(2,1)S(1)} %get-tuple-element.38.refs_0_, bf16[80,768]{1,0:T(8,128)(2,1)S(1)} %collective-permute-done.refs_1_, bf16[80,768]{1,0:T(8,128)(2,1)S(1)} %collective-permute-done.1.refs_2_, ...), custom_call_target="tpu_custom_call" | custom-call | flops 1132462080 | bytes 5996544 | tf_op jit(solution)/shard_map/grads/pallas_call | solution.py:38
  63.2 1.2 %collective-permute-done.7.refs_2_ = bf16[80,768]{1,0:T(8,128)(2,1)S(1)} collective-permute-done((bf16[80,768]{1,0:T(8,128)(2,1)S(1)}, bf16[80,768]{1,0:T(8,128)(2,1)S(1)}, u32[]{:S(2)}, u32[]{:S(2)}) %collective-permute-start.7) | collective-permute-done | bytes 122912 | tf_op jit(solution)/shard_map/ppermute | solution.py:17
  64.4 10.5 %collective-permute-done.16.refs_6_ = bf16[80,768]{1,0:T(8,128)(2,1)S(1)} collective-permute-done((bf16[80,768]{1,0:T(8,128)(2,1)S(1)}, bf16[80,768]{1,0:T(8,128)(2,1)S(1)}, u32[]{:S(2)}, u32[]{:S(2)}) %collective-permute-start.16) | collective-permute-done | bytes 122912 | tf_op jit(solution)/shard_map/ppermute | solution.py:17
  74.9 1.2 %merge.1 = (bf16[128,768]{1,0:T(8,128)(2,1)}, bf16[128,768]{1,0:T(8,128)(2,1)}, f32[2,128]{1,0:T(2,128)}) custom-call(s32[1]{0:T(128)} %bitcast.me_ref, s32[2,128]{1,0:T(2,128)S(1)} %bitcast.18, f32[2,128]{1,0:T(2,128)S(1)} %bitcast.20, bf16[320,128]{1,0:T(8,128)(2,1)S(1)} %get-tuple-element.37.place_ref, bf16[80,768]{1,0:T(8,128)(2,1)S(1)} %get-tuple-element.44.refs_0_, ...), custom_call_target="tpu_custom_call" | custom-call | flops 188743680 | bytes 1461252 | tf_op jit(solution)/shard_map/merge/pallas_call | solution.py:38
  (21 shorter events, 0.0 us)
Async XLA Ops:
  0.6 0.7 copy-start.5
  1.3 0.7 copy-start.7
  2.0 0.9 %copy-start.9 = (bf16[128,768]{1,0:T(8,128)(2,1)S(1)}, bf16[128,768]{1,0:T(8,128)(2,1)}, u32[]{:S(2)}) copy-start(bf16[128,768]{1,0:T(8,128)(2,1)} %tokens_ref.1) | copy-start | bytes 589828
  2.9 0.9 %copy-start.10 = (bf16[128,768]{1,0:T(8,128)(2,1)S(1)}, bf16[128,768]{1,0:T(8,128)(2,1)}, u32[]{:S(2)}) copy-start(bf16[128,768]{1,0:T(8,128)(2,1)} %cot_ref.1) | copy-start | bytes 589828
  4.4 7.7 %collective-permute-start = (bf16[80,768]{1,0:T(8,128)(2,1)S(1)}, bf16[80,768]{1,0:T(8,128)(2,1)S(1)}, u32[]{:S(2)}, u32[]{:S(2)}) collective-permute-start(bf16[80,768]{1,0:T(8,128)(2,1)S(1)} %get-tuple-element.39), channel_id=1, source_target_pairs={{0,4},{4,0},{8,12},{12,8},{1,5},{5,1},{9,13},{13,9},{2,6},{6,2},{1... | collective-permute-start | bytes 368648 | tf_op jit(solution)/shard_map/ppermute | solution.py:17
  7.5 12.3 %collective-permute-start.1 = (bf16[80,768]{1,0:T(8,128)(2,1)S(1)}, bf16[80,768]{1,0:T(8,128)(2,1)S(1)}, u32[]{:S(2)}, u32[]{:S(2)}) collective-permute-start(bf16[80,768]{1,0:T(8,128)(2,1)S(1)} %get-tuple-element.40), channel_id=1, source_target_pairs={{0,8},{4,12},{8,0},{12,4},{1,9},{5,13},{9,1},{13,5},{2,10},{6,14},... | collective-permute-start | bytes 368648 | tf_op jit(solution)/shard_map/ppermute | solution.py:17
  10.1 9.7 %collective-permute-start.2 = (bf16[80,768]{1,0:T(8,128)(2,1)S(1)}, bf16[80,768]{1,0:T(8,128)(2,1)S(1)}, u32[]{:S(2)}, u32[]{:S(2)}) collective-permute-start(bf16[80,768]{1,0:T(8,128)(2,1)S(1)} %get-tuple-element.41), channel_id=1, source_target_pairs={{0,12},{4,8},{8,4},{12,0},{1,13},{5,9},{9,5},{13,1},{2,14},{6,10},... | collective-permute-start | bytes 368648 | tf_op jit(solution)/shard_map/ppermute | solution.py:17
  19.8 1.3 %copy-start = (bf16[1,768,768]{2,1,0:T(8,128)(2,1)S(1)}, bf16[1,768,768]{2,1,0:T(8,128)(2,1)}, u32[]{:S(2)}) copy-start(bf16[1,768,768]{2,1,0:T(8,128)(2,1)} %param.11) | copy-start | bytes 3538948
  21.1 1.3 %copy-start.2 = (bf16[1,768,768]{2,1,0:T(8,128)(2,1)S(1)}, bf16[1,768,768]{2,1,0:T(8,128)(2,1)}, u32[]{:S(2)}) copy-start(bf16[1,768,768]{2,1,0:T(8,128)(2,1)} %param.12) | copy-start | bytes 3538948
  23.8 14.4 %copy-start.4 = (bf16[1,768,768]{2,1,0:T(8,128)(2,1)S(1)}, bf16[1,768,768]{2,1,0:T(8,128)(2,1)}, u32[]{:S(2)}) copy-start(bf16[1,768,768]{2,1,0:T(8,128)(2,1)} %param.13) | copy-start | bytes 3538948
  23.8 4.5 %collective-permute-start.3 = (bf16[160,1536]{1,0:T(8,128)(2,1)S(1)}, bf16[160,1536]{1,0:T(8,128)(2,1)S(1)}, u32[]{:S(2)}, u32[]{:S(2)}) collective-permute-start(bf16[160,1536]{1,0:T(8,128)(2,1)S(1)} %get-tuple-element.43), channel_id=1, source_target_pairs={{0,1},{1,0},{2,3},{3,2},{4,5},{5,4},{6,7},{7,6},{8,9},{9,8},{10,11... | collective-permute-start | bytes 1474568 | tf_op jit(solution)/shard_map/ppermute | solution.py:17
  23.9 7.8 %collective-permute-start.9 = (bf16[80,768]{1,0:T(8,128)(2,1)S(1)}, bf16[80,768]{1,0:T(8,128)(2,1)S(1)}, u32[]{:S(2)}, u32[]{:S(2)}) collective-permute-start(bf16[80,768]{1,0:T(8,128)(2,1)S(1)} %get-tuple-element.51), channel_id=1, source_target_pairs={{0,4},{4,0},{8,12},{12,8},{1,5},{5,1},{9,13},{13,9},{2,6},{6,2},{1... | collective-permute-start | bytes 368648 | tf_op jit(solution)/shard_map/ppermute | solution.py:17
  25.8 12.4 %collective-permute-start.10 = (bf16[80,768]{1,0:T(8,128)(2,1)S(1)}, bf16[80,768]{1,0:T(8,128)(2,1)S(1)}, u32[]{:S(2)}, u32[]{:S(2)}) collective-permute-start(bf16[80,768]{1,0:T(8,128)(2,1)S(1)} %get-tuple-element.52), channel_id=1, source_target_pairs={{0,8},{4,12},{8,0},{12,4},{1,9},{5,13},{9,1},{13,5},{2,10},{6,14},... | collective-permute-start | bytes 368648 | tf_op jit(solution)/shard_map/ppermute | solution.py:17
  26.9 11.3 %collective-permute-start.11 = (bf16[80,768]{1,0:T(8,128)(2,1)S(1)}, bf16[80,768]{1,0:T(8,128)(2,1)S(1)}, u32[]{:S(2)}, u32[]{:S(2)}) collective-permute-start(bf16[80,768]{1,0:T(8,128)(2,1)S(1)} %get-tuple-element.53), channel_id=1, source_target_pairs={{0,12},{4,8},{8,4},{12,0},{1,13},{5,9},{9,5},{13,1},{2,14},{6,10},... | collective-permute-start | bytes 368648 | tf_op jit(solution)/shard_map/ppermute | solution.py:17
  28.5 13.6 %collective-permute-start.4 = (bf16[160,1536]{1,0:T(8,128)(2,1)S(1)}, bf16[160,1536]{1,0:T(8,128)(2,1)S(1)}, u32[]{:S(2)}, u32[]{:S(2)}) collective-permute-start(bf16[160,1536]{1,0:T(8,128)(2,1)S(1)} %add_convert_fusion.1), channel_id=1, source_target_pairs={{0,2},{1,3},{2,0},{3,1},{4,6},{5,7},{6,4},{7,5},{8,10},{9,11},{10,... | collective-permute-start | bytes 1474568 | tf_op jit(solution)/shard_map/ppermute | solution.py:17
  38.8 1.6 %collective-permute-start.12 = (bf16[160,768]{1,0:T(8,128)(2,1)S(1)}, bf16[160,768]{1,0:T(8,128)(2,1)S(1)}, u32[]{:S(2)}, u32[]{:S(2)}) collective-permute-start(bf16[160,768]{1,0:T(8,128)(2,1)S(1)} %get-tuple-element.55), channel_id=1, source_target_pairs={{0,1},{1,0},{2,3},{3,2},{4,5},{5,4},{6,7},{7,6},{8,9},{9,8},{10,11... | collective-permute-start | bytes 737288 | tf_op jit(solution)/shard_map/ppermute | solution.py:17
  40.5 8.1 %collective-permute-start.13 = (bf16[160,768]{1,0:T(8,128)(2,1)S(1)}, bf16[160,768]{1,0:T(8,128)(2,1)S(1)}, u32[]{:S(2)}, u32[]{:S(2)}) collective-permute-start(bf16[160,768]{1,0:T(8,128)(2,1)S(1)} %add_convert_fusion.3), channel_id=1, source_target_pairs={{0,2},{1,3},{2,0},{3,1},{4,6},{5,7},{6,4},{7,5},{8,10},{9,11},{10,... | collective-permute-start | bytes 737288 | tf_op jit(solution)/shard_map/ppermute | solution.py:17
  42.2 6.5 %collective-permute-start.5 = (bf16[160,1536]{1,0:T(8,128)(2,1)S(1)}, bf16[160,1536]{1,0:T(8,128)(2,1)S(1)}, u32[]{:S(2)}, u32[]{:S(2)}) collective-permute-start(bf16[160,1536]{1,0:T(8,128)(2,1)S(1)} %add_convert_fusion.mine_ref), channel_id=1, source_target_pairs={{0,1},{1,0},{2,3},{3,2},{4,5},{5,4},{6,7},{7,6},{8,9},{9,8},{10,11... | collective-permute-start | bytes 1474568 | tf_op jit(solution)/shard_map/ppermute | solution.py:17
  48.5 5.8 %copy-start.3 = (bf16[1,768,768]{2,1,0:T(8,128)(2,1)S(1)}, bf16[1,768,768]{2,1,0:T(8,128)(2,1)}, u32[]{:S(2)}) copy-start(bf16[1,768,768]{2,1,0:T(8,128)(2,1)} %param.12) | copy-start | bytes 3538948
  48.6 5.8 %copy-start.1 = (bf16[1,768,768]{2,1,0:T(8,128)(2,1)S(1)}, bf16[1,768,768]{2,1,0:T(8,128)(2,1)}, u32[]{:S(2)}) copy-start(bf16[1,768,768]{2,1,0:T(8,128)(2,1)} %param.11) | copy-start | bytes 3538948
  48.6 5.8 %collective-permute-start.14 = (bf16[160,768]{1,0:T(8,128)(2,1)S(1)}, bf16[160,768]{1,0:T(8,128)(2,1)S(1)}, u32[]{:S(2)}, u32[]{:S(2)}) collective-permute-start(bf16[160,768]{1,0:T(8,128)(2,1)S(1)} %add_convert_fusion.2.mine_ref), channel_id=1, source_target_pairs={{0,1},{1,0},{2,3},{3,2},{4,5},{5,4},{6,7},{7,6},{8,9},{9,8},{10,11... | collective-permute-start | bytes 737288 | tf_op jit(solution)/shard_map/ppermute | solution.py:17
  49.5 9.2 %collective-permute-start.6 = (bf16[80,768]{1,0:T(8,128)(2,1)S(1)}, bf16[80,768]{1,0:T(8,128)(2,1)S(1)}, u32[]{:S(2)}, u32[]{:S(2)}) collective-permute-start(bf16[80,768]{1,0:T(8,128)(2,1)S(1)} %get-tuple-element.45), channel_id=1, source_target_pairs={{0,4},{4,0},{8,12},{12,8},{1,5},{5,1},{9,13},{13,9},{2,6},{6,2},{1... | collective-permute-start | bytes 368648 | tf_op jit(solution)/shard_map/ppermute | solution.py:17
  52.0 12.4 %collective-permute-start.7 = (bf16[80,768]{1,0:T(8,128)(2,1)S(1)}, bf16[80,768]{1,0:T(8,128)(2,1)S(1)}, u32[]{:S(2)}, u32[]{:S(2)}) collective-permute-start(bf16[80,768]{1,0:T(8,128)(2,1)S(1)} %get-tuple-element.46), channel_id=1, source_target_pairs={{0,8},{4,12},{8,0},{12,4},{1,9},{5,13},{9,1},{13,5},{2,10},{6,14},... | collective-permute-start | bytes 368648 | tf_op jit(solution)/shard_map/ppermute | solution.py:17
  53.0 11.4 %collective-permute-start.8 = (bf16[80,768]{1,0:T(8,128)(2,1)S(1)}, bf16[80,768]{1,0:T(8,128)(2,1)S(1)}, u32[]{:S(2)}, u32[]{:S(2)}) collective-permute-start(bf16[80,768]{1,0:T(8,128)(2,1)S(1)} %get-tuple-element.47), channel_id=1, source_target_pairs={{0,12},{4,8},{8,4},{12,0},{1,13},{5,9},{9,5},{13,1},{2,14},{6,10},... | collective-permute-start | bytes 368648 | tf_op jit(solution)/shard_map/ppermute | solution.py:17
  55.6 8.7 %collective-permute-start.15 = (bf16[80,768]{1,0:T(8,128)(2,1)S(1)}, bf16[80,768]{1,0:T(8,128)(2,1)S(1)}, u32[]{:S(2)}, u32[]{:S(2)}) collective-permute-start(bf16[80,768]{1,0:T(8,128)(2,1)S(1)} %get-tuple-element.57), channel_id=1, source_target_pairs={{0,4},{4,0},{8,12},{12,8},{1,5},{5,1},{9,13},{13,9},{2,6},{6,2},{1... | collective-permute-start | bytes 368648 | tf_op jit(solution)/shard_map/ppermute | solution.py:17
  56.8 18.1 %collective-permute-start.16 = (bf16[80,768]{1,0:T(8,128)(2,1)S(1)}, bf16[80,768]{1,0:T(8,128)(2,1)S(1)}, u32[]{:S(2)}, u32[]{:S(2)}) collective-permute-start(bf16[80,768]{1,0:T(8,128)(2,1)S(1)} %get-tuple-element.58), channel_id=1, source_target_pairs={{0,8},{4,12},{8,0},{12,4},{1,9},{5,13},{9,1},{13,5},{2,10},{6,14},... | collective-permute-start | bytes 368648 | tf_op jit(solution)/shard_map/ppermute | solution.py:17
  58.7 16.2 %collective-permute-start.17 = (bf16[80,768]{1,0:T(8,128)(2,1)S(1)}, bf16[80,768]{1,0:T(8,128)(2,1)S(1)}, u32[]{:S(2)}, u32[]{:S(2)}) collective-permute-start(bf16[80,768]{1,0:T(8,128)(2,1)S(1)} %get-tuple-element.59), channel_id=1, source_target_pairs={{0,12},{4,8},{8,4},{12,0},{1,13},{5,9},{9,5},{13,1},{2,14},{6,10},... | collective-permute-start | bytes 368648 | tf_op jit(solution)/shard_map/ppermute | solution.py:17
  60.1 14.8 %copy-start.6 = (s32[128,2]{0,1:T(2,128)S(1)}, s32[128,2]{0,1:T(2,128)}, u32[]{:S(2)}) copy-start(s32[128,2]{0,1:T(2,128)} %param.9) | copy-start | bytes 3076
  60.1 14.8 %copy-start.8 = (f32[128,2]{0,1:T(2,128)S(1)}, f32[128,2]{0,1:T(2,128)}, u32[]{:S(2)}) copy-start(f32[128,2]{0,1:T(2,128)} %param.10) | copy-start | bytes 3076

commit v2 on v1

v2 whole, which is shorter than its diff:
```python
import functools

import jax
import jax.numpy as jnp
from jax import lax
from jax.experimental import pallas as pl
from jax.experimental.pallas import tpu as pltpu
from jax.sharding import PartitionSpec as P

BF = jnp.bfloat16
F32 = jnp.float32
VMEM_BYTES = 40 * 1024 * 1024
SYNC = (True, False, False, False)


def swap(block, axis, offset):
    count = lax.axis_size(axis)
    return lax.ppermute(block, axis, [(i, i ^ offset) for i in range(count)])


def dot(a, b):
    return lax.dot_general(a, b, (((1,), (0,)), ((), ())), preferred_element_type=F32)


def dot_nt(a, b):
    return lax.dot_general(a, b, (((1,), (1,)), ((), ())), preferred_element_type=F32)


def dot_tn(a, b):
    return lax.dot_general(a, b, (((0,), (0,)), ((), ())), preferred_element_type=F32)


def call(kernel, name, outs, args, scalars=1, hbm=0, scratch=(), flops=0):
    smem = pl.BlockSpec(memory_space=pltpu.SMEM)
    vmem = pl.BlockSpec(memory_space=pltpu.VMEM)
    moved = sum(a.size * a.dtype.itemsize for a in args) + sum(
        o.size * o.dtype.itemsize for o in outs
    )
    return pl.pallas_call(
        kernel,
        name=name,
        out_shape=outs,
        in_specs=[smem] * scalars
        + [pl.BlockSpec(memory_space=pltpu.HBM)] * hbm
        + [vmem] * (len(args) - scalars - hbm),
        out_specs=[vmem] * len(outs),
        scratch_shapes=list(scratch),
        compiler_params=pltpu.CompilerParams(vmem_limit_bytes=VMEM_BYTES),
        cost_estimate=pl.CostEstimate(flops=flops, bytes_accessed=moved, transcendentals=0),
    )(*args)


def chosen(routes, expert):
    return jnp.sum((routes == expert).astype(F32), axis=0, keepdims=True)


def gate_row(routes, gates, expert):
    return jnp.sum(jnp.where(routes == expert, gates, 0.0), axis=0, keepdims=True)


def pack_kernel(peers, me_ref, routes_ref, tokens_ref, *refs):
    near = peers // 2
    near_ref, x_refs, place_ref = refs[0], refs[1 : 1 + near], refs[1 + near]
    me = me_ref[0]
    count = routes_ref.shape[1]
    rows = x_refs[0].shape[0]
    earlier = (
        lax.broadcasted_iota(jnp.int32, (count, count), 0)
        < lax.broadcasted_iota(jnp.int32, (count, count), 1)
    ).astype(BF)
    slot = lax.broadcasted_iota(jnp.int32, (rows, count), 0)
    routes = routes_ref[...]
    taken = jnp.concatenate([chosen(routes, me ^ j) for j in range(peers)], axis=0)
    rank = dot(taken.astype(BF), earlier)
    rank = jnp.where(taken > 0.0, rank, -1.0).astype(jnp.int32)
    for j in range(peers):
        part = slice(j * rows, (j + 1) * rows)
        place_ref[part, :] = (slot == rank[j : j + 1]).astype(F32).astype(BF)
    tokens = tokens_ref[...]
    for j in range(near):
        part = slice((near + j) * rows, (near + j + 1) * rows)
        x_refs[j][...] = dot(place_ref[part, :], tokens).astype(BF)
    near_ref[...] = dot(place_ref[: near * rows, :], tokens).astype(BF)


def pack_cot_kernel(peers, me_ref, routes_ref, gates_ref, cot_ref, x_ref, place_ref, *refs):
    near = peers // 2
    pair_refs, c_refs = refs[:near], refs[near:]
    me = me_ref[0]
    rows = c_refs[0].shape[0]
    routes, gates = routes_ref[...], gates_ref[...]
    cot = cot_ref[...]
    for j in reversed(range(peers)):
        place = place_ref[j * rows : (j + 1) * rows, :]
        gate = gate_row(routes, gates, me ^ j)
        scale = jnp.sum(place.astype(F32) * gate, axis=1, keepdims=True)
        c = (dot(place, cot) * scale).astype(BF)
        if j < near:
            pair_refs[j][:rows, :] = x_ref[j * rows : (j + 1) * rows, :]
            pair_refs[j][rows:, :] = c
        else:
            c_refs[j - near][...] = c


def load_kernel(*refs):
    count = (len(refs) - 1) // 2
    sem = refs[-1]
    copies = [pltpu.make_async_copy(refs[i], refs[count + i], sem.at[i]) for i in range(count)]
    for copy in copies:
        copy.start()
    for copy in copies:
        copy.wait()


def hand_out(half, y, refs):
    rows = y.shape[0] // 2
    width = y.shape[1]
    lanes = pl.ds(half[1], width)
    if len(refs) == 1:
        refs[0][0, :, lanes] = y[:rows]
        refs[0][1, :, lanes] = y[rows:]
        return
    for h in range(2):

        @pl.when(half[0] == h)
        def _():
            refs[0][:, lanes] = y[h * rows : (h + 1) * rows]
            refs[1][:, lanes] = y[(1 - h) * rows : (2 - h) * rows]


def both_halves(half, refs, store_ref):
    if len(refs) == 1:
        return refs[0]
    store_ref[half] = refs[0][...]
    store_ref[1 - half] = refs[1][...]
    return store_ref


def stack(refs, part=slice(None)):
    return jnp.concatenate([r[part, :] for r in refs], axis=0)


def rows_of(pair_refs, refs, which):
    cp = refs[0].shape[0]
    return jnp.concatenate(
        [stack(pair_refs, slice(which * cp, (which + 1) * cp)), stack(refs)], axis=0
    )


def up_kernel(near, half_ref, *refs):
    pair_refs, x_refs, (gate_ref, up_ref, *to_refs) = refs[:near], refs[near : 2 * near], refs[2 * near :]
    x = rows_of(pair_refs, x_refs, 0)
    width = gate_ref.shape[1]
    hand_out((half_ref[0], 0), dot(x, gate_ref[...]).astype(BF), to_refs)
    hand_out((half_ref[0], width), dot(x, up_ref[...]).astype(BF), to_refs)


def back_kernel(near, half_ref, *refs):
    pair_refs, c_refs, (down_ref, *to_refs) = refs[:near], refs[near : 2 * near], refs[2 * near :]
    c = rows_of(pair_refs, c_refs, 1)
    hand_out((half_ref[0], 0), dot_nt(c, down_ref[...]).astype(BF), to_refs)


def activate(g, u):
    return (g * jax.nn.sigmoid(g) * u).astype(BF)


def derive(g, u, dh):
    s = jax.nn.sigmoid(g)
    return (dh * u * s * (1.0 + g * (1.0 - s))).astype(BF), (dh * (g * s)).astype(BF)


def row_dots(hidden, dh):
    return jnp.sum(hidden.astype(F32) * dh, axis=1, keepdims=True)


def store_dx(cap, dx_ref, block, dots):
    cp = dx_ref.shape[0]
    lanes = 128 * (-(-cp // 128))
    row = lax.broadcasted_iota(jnp.int32, (cp, lanes), 0)
    eye = row == lax.broadcasted_iota(jnp.int32, (cp, lanes), 1)
    dots = jnp.sum(jnp.where(eye, dots, 0.0), axis=0, keepdims=True)
    high = dots.astype(BF).astype(F32)
    middle = (dots - high).astype(BF).astype(F32)
    low = dots - high - middle
    first = jnp.where(row == cap, high, block[:, :lanes])
    first = jnp.where(row == cap + 1, middle, first)
    first = jnp.where(row == cap + 2, low, first)
    dx_ref[:, :lanes] = first.astype(BF)
    dx_ref[:, lanes:] = block[:, lanes:].astype(BF)


def out_kernel(peers, waits, half_ref, down_ref, *refs):
    from_refs, refs = refs[: 2 - waits], refs[2 - waits :]
    out_refs, hidden_ref, sums_ref = refs[:peers], refs[peers], refs[-1]
    width = down_ref.shape[0]
    source_ref = both_halves(half_ref[0], from_refs, sums_ref)
    rows = source_ref.shape[1]
    for h in range(2):
        g = source_ref[h, :, :width].astype(F32)
        u = source_ref[h, :, width:].astype(F32)
        hidden_ref[h * rows : (h + 1) * rows, :] = activate(g, u)
    out = dot(hidden_ref[...], down_ref[...]).astype(BF)
    cp = out_refs[0].shape[0]
    for j in range(peers):
        out_refs[j][...] = out[j * cp : (j + 1) * cp]


def dx_kernel(peers, cap, half_ref, sums_ref, hidden_ref, gate_ref, up_ref, *refs):
    from_refs = refs[: -peers - 4]
    dx_refs, (dgate_ref, dup_ref, dh_ref, dot_ref) = refs[-peers - 4 : -4], refs[-4:]
    width = gate_ref.shape[1]
    source_ref = both_halves(half_ref[0], from_refs, dh_ref)
    rows = source_ref.shape[1]
    for h in range(2):
        part = slice(h * rows, (h + 1) * rows)
        g = sums_ref[h, :, :width].astype(F32)
        u = sums_ref[h, :, width:].astype(F32)
        dh = source_ref[h].astype(F32)
        dgate_ref[part, :], dup_ref[part, :] = derive(g, u, dh)
        dot_ref[part, :] = row_dots(hidden_ref[part, :], dh)
    dx = dot_nt(dgate_ref[...], gate_ref[...]) + dot_nt(dup_ref[...], up_ref[...])
    cp = dx_refs[0].shape[0]
    for j in range(peers):
        part = slice(j * cp, (j + 1) * cp)
        store_dx(cap, dx_refs[j], dx[part], dot_ref[part, :])


def grad_kernel(near, *refs):
    pair_refs, x_refs, c_refs = refs[:near], refs[near : 2 * near], refs[2 * near : 3 * near]
    hidden_ref, dgate_ref, dup_ref, gg_ref, gu_ref, gd_ref = refs[3 * near :]
    x = rows_of(pair_refs, x_refs, 0)
    gg_ref[...] = dot_tn(x, dgate_ref[...]).astype(BF)
    gu_ref[...] = dot_tn(x, dup_ref[...]).astype(BF)
    gd_ref[...] = dot_tn(hidden_ref[...], rows_of(pair_refs, c_refs, 1)).astype(BF)


def mix_kernel(peers, me_ref, routes_ref, gates_ref, place_ref, *refs):
    out_refs, mixed_ref = refs[:peers], refs[peers]
    me = me_ref[0]
    routes, gates = routes_ref[...], gates_ref[...]
    cp = out_refs[0].shape[0]
    highs, lows = [], []
    for j in range(peers):
        place = place_ref[j * cp : (j + 1) * cp, :].astype(F32)
        gate = gate_row(routes, gates, me ^ j)
        high = gate.astype(BF).astype(F32)
        highs.append((place * high).astype(BF))
        lows.append((place * (gate - high)).astype(BF))
    out = stack(out_refs)
    mixed = dot_tn(jnp.concatenate(highs, axis=0), out) + dot_tn(jnp.concatenate(lows, axis=0), out)
    mixed_ref[...] = mixed.astype(BF)


def merge_kernel(peers, cap, me_ref, routes_ref, gates_ref, place_ref, *refs):
    dx_refs, (grad_ref, gates_out_ref) = refs[:peers], refs[peers:]
    me = me_ref[0]
    routes, gates = routes_ref[...], gates_ref[...]
    cp = dx_refs[0].shape[0]
    grad_ref[...] = dot_tn(place_ref[...], stack(dx_refs)).astype(BF)
    total = jnp.zeros(gates.shape, F32)
    base = cap // 16 * 16
    at = cap - base
    for j in range(peers):
        place = place_ref[j * cp : (j + 1) * cp, :]
        found = dot(dx_refs[j][base:cp, :cp], place)
        value = found[at : at + 1] + found[at + 1 : at + 2] + found[at + 2 : at + 3]
        total = total + jnp.where(routes == (me ^ j), value, 0.0)
    gates_out_ref[...] = total / gates


def added(a, b):
    return (a.astype(F32) + b.astype(F32)).astype(BF)


def after(first, arrays):
    return lax.optimization_barrier((*first, *arrays))[len(first) :]


def pairs_of(count):
    return [[i, i + 1] for i in range(0, count, 2)]


def reduced(parts, dp_count):
    if len(parts) == 1:
        arrived = lax.all_to_all(parts[0], "dp", 0, 0, axis_index_groups=pairs_of(dp_count))
        total = added(arrived[0], arrived[1])
    else:
        total = added(parts[0], swap(parts[1], "dp", 1))
    bit = 2
    while bit < dp_count:
        total = added(total, swap(total, "dp", bit))
        bit *= 2
    return total


def whole(total, dp_count, waits):
    if waits:
        twice = jnp.broadcast_to(total[None], (2, *total.shape))
        return [lax.all_to_all(twice, "dp", 0, 0, axis_index_groups=pairs_of(dp_count))]
    return [total, swap(total, "dp", 1)]


def shards(tokens, cotangent, routes, route_gates, gate_weight, up_weight, down_weight):
    peers = lax.axis_size("expert")
    near = peers // 2
    dp_count = lax.axis_size("dp")
    count, top = routes.shape
    width = tokens.shape[1]
    ff = gate_weight.shape[2]
    cap = 7 * count * top // (6 * peers)
    cp = -(-(cap + 3) // 16) * 16
    rows = near * cp
    gate_w, up_w, down_w = gate_weight[0], up_weight[0], down_weight[0]
    me = lax.axis_index("expert").astype(jnp.int32).reshape(1)
    half = (lax.axis_index("dp").astype(jnp.int32) & 1).reshape(1)
    routes_t, gates_t = routes.T, route_gates.T

    def sds(shape, dtype=BF):
        return jax.ShapeDtypeStruct(shape, dtype)

    part, pair = sds((cp, width)), sds((2 * cp, width))
    near_x, *xs, place = call(
        functools.partial(pack_kernel, peers),
        "pack",
        [sds((rows, width))] + [part] * near + [sds((2 * rows, count))],
        (me, routes_t, tokens),
        flops=4 * rows * count * width,
    )
    packed = call(
        functools.partial(pack_cot_kernel, peers),
        "pack_cot",
        [pair] * near + [part] * near,
        (me, routes_t, gates_t, cotangent, near_x, place),
        flops=4 * rows * count * width,
    )
    xcs, cs = packed[:near], packed[near:]
    weights = lax.optimization_barrier((gate_w, up_w, down_w, cs[0]))[:3]
    gate_w, up_w, down_w = call(
        load_kernel,
        "load",
        [sds(w.shape) for w in weights],
        weights,
        scalars=0,
        scratch=[pltpu.SemaphoreType.DMA((3,))],
    )
    xs = [swap(xs[j], "expert", near + j) for j in range(near)]
    xcs = [xcs[0]] + [swap(xcs[j], "expert", j) for j in range(1, near)]
    cs = [swap(cs[j], "expert", near + j) for j in range(near)]
    work = 2 * rows * width * ff

    def parts_of(waits, wide):
        return [sds((2, rows, wide))] if waits else [sds((rows, wide))] * 2

    up_parts = call(
        functools.partial(up_kernel, near),
        "up",
        parts_of(SYNC[0], 2 * ff),
        (half, *xcs, *xs, gate_w, up_w),
        flops=4 * work,
    )
    up_sum = reduced(up_parts, dp_count)
    dh_parts = call(
        functools.partial(back_kernel, near),
        "back",
        parts_of(SYNC[1], ff),
        (half, *xcs, *cs, down_w),
        flops=2 * work,
    )
    dh_sum = reduced(dh_parts, dp_count)
    up_both = whole(up_sum, dp_count, SYNC[2])
    produced = call(
        functools.partial(out_kernel, peers, SYNC[2]),
        "out",
        [part] * peers + [sds((2 * rows, ff))] + [sds((2, rows, 2 * ff))] * (not SYNC[2]),
        (half, down_w, *up_both),
        flops=2 * work,
    )
    outs, hidden = produced[:peers], produced[peers]
    sums = up_both[0] if SYNC[2] else produced[-1]
    *dxs, dgate, dup = call(
        functools.partial(dx_kernel, peers, cap),
        "dx",
        [part] * peers + [sds((2 * rows, ff))] * 2,
        (half, sums, hidden, gate_w, up_w, *whole(dh_sum, dp_count, SYNC[3])),
        scratch=[pltpu.VMEM((2, rows, ff), BF), pltpu.VMEM((2 * rows, 1), F32)],
        flops=4 * work,
    )
    outs = [outs[0]] + [swap(outs[j], "expert", j) for j in range(1, peers)]
    dxs = [dxs[0]] + [swap(dxs[j], "expert", j) for j in range(1, peers)]
    grad_gate, grad_up, grad_down = call(
        functools.partial(grad_kernel, near),
        "grads",
        [sds((width, ff))] * 2 + [sds((ff, width))],
        (*xcs, *xs, *cs, hidden, dgate, dup),
        scalars=0,
        flops=6 * work,
    )
    (mixed,) = call(
        functools.partial(mix_kernel, peers),
        "mix",
        [sds((count, width))],
        (me, routes_t, gates_t, place, *outs),
        flops=8 * rows * count * width,
    )
    grad_tokens, gates_grad = call(
        functools.partial(merge_kernel, peers, cap),
        "merge",
        [sds((count, width)), sds((top, count), F32)],
        (me, routes_t, gates_t, place, *dxs),
        flops=4 * rows * count * width,
    )
    return (mixed, grad_tokens, gates_grad.T, grad_gate[None], grad_up[None], grad_down[None])


def solution(mesh):
    in_specs = (
        P(("group", "expert"), "dp"),
        P(("group", "expert"), "dp"),
        P(("group", "expert"), None),
        P(("group", "expert"), None),
        P("expert", "dp", None),
        P("expert", "dp", None),
        P("expert", None, "dp"),
    )
    out_specs = (
        P(("group", "expert"), "dp"),
        P(("group", "expert"), "dp"),
        P(("group", "expert"), None),
        P(("group", "expert"), "dp", None),
        P(("group", "expert"), "dp", None),
        P(("group", "expert"), None, "dp"),
    )
    return jax.shard_map(shards, mesh=mesh, in_specs=in_specs, out_specs=out_specs, check_vma=False)
```

time: 76.4 us -> 78 us (1.021)
  waiting for transfers between devices: 37.4 us -> 28.7 us
  blocking collectives: 0 us -> 4.52 us
  starting transfers between devices: 22.9 us -> 26 us
  local copies, waits for them, and re-layouts: 5.77 us -> 7.02 us
  Pallas kernels: 8.87 us -> 10.1 us
    ppermute x18 -> x16, waiting for transfers between devices: 37.4 us -> 28.7 us  [swap(): return lax.ppermute(block, axis, [(i, i ^ offset) for i in range(count)])]
    all_to_all x0 -> x1, blocking collectives: none -> 4.52 us  [reduced(): lax.all_to_all(parts[0], 'dp', 0, 0, axis_index_groups=pairs_of(dp_count))]
    ppermute x18 -> x16, starting transfers between devices: 22.9 us -> 26 us  [swap(): return lax.ppermute(block, axis, [(i, i ^ offset) for i in range(count)])]
    unnamed x22 -> x18, local copies, waits for them, and re-layouts: 5.77 us -> 7.02 us
    pallas_call x7 -> x10, Pallas kernels: 8.87 us -> 10.1 us  [call(): pl.pallas_call(kernel, name=name, out_shape=outs, in_specs=[smem] * scala...]
  transfers between devices with their start and end apart: 18 -> 16, of which waited for: 8 -> 7; matrix products, arithmetic and copies ran while one was open for 1% -> 1% of each run, Pallas kernels for 7% -> 11%
where the time goes in v2:
time: 78 us; the launch traced here: 77.6 us
  waiting for transfers between devices  28.7 us (37%)
  starting transfers between devices  26 us (33%)
  Pallas kernels  10.1 us (13%)
  local copies, waits for them, and re-layouts  7.02 us (9%)
  blocking collectives  4.52 us (6%)
  between operations  0.79 us (1%)
    ppermute x16, waiting for transfers between devices, swap(): return lax.ppermute(block, axis, [(i, i ^ offset) for i in range(count)])  28.7 us
    ppermute x16, starting transfers between devices, swap(): return lax.ppermute(block, axis, [(i, i ^ offset) for i in range(count)])  26 us
    pallas_call x10, Pallas kernels, call(): pl.pallas_call(kernel, name=name, out_shape=outs, in_specs=[smem] * scala...  10.1 us
    unnamed x18, local copies, waits for them, and re-layouts  7.02 us
    all_to_all x1, blocking collectives, reduced(): lax.all_to_all(parts[0], 'dp', 0, 0, axis_index_groups=pairs_of(dp_count))  4.52 us
  transfers between devices with their start and end apart: 16, of which 7 were waited for; matrix products, arithmetic and copies ran while one was open for 1% of the time, Pallas kernels for 11%

profile of v2, /device:TPU:0, one launch (start us, length us, event | category | flops | bytes accessed | tf_op | source)
XLA Modules:
  0.0 77.6 jit_solution(16159561903287028514)
XLA Ops:
  0.6 0.0 copy-start.4
  0.6 0.7 copy-done.4
  1.3 0.9 %copy-done.8 = bf16[128,768]{1,0:T(8,128)(2,1)S(1)} copy-done((bf16[128,768]{1,0:T(8,128)(2,1)S(1)}, bf16[128,768]{1,0:T(8,128)(2,1)}, u32[]{:S(2)}) %copy-start.8) | copy-done | bytes 196632
  2.2 0.4 pack.1
  2.7 0.0 copy-start.3
  2.7 0.9 %copy-done.3 = bf16[128,768]{1,0:T(8,128)(2,1)S(1)} copy-done((bf16[128,768]{1,0:T(8,128)(2,1)S(1)}, bf16[128,768]{1,0:T(8,128)(2,1)}, u32[]{:S(2)}) %copy-start.3) | copy-done | bytes 196632
  3.6 0.7 copy-done.6
  4.3 0.3 pack_cot.1
  4.6 3.1 %collective-permute-start = (bf16[160,768]{1,0:T(8,128)(2,1)S(1)}, bf16[160,768]{1,0:T(8,128)(2,1)S(1)}, u32[]{:S(2)}, u32[]{:S(2)}) collective-permute-start(bf16[160,768]{1,0:T(8,128)(2,1)S(1)} %get-tuple-element.47), channel_id=1, source_target_pairs={{0,4},{4,0},{8,12},{12,8},{1,5},{5,1},{9,13},{13,9},{2,6},{6,2},{1... | collective-permute-start | bytes 737288 | tf_op jit(solution)/shard_map/ppermute | solution.py:18
  7.7 2.6 %collective-permute-start.1 = (bf16[80,768]{1,0:T(8,128)(2,1)S(1)}, bf16[80,768]{1,0:T(8,128)(2,1)S(1)}, u32[]{:S(2)}, u32[]{:S(2)}) collective-permute-start(bf16[80,768]{1,0:T(8,128)(2,1)S(1)} %get-tuple-element.48), channel_id=1, source_target_pairs={{0,8},{4,12},{8,0},{12,4},{1,9},{5,13},{9,1},{13,5},{2,10},{6,14},... | collective-permute-start | bytes 368648 | tf_op jit(solution)/shard_map/ppermute | solution.py:18
  10.2 1.9 %collective-permute-start.8 = (bf16[80,768]{1,0:T(8,128)(2,1)S(1)}, bf16[80,768]{1,0:T(8,128)(2,1)S(1)}, u32[]{:S(2)}, u32[]{:S(2)}) collective-permute-start(bf16[80,768]{1,0:T(8,128)(2,1)S(1)} %get-tuple-element.41), channel_id=1, source_target_pairs={{0,8},{4,12},{8,0},{12,4},{1,9},{5,13},{9,1},{13,5},{2,10},{6,14},... | collective-permute-start | bytes 368648 | tf_op jit(solution)/shard_map/ppermute | solution.py:18
  12.2 1.9 %collective-permute-start.9 = (bf16[80,768]{1,0:T(8,128)(2,1)S(1)}, bf16[80,768]{1,0:T(8,128)(2,1)S(1)}, u32[]{:S(2)}, u32[]{:S(2)}) collective-permute-start(bf16[80,768]{1,0:T(8,128)(2,1)S(1)} %get-tuple-element.58), channel_id=1, source_target_pairs={{0,12},{4,8},{8,4},{12,0},{1,13},{5,9},{9,5},{13,1},{2,14},{6,10},... | collective-permute-start | bytes 368648 | tf_op jit(solution)/shard_map/ppermute | solution.py:18
  14.1 1.3 %copy-done = bf16[1,768,768]{2,1,0:T(8,128)(2,1)S(1)} copy-done((bf16[1,768,768]{2,1,0:T(8,128)(2,1)S(1)}, bf16[1,768,768]{2,1,0:T(8,128)(2,1)}, u32[]{:S(2)}) %copy-start) | copy-done | bytes 1179672
  15.3 1.3 %copy-done.1 = bf16[1,768,768]{2,1,0:T(8,128)(2,1)S(1)} copy-done((bf16[1,768,768]{2,1,0:T(8,128)(2,1)S(1)}, bf16[1,768,768]{2,1,0:T(8,128)(2,1)}, u32[]{:S(2)}) %copy-start.1) | copy-done | bytes 1179672
  16.6 1.3 %copy-done.2 = bf16[1,768,768]{2,1,0:T(8,128)(2,1)S(1)} copy-done((bf16[1,768,768]{2,1,0:T(8,128)(2,1)S(1)}, bf16[1,768,768]{2,1,0:T(8,128)(2,1)}, u32[]{:S(2)}) %copy-start.2) | copy-done | bytes 1179672
  17.9 0.7 load.1
  18.6 0.0 collective-permute-done.1.refs_2_
  18.7 3.7 %collective-permute-done.2.refs_3_ = bf16[80,768]{1,0:T(8,128)(2,1)S(1)} collective-permute-done((bf16[80,768]{1,0:T(8,128)(2,1)S(1)}, bf16[80,768]{1,0:T(8,128)(2,1)S(1)}, u32[]{:S(2)}, u32[]{:S(2)}) %collective-permute-start.2) | collective-permute-done | bytes 122912 | tf_op jit(solution)/shard_map/ppermute | solution.py:18
  22.3 0.0 collective-permute-done.refs_1_
  22.3 0.9 %up.1 = bf16[2,160,1536]{2,1,0:T(8,128)(2,1)S(1)} custom-call(s32[1]{0:T(128)} %bitcast.3.half_ref, bf16[160,768]{1,0:T(8,128)(2,1)S(1)} %get-tuple-element.46.refs_0_, bf16[160,768]{1,0:T(8,128)(2,1)S(1)} %collective-permute-done.refs_1_, bf16[80,768]{1,0:T(8,128)(2,1)S(1)} %collective-permute-done.1.refs_2_, ...), custom_call_target="tpu_custom_call" | custom-call | flops 754974720 | bytes 4079620 | tf_op jit(solution)/shard_map/up/pallas_call | solution.py:39
  23.3 4.5 %all_to_all.5 = bf16[2,160,1536]{2,1,0:T(8,128)(2,1)S(1)} all-to-all(bf16[2,160,1536]{2,1,0:T(8,128)(2,1)S(1)} %up.1), channel_id=1, replica_groups={{0,1},{2,3},{4,5},{6,7},{8,9},{10,11},{12,13},{14,15},{16,17},{18,19},{..., dimensions={0} | all-to-all | bytes 1966080 | tf_op jit(solution)/shard_map/all_to_all | solution.py:286
  27.8 0.1 fusion
  27.9 1.6 %collective-permute-start.3 = (bf16[160,1536]{1,0:T(8,128)(2,1)S(1)}, bf16[160,1536]{1,0:T(8,128)(2,1)S(1)}, u32[]{:S(2)}, u32[]{:S(2)}) collective-permute-start(bf16[160,1536]{1,0:T(8,128)(2,1)S(1)} %fusion), channel_id=1, source_target_pairs={{0,2},{1,3},{2,0},{3,1},{4,6},{5,7},{6,4},{7,5},{8,10},{9,11},{10,... | collective-permute-start | bytes 1474568 | tf_op jit(solution)/shard_map/ppermute | solution.py:18
  29.4 1.1 %collective-permute-done.8.refs_2_.refs_4_ = bf16[80,768]{1,0:T(8,128)(2,1)S(1)} collective-permute-done((bf16[80,768]{1,0:T(8,128)(2,1)S(1)}, bf16[80,768]{1,0:T(8,128)(2,1)S(1)}, u32[]{:S(2)}, u32[]{:S(2)}) %collective-permute-start.8) | collective-permute-done | bytes 122912 | tf_op jit(solution)/shard_map/ppermute | solution.py:18
  30.5 0.6 back.1
  31.1 0.1 collective-permute-start.10
  31.2 1.5 %collective-permute-done.10 = bf16[160,768]{1,0:T(8,128)(2,1)S(1)} collective-permute-done((bf16[160,768]{1,0:T(8,128)(2,1)S(1)}, bf16[160,768]{1,0:T(8,128)(2,1)S(1)}, u32[]{:S(2)}, u32[]{:S(2)}) %collective-permute-start.10) | collective-permute-done | bytes 245792 | tf_op jit(solution)/shard_map/ppermute | solution.py:18
  32.7 0.1 add_convert_fusion.3
  32.8 1.6 %collective-permute-start.11 = (bf16[160,768]{1,0:T(8,128)(2,1)S(1)}, bf16[160,768]{1,0:T(8,128)(2,1)S(1)}, u32[]{:S(2)}, u32[]{:S(2)}) collective-permute-start(bf16[160,768]{1,0:T(8,128)(2,1)S(1)} %add_convert_fusion.3), channel_id=1, source_target_pairs={{0,2},{1,3},{2,0},{3,1},{4,6},{5,7},{6,4},{7,5},{8,10},{9,11},{10,... | collective-permute-start | bytes 737288 | tf_op jit(solution)/shard_map/ppermute | solution.py:18
  34.3 7.7 %collective-permute-done.3 = bf16[160,1536]{1,0:T(8,128)(2,1)S(1)} collective-permute-done((bf16[160,1536]{1,0:T(8,128)(2,1)S(1)}, bf16[160,1536]{1,0:T(8,128)(2,1)S(1)}, u32[]{:S(2)}, u32[]{:S(2)}) %collective-permute-start.3) | collective-permute-done | bytes 491552 | tf_op jit(solution)/shard_map/ppermute | solution.py:18
  42.0 0.2 add_convert_fusion.refs_0_
  42.2 0.1 collective-permute-start.4
  42.3 4.2 %collective-permute-done.11 = bf16[160,768]{1,0:T(8,128)(2,1)S(1)} collective-permute-done((bf16[160,768]{1,0:T(8,128)(2,1)S(1)}, bf16[160,768]{1,0:T(8,128)(2,1)S(1)}, u32[]{:S(2)}, u32[]{:S(2)}) %collective-permute-start.11) | collective-permute-done | bytes 245792 | tf_op jit(solution)/shard_map/ppermute | solution.py:18
  46.5 0.1 add_convert_fusion.2.refs_0_
  46.6 0.1 collective-permute-start.12
  46.6 0.7 out.1
  47.4 6.3 %collective-permute-start.5 = (bf16[80,768]{1,0:T(8,128)(2,1)S(1)}, bf16[80,768]{1,0:T(8,128)(2,1)S(1)}, u32[]{:S(2)}, u32[]{:S(2)}) collective-permute-start(bf16[80,768]{1,0:T(8,128)(2,1)S(1)} %get-tuple-element.53), channel_id=1, source_target_pairs={{0,4},{4,0},{8,12},{12,8},{1,5},{5,1},{9,13},{13,9},{2,6},{6,2},{1... | collective-permute-start | bytes 368648 | tf_op jit(solution)/shard_map/ppermute | solution.py:18
  53.7 1.1 %collective-permute-start.6 = (bf16[80,768]{1,0:T(8,128)(2,1)S(1)}, bf16[80,768]{1,0:T(8,128)(2,1)S(1)}, u32[]{:S(2)}, u32[]{:S(2)}) collective-permute-start(bf16[80,768]{1,0:T(8,128)(2,1)S(1)} %get-tuple-element.54), channel_id=1, source_target_pairs={{0,8},{4,12},{8,0},{12,4},{1,9},{5,13},{9,1},{13,5},{2,10},{6,14},... | collective-permute-start | bytes 368648 | tf_op jit(solution)/shard_map/ppermute | solution.py:18
  54.8 1.4 %collective-permute-start.7 = (bf16[80,768]{1,0:T(8,128)(2,1)S(1)}, bf16[80,768]{1,0:T(8,128)(2,1)S(1)}, u32[]{:S(2)}, u32[]{:S(2)}) collective-permute-start(bf16[80,768]{1,0:T(8,128)(2,1)S(1)} %get-tuple-element.55), channel_id=1, source_target_pairs={{0,12},{4,8},{8,4},{12,0},{1,13},{5,9},{9,5},{13,1},{2,14},{6,10},... | collective-permute-start | bytes 368648 | tf_op jit(solution)/shard_map/ppermute | solution.py:18
  56.2 1.2 %dx.1 = (bf16[80,768]{1,0:T(8,128)(2,1)S(1)}, bf16[80,768]{1,0:T(8,128)(2,1)S(1)}, bf16[80,768]{1,0:T(8,128)(2,1)S(1)}, bf16[80,768]{1,0:T(8,128)(2,1)S(1)}, bf1...) custom-call(s32[1]{0:T(128)} %bitcast.3.half_ref, bf16[2,160,1536]{2,1,0:T(8,128)(2,1)S(1)} %get-tuple-element.56.sums_ref, ...), custom_call_target="tpu_custom_call" | custom-call | flops 754974720 | bytes 5799940 | tf_op jit(solution)/shard_map/dx/pallas_call | solution.py:39
  57.4 1.1 %collective-permute-start.13 = (bf16[80,768]{1,0:T(8,128)(2,1)S(1)}, bf16[80,768]{1,0:T(8,128)(2,1)S(1)}, u32[]{:S(2)}, u32[]{:S(2)}) collective-permute-start(bf16[80,768]{1,0:T(8,128)(2,1)S(1)} %get-tuple-element.62), channel_id=1, source_target_pairs={{0,4},{4,0},{8,12},{12,8},{1,5},{5,1},{9,13},{13,9},{2,6},{6,2},{1... | collective-permute-start | bytes 368648 | tf_op jit(solution)/shard_map/ppermute | solution.py:18
  58.4 2.0 %collective-permute-start.14 = (bf16[80,768]{1,0:T(8,128)(2,1)S(1)}, bf16[80,768]{1,0:T(8,128)(2,1)S(1)}, u32[]{:S(2)}, u32[]{:S(2)}) collective-permute-start(bf16[80,768]{1,0:T(8,128)(2,1)S(1)} %get-tuple-element.63), channel_id=1, source_target_pairs={{0,8},{4,12},{8,0},{12,4},{1,9},{5,13},{9,1},{13,5},{2,10},{6,14},... | collective-permute-start | bytes 368648 | tf_op jit(solution)/shard_map/ppermute | solution.py:18
  60.4 1.4 %collective-permute-start.15 = (bf16[80,768]{1,0:T(8,128)(2,1)S(1)}, bf16[80,768]{1,0:T(8,128)(2,1)S(1)}, u32[]{:S(2)}, u32[]{:S(2)}) collective-permute-start(bf16[80,768]{1,0:T(8,128)(2,1)S(1)} %get-tuple-element.64), channel_id=1, source_target_pairs={{0,12},{4,8},{8,4},{12,0},{1,13},{5,9},{9,5},{13,1},{2,14},{6,10},... | collective-permute-start | bytes 368648 | tf_op jit(solution)/shard_map/ppermute | solution.py:18
  61.8 3.1 %grads.1 = (bf16[768,768]{1,0:T(8,128)(2,1)}, bf16[768,768]{1,0:T(8,128)(2,1)}, bf16[768,768]{1,0:T(8,128)(2,1)}) custom-call(bf16[160,768]{1,0:T(8,128)(2,1)S(1)} %get-tuple-element.46.refs_0_, bf16[160,768]{1,0:T(8,128)(2,1)S(1)} %collective-permute-done.refs_1_, bf16[80,768]{1,0:T(8,128)(2,1)S(1)} %collective-permute-done.1.refs_2_, ...), custom_call_target="tpu_custom_call" | custom-call | flops 1132462080 | bytes 5996544 | tf_op jit(solution)/shard_map/grads/pallas_call | solution.py:39
  64.9 1.2 %collective-permute-done.6.refs_2_ = bf16[80,768]{1,0:T(8,128)(2,1)S(1)} collective-permute-done((bf16[80,768]{1,0:T(8,128)(2,1)S(1)}, bf16[80,768]{1,0:T(8,128)(2,1)S(1)}, u32[]{:S(2)}, u32[]{:S(2)}) %collective-permute-start.6) | collective-permute-done | bytes 122912 | tf_op jit(solution)/shard_map/ppermute | solution.py:18
  66.1 1.1 %mix.1 = bf16[128,768]{1,0:T(8,128)(2,1)} custom-call(s32[1]{0:T(128)} %bitcast.me_ref, s32[2,128]{1,0:T(2,128)S(1)} %bitcast.20, f32[2,128]{1,0:T(2,128)S(1)} %bitcast.23, bf16[320,128]{1,0:T(8,128)(2,1)S(1)} %get-tuple-element.39.place_ref, bf16[80,768]{1,0:T(8,128)(2,1)S(1)} %get-tuple-element.52.refs_0_, ...), custom_call_target="tpu_custom_call" | custom-call | flops 125829120 | bytes 772100 | tf_op jit(solution)/shard_map/mix/pallas_call | solution.py:39
  67.2 9.4 %collective-permute-done.14.refs_2_ = bf16[80,768]{1,0:T(8,128)(2,1)S(1)} collective-permute-done((bf16[80,768]{1,0:T(8,128)(2,1)S(1)}, bf16[80,768]{1,0:T(8,128)(2,1)S(1)}, u32[]{:S(2)}, u32[]{:S(2)}) %collective-permute-start.14) | collective-permute-done | bytes 122912 | tf_op jit(solution)/shard_map/ppermute | solution.py:18
  76.6 1.0 %merge.1 = (bf16[128,768]{1,0:T(8,128)(2,1)}, f32[2,128]{1,0:T(2,128)}) custom-call(s32[1]{0:T(128)} %bitcast.me_ref, s32[2,128]{1,0:T(2,128)S(1)} %bitcast.21, f32[2,128]{1,0:T(2,128)S(1)} %bitcast.24, bf16[320,128]{1,0:T(8,128)(2,1)S(1)} %get-tuple-element.39.place_ref, bf16[80,768]{1,0:T(8,128)(2,1)S(1)} %get-tuple-element.61.refs_0_, ...), custom_call_target="tpu_custom_call" | custom-call | flops 62914560 | bytes 773124 | tf_op jit(solution)/shard_map/merge/pallas_call | solution.py:39
  (17 shorter events, 0.0 us)
Async XLA Ops:
  0.6 0.7 copy-start.4
  1.3 0.9 %copy-start.8 = (bf16[128,768]{1,0:T(8,128)(2,1)S(1)}, bf16[128,768]{1,0:T(8,128)(2,1)}, u32[]{:S(2)}) copy-start(bf16[128,768]{1,0:T(8,128)(2,1)} %tokens_ref.1) | copy-start | bytes 589828
  2.7 0.9 %copy-start.3 = (bf16[128,768]{1,0:T(8,128)(2,1)S(1)}, bf16[128,768]{1,0:T(8,128)(2,1)}, u32[]{:S(2)}) copy-start(bf16[128,768]{1,0:T(8,128)(2,1)} %cot_ref.1) | copy-start | bytes 589828
  3.6 0.7 copy-start.6
  4.6 17.8 %collective-permute-start = (bf16[160,768]{1,0:T(8,128)(2,1)S(1)}, bf16[160,768]{1,0:T(8,128)(2,1)S(1)}, u32[]{:S(2)}, u32[]{:S(2)}) collective-permute-start(bf16[160,768]{1,0:T(8,128)(2,1)S(1)} %get-tuple-element.47), channel_id=1, source_target_pairs={{0,4},{4,0},{8,12},{12,8},{1,5},{5,1},{9,13},{13,9},{2,6},{6,2},{1... | collective-permute-start | bytes 737288 | tf_op jit(solution)/shard_map/ppermute | solution.py:18
  7.7 11.0 %collective-permute-start.1 = (bf16[80,768]{1,0:T(8,128)(2,1)S(1)}, bf16[80,768]{1,0:T(8,128)(2,1)S(1)}, u32[]{:S(2)}, u32[]{:S(2)}) collective-permute-start(bf16[80,768]{1,0:T(8,128)(2,1)S(1)} %get-tuple-element.48), channel_id=1, source_target_pairs={{0,8},{4,12},{8,0},{12,4},{1,9},{5,13},{9,1},{13,5},{2,10},{6,14},... | collective-permute-start | bytes 368648 | tf_op jit(solution)/shard_map/ppermute | solution.py:18
  10.2 12.1 %collective-permute-start.2 = (bf16[80,768]{1,0:T(8,128)(2,1)S(1)}, bf16[80,768]{1,0:T(8,128)(2,1)S(1)}, u32[]{:S(2)}, u32[]{:S(2)}) collective-permute-start(bf16[80,768]{1,0:T(8,128)(2,1)S(1)} %get-tuple-element.49), channel_id=1, source_target_pairs={{0,12},{4,8},{8,4},{12,0},{1,13},{5,9},{9,5},{13,1},{2,14},{6,10},... | collective-permute-start | bytes 368648 | tf_op jit(solution)/shard_map/ppermute | solution.py:18
  10.2 20.3 %collective-permute-start.8 = (bf16[80,768]{1,0:T(8,128)(2,1)S(1)}, bf16[80,768]{1,0:T(8,128)(2,1)S(1)}, u32[]{:S(2)}, u32[]{:S(2)}) collective-permute-start(bf16[80,768]{1,0:T(8,128)(2,1)S(1)} %get-tuple-element.41), channel_id=1, source_target_pairs={{0,8},{4,12},{8,0},{12,4},{1,9},{5,13},{9,1},{13,5},{2,10},{6,14},... | collective-permute-start | bytes 368648 | tf_op jit(solution)/shard_map/ppermute | solution.py:18
  12.2 18.3 %collective-permute-start.9 = (bf16[80,768]{1,0:T(8,128)(2,1)S(1)}, bf16[80,768]{1,0:T(8,128)(2,1)S(1)}, u32[]{:S(2)}, u32[]{:S(2)}) collective-permute-start(bf16[80,768]{1,0:T(8,128)(2,1)S(1)} %get-tuple-element.58), channel_id=1, source_target_pairs={{0,12},{4,8},{8,4},{12,0},{1,13},{5,9},{9,5},{13,1},{2,14},{6,10},... | collective-permute-start | bytes 368648 | tf_op jit(solution)/shard_map/ppermute | solution.py:18
  14.1 1.3 %copy-start = (bf16[1,768,768]{2,1,0:T(8,128)(2,1)S(1)}, bf16[1,768,768]{2,1,0:T(8,128)(2,1)}, u32[]{:S(2)}) copy-start(bf16[1,768,768]{2,1,0:T(8,128)(2,1)} %param.11) | copy-start | bytes 3538948
  15.3 1.3 %copy-start.1 = (bf16[1,768,768]{2,1,0:T(8,128)(2,1)S(1)}, bf16[1,768,768]{2,1,0:T(8,128)(2,1)}, u32[]{:S(2)}) copy-start(bf16[1,768,768]{2,1,0:T(8,128)(2,1)} %param.12) | copy-start | bytes 3538948
  16.6 1.3 %copy-start.2 = (bf16[1,768,768]{2,1,0:T(8,128)(2,1)S(1)}, bf16[1,768,768]{2,1,0:T(8,128)(2,1)}, u32[]{:S(2)}) copy-start(bf16[1,768,768]{2,1,0:T(8,128)(2,1)} %param.13) | copy-start | bytes 3538948
  27.9 14.1 %collective-permute-start.3 = (bf16[160,1536]{1,0:T(8,128)(2,1)S(1)}, bf16[160,1536]{1,0:T(8,128)(2,1)S(1)}, u32[]{:S(2)}, u32[]{:S(2)}) collective-permute-start(bf16[160,1536]{1,0:T(8,128)(2,1)S(1)} %fusion), channel_id=1, source_target_pairs={{0,2},{1,3},{2,0},{3,1},{4,6},{5,7},{6,4},{7,5},{8,10},{9,11},{10,... | collective-permute-start | bytes 1474568 | tf_op jit(solution)/shard_map/ppermute | solution.py:18
  31.1 1.6 %collective-permute-start.10 = (bf16[160,768]{1,0:T(8,128)(2,1)S(1)}, bf16[160,768]{1,0:T(8,128)(2,1)S(1)}, u32[]{:S(2)}, u32[]{:S(2)}) collective-permute-start(bf16[160,768]{1,0:T(8,128)(2,1)S(1)} %get-tuple-element.60), channel_id=1, source_target_pairs={{0,1},{1,0},{2,3},{3,2},{4,5},{5,4},{6,7},{7,6},{8,9},{9,8},{10,11... | collective-permute-start | bytes 737288 | tf_op jit(solution)/shard_map/ppermute | solution.py:18
  32.8 13.7 %collective-permute-start.11 = (bf16[160,768]{1,0:T(8,128)(2,1)S(1)}, bf16[160,768]{1,0:T(8,128)(2,1)S(1)}, u32[]{:S(2)}, u32[]{:S(2)}) collective-permute-start(bf16[160,768]{1,0:T(8,128)(2,1)S(1)} %add_convert_fusion.3), channel_id=1, source_target_pairs={{0,2},{1,3},{2,0},{3,1},{4,6},{5,7},{6,4},{7,5},{8,10},{9,11},{10,... | collective-permute-start | bytes 737288 | tf_op jit(solution)/shard_map/ppermute | solution.py:18
  42.2 4.4 %collective-permute-start.4 = (bf16[160,1536]{1,0:T(8,128)(2,1)S(1)}, bf16[160,1536]{1,0:T(8,128)(2,1)S(1)}, u32[]{:S(2)}, u32[]{:S(2)}) collective-permute-start(bf16[160,1536]{1,0:T(8,128)(2,1)S(1)} %add_convert_fusion.refs_0_), channel_id=1, source_target_pairs={{0,1},{1,0},{2,3},{3,2},{4,5},{5,4},{6,7},{7,6},{8,9},{9,8},{10,11... | collective-permute-start | bytes 1474568 | tf_op jit(solution)/shard_map/ppermute | solution.py:18
  46.6 9.6 %collective-permute-start.12 = (bf16[160,768]{1,0:T(8,128)(2,1)S(1)}, bf16[160,768]{1,0:T(8,128)(2,1)S(1)}, u32[]{:S(2)}, u32[]{:S(2)}) collective-permute-start(bf16[160,768]{1,0:T(8,128)(2,1)S(1)} %add_convert_fusion.2.refs_0_), channel_id=1, source_target_pairs={{0,1},{1,0},{2,3},{3,2},{4,5},{5,4},{6,7},{7,6},{8,9},{9,8},{10,11... | collective-permute-start | bytes 737288 | tf_op jit(solution)/shard_map/ppermute | solution.py:18
  47.4 13.0 %collective-permute-start.5 = (bf16[80,768]{1,0:T(8,128)(2,1)S(1)}, bf16[80,768]{1,0:T(8,128)(2,1)S(1)}, u32[]{:S(2)}, u32[]{:S(2)}) collective-permute-start(bf16[80,768]{1,0:T(8,128)(2,1)S(1)} %get-tuple-element.53), channel_id=1, source_target_pairs={{0,4},{4,0},{8,12},{12,8},{1,5},{5,1},{9,13},{13,9},{2,6},{6,2},{1... | collective-permute-start | bytes 368648 | tf_op jit(solution)/shard_map/ppermute | solution.py:18
  53.7 12.4 %collective-permute-start.6 = (bf16[80,768]{1,0:T(8,128)(2,1)S(1)}, bf16[80,768]{1,0:T(8,128)(2,1)S(1)}, u32[]{:S(2)}, u32[]{:S(2)}) collective-permute-start(bf16[80,768]{1,0:T(8,128)(2,1)S(1)} %get-tuple-element.54), channel_id=1, source_target_pairs={{0,8},{4,12},{8,0},{12,4},{1,9},{5,13},{9,1},{13,5},{2,10},{6,14},... | collective-permute-start | bytes 368648 | tf_op jit(solution)/shard_map/ppermute | solution.py:18
  54.8 11.3 %collective-permute-start.7 = (bf16[80,768]{1,0:T(8,128)(2,1)S(1)}, bf16[80,768]{1,0:T(8,128)(2,1)S(1)}, u32[]{:S(2)}, u32[]{:S(2)}) collective-permute-start(bf16[80,768]{1,0:T(8,128)(2,1)S(1)} %get-tuple-element.55), channel_id=1, source_target_pairs={{0,12},{4,8},{8,4},{12,0},{1,13},{5,9},{9,5},{13,1},{2,14},{6,10},... | collective-permute-start | bytes 368648 | tf_op jit(solution)/shard_map/ppermute | solution.py:18
  57.4 9.8 %collective-permute-start.13 = (bf16[80,768]{1,0:T(8,128)(2,1)S(1)}, bf16[80,768]{1,0:T(8,128)(2,1)S(1)}, u32[]{:S(2)}, u32[]{:S(2)}) collective-permute-start(bf16[80,768]{1,0:T(8,128)(2,1)S(1)} %get-tuple-element.62), channel_id=1, source_target_pairs={{0,4},{4,0},{8,12},{12,8},{1,5},{5,1},{9,13},{13,9},{2,6},{6,2},{1... | collective-permute-start | bytes 368648 | tf_op jit(solution)/shard_map/ppermute | solution.py:18
  58.4 18.2 %collective-permute-start.14 = (bf16[80,768]{1,0:T(8,128)(2,1)S(1)}, bf16[80,768]{1,0:T(8,128)(2,1)S(1)}, u32[]{:S(2)}, u32[]{:S(2)}) collective-permute-start(bf16[80,768]{1,0:T(8,128)(2,1)S(1)} %get-tuple-element.63), channel_id=1, source_target_pairs={{0,8},{4,12},{8,0},{12,4},{1,9},{5,13},{9,1},{13,5},{2,10},{6,14},... | collective-permute-start | bytes 368648 | tf_op jit(solution)/shard_map/ppermute | solution.py:18
  60.4 16.2 %collective-permute-start.15 = (bf16[80,768]{1,0:T(8,128)(2,1)S(1)}, bf16[80,768]{1,0:T(8,128)(2,1)S(1)}, u32[]{:S(2)}, u32[]{:S(2)}) collective-permute-start(bf16[80,768]{1,0:T(8,128)(2,1)S(1)} %get-tuple-element.64), channel_id=1, source_target_pairs={{0,12},{4,8},{8,4},{12,0},{1,13},{5,9},{9,5},{13,1},{2,14},{6,10},... | collective-permute-start | bytes 368648 | tf_op jit(solution)/shard_map/ppermute | solution.py:18
  61.8 4.3 %copy-start.5 = (s32[128,2]{0,1:T(2,128)S(1)}, s32[128,2]{0,1:T(2,128)}, u32[]{:S(2)}) copy-start(s32[128,2]{0,1:T(2,128)} %param.9) | copy-start | bytes 3076
  61.8 4.3 %copy-start.7 = (f32[128,2]{0,1:T(2,128)S(1)}, f32[128,2]{0,1:T(2,128)}, u32[]{:S(2)}) copy-start(f32[128,2]{0,1:T(2,128)} %param.10) | copy-start | bytes 3076

commit v3 on v2

--- a/solution.py
+++ b/solution.py
@@ -10,7 +10,8 @@
 BF = jnp.bfloat16
 F32 = jnp.float32
 VMEM_BYTES = 40 * 1024 * 1024
-SYNC = (True, False, False, False)
+DH_AFTER = True
+SYNC = (False, False, False, True)
 
 
 def swap(block, axis, offset):
@@ -59,8 +60,7 @@
 
 
 def pack_kernel(peers, me_ref, routes_ref, tokens_ref, *refs):
-    near = peers // 2
-    near_ref, x_refs, place_ref = refs[0], refs[1 : 1 + near], refs[1 + near]
+    x_refs, place_ref = refs[:peers], refs[peers]
     me = me_ref[0]
     count = routes_ref.shape[1]
     rows = x_refs[0].shape[0]
@@ -77,15 +77,12 @@
         part = slice(j * rows, (j + 1) * rows)
         place_ref[part, :] = (slot == rank[j : j + 1]).astype(F32).astype(BF)
     tokens = tokens_ref[...]
-    for j in range(near):
-        part = slice((near + j) * rows, (near + j + 1) * rows)
+    for j in reversed(range(peers)):
+        part = slice(j * rows, (j + 1) * rows)
         x_refs[j][...] = dot(place_ref[part, :], tokens).astype(BF)
-    near_ref[...] = dot(place_ref[: near * rows, :], tokens).astype(BF)
-
-
-def pack_cot_kernel(peers, me_ref, routes_ref, gates_ref, cot_ref, x_ref, place_ref, *refs):
-    near = peers // 2
-    pair_refs, c_refs = refs[:near], refs[near:]
+
+
+def pack_cot_kernel(peers, me_ref, routes_ref, gates_ref, cot_ref, place_ref, *c_refs):
     me = me_ref[0]
     rows = c_refs[0].shape[0]
     routes, gates = routes_ref[...], gates_ref[...]
@@ -94,12 +91,7 @@
         place = place_ref[j * rows : (j + 1) * rows, :]
         gate = gate_row(routes, gates, me ^ j)
         scale = jnp.sum(place.astype(F32) * gate, axis=1, keepdims=True)
-        c = (dot(place, cot) * scale).astype(BF)
-        if j < near:
-            pair_refs[j][:rows, :] = x_ref[j * rows : (j + 1) * rows, :]
-            pair_refs[j][rows:, :] = c
-        else:
-            c_refs[j - near][...] = c
+        c_refs[j][...] = (dot(place, cot) * scale).astype(BF)
 
 
 def load_kernel(*refs):
@@ -140,25 +132,17 @@
     return jnp.concatenate([r[part, :] for r in refs], axis=0)
 
 
-def rows_of(pair_refs, refs, which):
-    cp = refs[0].shape[0]
-    return jnp.concatenate(
-        [stack(pair_refs, slice(which * cp, (which + 1) * cp)), stack(refs)], axis=0
-    )
-
-
-def up_kernel(near, half_ref, *refs):
-    pair_refs, x_refs, (gate_ref, up_ref, *to_refs) = refs[:near], refs[near : 2 * near], refs[2 * near :]
-    x = rows_of(pair_refs, x_refs, 0)
+def up_kernel(peers, half_ref, *refs):
+    x_refs, (gate_ref, up_ref, *to_refs) = refs[:peers], refs[peers:]
+    x = stack(x_refs)
     width = gate_ref.shape[1]
     hand_out((half_ref[0], 0), dot(x, gate_ref[...]).astype(BF), to_refs)
     hand_out((half_ref[0], width), dot(x, up_ref[...]).astype(BF), to_refs)
 
 
-def back_kernel(near, half_ref, *refs):
-    pair_refs, c_refs, (down_ref, *to_refs) = refs[:near], refs[near : 2 * near], refs[2 * near :]
-    c = rows_of(pair_refs, c_refs, 1)
-    hand_out((half_ref[0], 0), dot_nt(c, down_ref[...]).astype(BF), to_refs)
+def back_kernel(peers, half_ref, *refs):
+    c_refs, (down_ref, *to_refs) = refs[:peers], refs[peers:]
+    hand_out((half_ref[0], 0), dot_nt(stack(c_refs), down_ref[...]).astype(BF), to_refs)
 
 
 def activate(g, u):
@@ -226,13 +210,13 @@
         store_dx(cap, dx_refs[j], dx[part], dot_ref[part, :])
 
 
-def grad_kernel(near, *refs):
-    pair_refs, x_refs, c_refs = refs[:near], refs[near : 2 * near], refs[2 * near : 3 * near]
-    hidden_ref, dgate_ref, dup_ref, gg_ref, gu_ref, gd_ref = refs[3 * near :]
-    x = rows_of(pair_refs, x_refs, 0)
+def grad_kernel(peers, *refs):
+    x_refs, c_refs = refs[:peers], refs[peers : 2 * peers]
+    hidden_ref, dgate_ref, dup_ref, gg_ref, gu_ref, gd_ref = refs[2 * peers :]
+    x = stack(x_refs)
     gg_ref[...] = dot_tn(x, dgate_ref[...]).astype(BF)
     gu_ref[...] = dot_tn(x, dup_ref[...]).astype(BF)
-    gd_ref[...] = dot_tn(hidden_ref[...], rows_of(pair_refs, c_refs, 1)).astype(BF)
+    gd_ref[...] = dot_tn(hidden_ref[...], stack(c_refs)).astype(BF)
 
 
 def mix_kernel(peers, me_ref, routes_ref, gates_ref, place_ref, *refs):
@@ -281,7 +265,7 @@
     return [[i, i + 1] for i in range(0, count, 2)]
 
 
-def reduced(parts, dp_count):
+def reduced(parts, dp_count, first=()):
     if len(parts) == 1:
         arrived = lax.all_to_all(parts[0], "dp", 0, 0, axis_index_groups=pairs_of(dp_count))
         total = added(arrived[0], arrived[1])
@@ -289,8 +273,11 @@
         total = added(parts[0], swap(parts[1], "dp", 1))
     bit = 2
     while bit < dp_count:
-        total = added(total, swap(total, "dp", bit))
+        arrived = swap(total, "dp", bit)
         bit *= 2
+        if first and bit >= dp_count:
+            (arrived,) = after(first, (arrived,))
+        total = added(total, arrived)
     return total
 
 
@@ -319,22 +306,21 @@
     def sds(shape, dtype=BF):
         return jax.ShapeDtypeStruct(shape, dtype)
 
-    part, pair = sds((cp, width)), sds((2 * cp, width))
-    near_x, *xs, place = call(
+    part = sds((cp, width))
+    *xs, place = call(
         functools.partial(pack_kernel, peers),
         "pack",
-        [sds((rows, width))] + [part] * near + [sds((2 * rows, count))],
+        [part] * peers + [sds((2 * rows, count))],
         (me, routes_t, tokens),
         flops=4 * rows * count * width,
     )
-    packed = call(
+    cs = call(
         functools.partial(pack_cot_kernel, peers),
         "pack_cot",
-        [pair] * near + [part] * near,
-        (me, routes_t, gates_t, cotangent, near_x, place),
+        [part] * peers,
+        (me, routes_t, gates_t, cotangent, place),
         flops=4 * rows * count * width,
     )
-    xcs, cs = packed[:near], packed[near:]
     weights = lax.optimization_barrier((gate_w, up_w, down_w, cs[0]))[:3]
     gate_w, up_w, down_w = call(
         load_kernel,
@@ -344,30 +330,28 @@
         scalars=0,
         scratch=[pltpu.SemaphoreType.DMA((3,))],
     )
-    xs = [swap(xs[j], "expert", near + j) for j in range(near)]
-    xcs = [xcs[0]] + [swap(xcs[j], "expert", j) for j in range(1, near)]
-    cs = [swap(cs[j], "expert", near + j) for j in range(near)]
+    xs = [xs[0]] + [swap(xs[j], "expert", j) for j in range(1, peers)]
+    cs = [cs[0]] + [swap(cs[j], "expert", j) for j in range(1, peers)]
     work = 2 * rows * width * ff
 
     def parts_of(waits, wide):
         return [sds((2, rows, wide))] if waits else [sds((rows, wide))] * 2
 
     up_parts = call(
-        functools.partial(up_kernel, near),
+        functools.partial(up_kernel, peers),
         "up",
         parts_of(SYNC[0], 2 * ff),
-        (half, *xcs, *xs, gate_w, up_w),
+        (half, *xs, gate_w, up_w),
         flops=4 * work,
     )
     up_sum = reduced(up_parts, dp_count)
     dh_parts = call(
-        functools.partial(back_kernel, near),
+        functools.partial(back_kernel, peers),
         "back",
         parts_of(SYNC[1], ff),
-        (half, *xcs, *cs, down_w),
+        (half, *cs, down_w),
         flops=2 * work,
     )
-    dh_sum = reduced(dh_parts, dp_count)
     up_both = whole(up_sum, dp_count, SYNC[2])
     produced = call(
         functools.partial(out_kernel, peers, SYNC[2]),
@@ -378,6 +362,7 @@
     )
     outs, hidden = produced[:peers], produced[peers]
     sums = up_both[0] if SYNC[2] else produced[-1]
+    dh_sum = reduced(dh_parts, dp_count, DH_AFTER and (outs[0],))
     *dxs, dgate, dup = call(
         functools.partial(dx_kernel, peers, cap),
         "dx",
@@ -389,10 +374,10 @@
     outs = [outs[0]] + [swap(outs[j], "expert", j) for j in range(1, peers)]
     dxs = [dxs[0]] + [swap(dxs[j], "expert", j) for j in range(1, peers)]
     grad_gate, grad_up, grad_down = call(
-        functools.partial(grad_kernel, near),
+        functools.partial(grad_kernel, peers),
         "grads",
         [sds((width, ff))] * 2 + [sds((ff, width))],
-        (*xcs, *xs, *cs, hidden, dgate, dup),
+        (*xs, *cs, hidden, dgate, dup),
         scalars=0,
         flops=6 * work,
     )

time: 78 us -> 68.7 us (0.88)
  waiting for transfers between devices: 28.7 us -> 23 us
  starting transfers between devices: 26 us -> 21.8 us
    ppermute x16 -> x17, waiting for transfers between devices: 28.7 us -> 23 us  [swap(): return lax.ppermute(block, axis, [(i, i ^ offset) for i in range(count)])]
    ppermute x16 -> x17, starting transfers between devices: 26 us -> 21.8 us  [swap(): return lax.ppermute(block, axis, [(i, i ^ offset) for i in range(count)])]
    unnamed x18 -> x20, local copies, waits for them, and re-layouts: 7.02 us -> 7.7 us
  transfers between devices with their start and end apart: 16 -> 17, of which waited for: 7 -> 7; matrix products, arithmetic and copies ran while one was open for 1% -> 0% of each run, Pallas kernels for 11% -> 11%
where the time goes in v3:
time: 68.7 us; the launch traced here: 68.4 us
  waiting for transfers between devices  23 us (33%)
  starting transfers between devices  21.8 us (32%)
  Pallas kernels  10.6 us (15%)
  local copies, waits for them, and re-layouts  7.73 us (11%)
  blocking collectives  4.11 us (6%)
  between operations  0.81 us (1%)
    ppermute x17, waiting for transfers between devices, swap(): return lax.ppermute(block, axis, [(i, i ^ offset) for i in range(count)])  23 us
    ppermute x17, starting transfers between devices, swap(): return lax.ppermute(block, axis, [(i, i ^ offset) for i in range(count)])  21.8 us
    pallas_call x10, Pallas kernels, call(): pl.pallas_call(kernel, name=name, out_shape=outs, in_specs=[smem] * scala...  10.6 us
    unnamed x20, local copies, waits for them, and re-layouts  7.7 us
    all_to_all x1, blocking collectives, whole(): lax.all_to_all(twice, 'dp', 0, 0, axis_index_groups=pairs_of(dp_count))  4.11 us
  transfers between devices with their start and end apart: 17, of which 7 were waited for; matrix products, arithmetic and copies ran while one was open for 0% of the time, Pallas kernels for 11%

profile of v3, /device:TPU:0, one launch (start us, length us, event | category | flops | bytes accessed | tf_op | source)
XLA Modules:
  0.0 68.4 jit_solution(15709564844601503024)
XLA Ops:
  0.6 0.7 copy-done.4
  1.3 0.9 %copy-done.9 = bf16[128,768]{1,0:T(8,128)(2,1)S(1)} copy-done((bf16[128,768]{1,0:T(8,128)(2,1)S(1)}, bf16[128,768]{1,0:T(8,128)(2,1)}, u32[]{:S(2)}) %copy-start.9) | copy-done | bytes 196632
  2.2 0.4 pack.1
  2.7 3.1 %collective-permute-start = (bf16[80,768]{1,0:T(8,128)(2,1)S(1)}, bf16[80,768]{1,0:T(8,128)(2,1)S(1)}, u32[]{:S(2)}, u32[]{:S(2)}) collective-permute-start(bf16[80,768]{1,0:T(8,128)(2,1)S(1)} %get-tuple-element.50), channel_id=1, source_target_pairs={{0,4},{4,0},{8,12},{12,8},{1,5},{5,1},{9,13},{13,9},{2,6},{6,2},{1... | collective-permute-start | bytes 368648 | tf_op jit(solution)/shard_map/ppermute | solution.py:19
  5.8 2.6 %collective-permute-start.1 = (bf16[80,768]{1,0:T(8,128)(2,1)S(1)}, bf16[80,768]{1,0:T(8,128)(2,1)S(1)}, u32[]{:S(2)}, u32[]{:S(2)}) collective-permute-start(bf16[80,768]{1,0:T(8,128)(2,1)S(1)} %get-tuple-element.51), channel_id=1, source_target_pairs={{0,8},{4,12},{8,0},{12,4},{1,9},{5,13},{9,1},{13,5},{2,10},{6,14},... | collective-permute-start | bytes 368648 | tf_op jit(solution)/shard_map/ppermute | solution.py:19
  8.3 0.9 %copy-done.3 = bf16[128,768]{1,0:T(8,128)(2,1)S(1)} copy-done((bf16[128,768]{1,0:T(8,128)(2,1)S(1)}, bf16[128,768]{1,0:T(8,128)(2,1)}, u32[]{:S(2)}) %copy-start.3) | copy-done | bytes 196632
  9.3 0.7 copy-done.5
  10.0 0.7 copy-done.7
  10.6 0.3 pack_cot.1
  10.9 0.0 copy-start
  10.9 1.3 %copy-done = bf16[1,768,768]{2,1,0:T(8,128)(2,1)S(1)} copy-done((bf16[1,768,768]{2,1,0:T(8,128)(2,1)S(1)}, bf16[1,768,768]{2,1,0:T(8,128)(2,1)}, u32[]{:S(2)}) %copy-start) | copy-done | bytes 1179672
  12.2 1.3 %copy-done.1 = bf16[1,768,768]{2,1,0:T(8,128)(2,1)S(1)} copy-done((bf16[1,768,768]{2,1,0:T(8,128)(2,1)S(1)}, bf16[1,768,768]{2,1,0:T(8,128)(2,1)}, u32[]{:S(2)}) %copy-start.1) | copy-done | bytes 1179672
  13.5 1.3 %copy-done.2 = bf16[1,768,768]{2,1,0:T(8,128)(2,1)S(1)} copy-done((bf16[1,768,768]{2,1,0:T(8,128)(2,1)S(1)}, bf16[1,768,768]{2,1,0:T(8,128)(2,1)}, u32[]{:S(2)}) %copy-start.2) | copy-done | bytes 1179672
  14.7 0.7 %load.1 = (bf16[768,768]{1,0:T(8,128)(2,1)S(1)}, bf16[768,768]{1,0:T(8,128)(2,1)S(1)}, bf16[768,768]{1,0:T(8,128)(2,1)S(1)}) custom-call(bf16[768,768]{1,0:T(8,128)(2,1)S(1)} %bitcast.11, bf16[768,768]{1,0:T(8,128)(2,1)S(1)} %bitcast.12, bf16[768,768]{1,0:T(8,128)(2,1)S(1)} %bitcast.13), custom_call_target="tpu_custom_call" | custom-call | bytes 7077888 | tf_op jit(solution)/shard_map/load/pallas_call | solution.py:40
  15.5 2.6 %collective-permute-done.1.refs_2_ = bf16[80,768]{1,0:T(8,128)(2,1)S(1)} collective-permute-done((bf16[80,768]{1,0:T(8,128)(2,1)S(1)}, bf16[80,768]{1,0:T(8,128)(2,1)S(1)}, u32[]{:S(2)}, u32[]{:S(2)}) %collective-permute-start.1) | collective-permute-done | bytes 122912 | tf_op jit(solution)/shard_map/ppermute | solution.py:19
  18.1 1.4 %up.1 = (bf16[160,1536]{1,0:T(8,128)(2,1)S(1)}, bf16[160,1536]{1,0:T(8,128)(2,1)S(1)}) custom-call(s32[1]{0:T(128)} %bitcast.3.half_ref, bf16[80,768]{1,0:T(8,128)(2,1)S(1)} %get-tuple-element.49.refs_0_, bf16[80,768]{1,0:T(8,128)(2,1)S(1)} %collective-permute-done.refs_1_, bf16[80,768]{1,0:T(8,128)(2,1)S(1)} %collective-permute-done.1.refs_2_, ...), custom_call_target="tpu_custom_call" | custom-call | flops 754974720 | bytes 3833860 | tf_op jit(solution)/shard_map/up/pallas_call | solution.py:40
  19.5 0.1 collective-permute-start.3
  19.6 1.9 %collective-permute-done.3 = bf16[160,1536]{1,0:T(8,128)(2,1)S(1)} collective-permute-done((bf16[160,1536]{1,0:T(8,128)(2,1)S(1)}, bf16[160,1536]{1,0:T(8,128)(2,1)S(1)}, u32[]{:S(2)}, u32[]{:S(2)}) %collective-permute-start.3) | collective-permute-done | bytes 491552 | tf_op jit(solution)/shard_map/ppermute | solution.py:19
  21.4 0.1 add_convert_fusion.1
  21.6 1.6 %collective-permute-start.4 = (bf16[160,1536]{1,0:T(8,128)(2,1)S(1)}, bf16[160,1536]{1,0:T(8,128)(2,1)S(1)}, u32[]{:S(2)}, u32[]{:S(2)}) collective-permute-start(bf16[160,1536]{1,0:T(8,128)(2,1)S(1)} %add_convert_fusion.1), channel_id=1, source_target_pairs={{0,2},{1,3},{2,0},{3,1},{4,6},{5,7},{6,4},{7,5},{8,10},{9,11},{10,... | collective-permute-start | bytes 1474568 | tf_op jit(solution)/shard_map/ppermute | solution.py:19
  23.1 1.9 %collective-permute-start.9 = (bf16[80,768]{1,0:T(8,128)(2,1)S(1)}, bf16[80,768]{1,0:T(8,128)(2,1)S(1)}, u32[]{:S(2)}, u32[]{:S(2)}) collective-permute-start(bf16[80,768]{1,0:T(8,128)(2,1)S(1)} %get-tuple-element.63), channel_id=1, source_target_pairs={{0,4},{4,0},{8,12},{12,8},{1,5},{5,1},{9,13},{13,9},{2,6},{6,2},{1... | collective-permute-start | bytes 368648 | tf_op jit(solution)/shard_map/ppermute | solution.py:19
  25.0 1.1 %collective-permute-start.10 = (bf16[80,768]{1,0:T(8,128)(2,1)S(1)}, bf16[80,768]{1,0:T(8,128)(2,1)S(1)}, u32[]{:S(2)}, u32[]{:S(2)}) collective-permute-start(bf16[80,768]{1,0:T(8,128)(2,1)S(1)} %get-tuple-element.64), channel_id=1, source_target_pairs={{0,8},{4,12},{8,0},{12,4},{1,9},{5,13},{9,1},{13,5},{2,10},{6,14},... | collective-permute-start | bytes 368648 | tf_op jit(solution)/shard_map/ppermute | solution.py:19
  26.1 1.4 %collective-permute-start.11 = (bf16[80,768]{1,0:T(8,128)(2,1)S(1)}, bf16[80,768]{1,0:T(8,128)(2,1)S(1)}, u32[]{:S(2)}, u32[]{:S(2)}) collective-permute-start(bf16[80,768]{1,0:T(8,128)(2,1)S(1)} %get-tuple-element.65), channel_id=1, source_target_pairs={{0,12},{4,8},{8,4},{12,0},{1,13},{5,9},{9,5},{13,1},{2,14},{6,10},... | collective-permute-start | bytes 368648 | tf_op jit(solution)/shard_map/ppermute | solution.py:19
  27.5 2.2 %collective-permute-done.9.refs_1_.refs_5_ = bf16[80,768]{1,0:T(8,128)(2,1)S(1)} collective-permute-done((bf16[80,768]{1,0:T(8,128)(2,1)S(1)}, bf16[80,768]{1,0:T(8,128)(2,1)S(1)}, u32[]{:S(2)}, u32[]{:S(2)}) %collective-permute-start.9) | collective-permute-done | bytes 122912 | tf_op jit(solution)/shard_map/ppermute | solution.py:19
  29.7 7.6 %collective-permute-done.10.refs_2_.refs_6_ = bf16[80,768]{1,0:T(8,128)(2,1)S(1)} collective-permute-done((bf16[80,768]{1,0:T(8,128)(2,1)S(1)}, bf16[80,768]{1,0:T(8,128)(2,1)S(1)}, u32[]{:S(2)}, u32[]{:S(2)}) %collective-permute-start.10) | collective-permute-done | bytes 122912 | tf_op jit(solution)/shard_map/ppermute | solution.py:19
  37.3 0.6 back.1
  37.9 0.1 collective-permute-start.12
  38.0 0.1 add_convert_fusion.refs_0_
  38.2 0.5 collective-permute-start.5
  38.7 0.8 %collective-permute-done.12 = bf16[160,768]{1,0:T(8,128)(2,1)S(1)} collective-permute-done((bf16[160,768]{1,0:T(8,128)(2,1)S(1)}, bf16[160,768]{1,0:T(8,128)(2,1)S(1)}, u32[]{:S(2)}, u32[]{:S(2)}) %collective-permute-start.12) | collective-permute-done | bytes 245792 | tf_op jit(solution)/shard_map/ppermute | solution.py:19
  39.5 0.1 add_convert_fusion.3
  39.6 0.6 collective-permute-start.13
  40.2 0.0 collective-permute-done.5.refs_1_
  40.2 0.7 %out.1 = (bf16[80,768]{1,0:T(8,128)(2,1)S(1)}, bf16[80,768]{1,0:T(8,128)(2,1)S(1)}, bf16[80,768]{1,0:T(8,128)(2,1)S(1)}, bf16[80,768]{1,0:T(8,128)(2,1)S(1)}, bf...) custom-call(s32[1]{0:T(128)} %bitcast.3.half_ref, bf16[768,768]{1,0:T(8,128)(2,1)S(1)} %get-tuple-element.48.down_ref.refs_4_, ...), custom_call_target="tpu_custom_call" | custom-call | flops 377487360 | bytes 4128772 | tf_op jit(solution)/shard_map/out/pallas_call | solution.py:40
  41.0 1.9 %collective-permute-start.6 = (bf16[80,768]{1,0:T(8,128)(2,1)S(1)}, bf16[80,768]{1,0:T(8,128)(2,1)S(1)}, u32[]{:S(2)}, u32[]{:S(2)}) collective-permute-start(bf16[80,768]{1,0:T(8,128)(2,1)S(1)} %get-tuple-element.58), channel_id=1, source_target_pairs={{0,4},{4,0},{8,12},{12,8},{1,5},{5,1},{9,13},{13,9},{2,6},{6,2},{1... | collective-permute-start | bytes 368648 | tf_op jit(solution)/shard_map/ppermute | solution.py:19
  42.9 1.0 %collective-permute-start.7 = (bf16[80,768]{1,0:T(8,128)(2,1)S(1)}, bf16[80,768]{1,0:T(8,128)(2,1)S(1)}, u32[]{:S(2)}, u32[]{:S(2)}) collective-permute-start(bf16[80,768]{1,0:T(8,128)(2,1)S(1)} %get-tuple-element.59), channel_id=1, source_target_pairs={{0,8},{4,12},{8,0},{12,4},{1,9},{5,13},{9,1},{13,5},{2,10},{6,14},... | collective-permute-start | bytes 368648 | tf_op jit(solution)/shard_map/ppermute | solution.py:19
  44.0 1.5 %collective-permute-start.8 = (bf16[80,768]{1,0:T(8,128)(2,1)S(1)}, bf16[80,768]{1,0:T(8,128)(2,1)S(1)}, u32[]{:S(2)}, u32[]{:S(2)}) collective-permute-start(bf16[80,768]{1,0:T(8,128)(2,1)S(1)} %get-tuple-element.60), channel_id=1, source_target_pairs={{0,12},{4,8},{8,4},{12,0},{1,13},{5,9},{9,5},{13,1},{2,14},{6,10},... | collective-permute-start | bytes 368648 | tf_op jit(solution)/shard_map/ppermute | solution.py:19
  45.4 2.2 %collective-permute-done.13 = bf16[160,768]{1,0:T(8,128)(2,1)S(1)} collective-permute-done((bf16[160,768]{1,0:T(8,128)(2,1)S(1)}, bf16[160,768]{1,0:T(8,128)(2,1)S(1)}, u32[]{:S(2)}, u32[]{:S(2)}) %collective-permute-start.13) | collective-permute-done | bytes 245792 | tf_op jit(solution)/shard_map/ppermute | solution.py:19
  47.6 0.1 add_convert_fusion.2
  47.8 4.1 %all_to_all.5.refs_0_ = bf16[2,160,768]{2,1,0:T(8,128)(2,1)S(1)} all-to-all(bf16[2,160,768]{2,1,0:T(8,128)(2,1)S(1)} %broadcast_in_dim.15), channel_id=1, replica_groups={{0,1},{2,3},{4,5},{6,7},{8,9},{10,11},{12,13},{14,15},{16,17},{18,19},{..., dimensions={0} | all-to-all | bytes 983040 | tf_op jit(solution)/shard_map/all_to_all | solution.py:287
  51.9 1.2 %dx.1 = (bf16[80,768]{1,0:T(8,128)(2,1)S(1)}, bf16[80,768]{1,0:T(8,128)(2,1)S(1)}, bf16[80,768]{1,0:T(8,128)(2,1)S(1)}, bf16[80,768]{1,0:T(8,128)(2,1)S(1)}, bf1...) custom-call(s32[1]{0:T(128)} %bitcast.3.half_ref, bf16[2,160,1536]{2,1,0:T(8,128)(2,1)S(1)} %get-tuple-element.61.sums_ref, ...), custom_call_target="tpu_custom_call" | custom-call | flops 754974720 | bytes 5799940 | tf_op jit(solution)/shard_map/dx/pallas_call | solution.py:40
  53.0 1.9 %collective-permute-start.14 = (bf16[80,768]{1,0:T(8,128)(2,1)S(1)}, bf16[80,768]{1,0:T(8,128)(2,1)S(1)}, u32[]{:S(2)}, u32[]{:S(2)}) collective-permute-start(bf16[80,768]{1,0:T(8,128)(2,1)S(1)} %get-tuple-element.70), channel_id=1, source_target_pairs={{0,4},{4,0},{8,12},{12,8},{1,5},{5,1},{9,13},{13,9},{2,6},{6,2},{1... | collective-permute-start | bytes 368648 | tf_op jit(solution)/shard_map/ppermute | solution.py:19
  55.0 1.0 %collective-permute-start.15 = (bf16[80,768]{1,0:T(8,128)(2,1)S(1)}, bf16[80,768]{1,0:T(8,128)(2,1)S(1)}, u32[]{:S(2)}, u32[]{:S(2)}) collective-permute-start(bf16[80,768]{1,0:T(8,128)(2,1)S(1)} %get-tuple-element.71), channel_id=1, source_target_pairs={{0,8},{4,12},{8,0},{12,4},{1,9},{5,13},{9,1},{13,5},{2,10},{6,14},... | collective-permute-start | bytes 368648 | tf_op jit(solution)/shard_map/ppermute | solution.py:19
  56.0 1.5 %collective-permute-start.16 = (bf16[80,768]{1,0:T(8,128)(2,1)S(1)}, bf16[80,768]{1,0:T(8,128)(2,1)S(1)}, u32[]{:S(2)}, u32[]{:S(2)}) collective-permute-start(bf16[80,768]{1,0:T(8,128)(2,1)S(1)} %get-tuple-element.72), channel_id=1, source_target_pairs={{0,12},{4,8},{8,4},{12,0},{1,13},{5,9},{9,5},{13,1},{2,14},{6,10},... | collective-permute-start | bytes 368648 | tf_op jit(solution)/shard_map/ppermute | solution.py:19
  57.5 3.1 %grads.1 = (bf16[768,768]{1,0:T(8,128)(2,1)}, bf16[768,768]{1,0:T(8,128)(2,1)}, bf16[768,768]{1,0:T(8,128)(2,1)}) custom-call(bf16[80,768]{1,0:T(8,128)(2,1)S(1)} %get-tuple-element.49.refs_0_, bf16[80,768]{1,0:T(8,128)(2,1)S(1)} %collective-permute-done.refs_1_, bf16[80,768]{1,0:T(8,128)(2,1)S(1)} %collective-permute-done.1.refs_2_, ...), custom_call_target="tpu_custom_call" | custom-call | flops 1132462080 | bytes 5996544 | tf_op jit(solution)/shard_map/grads/pallas_call | solution.py:40
  60.6 1.1 %mix.1 = bf16[128,768]{1,0:T(8,128)(2,1)} custom-call(s32[1]{0:T(128)} %bitcast.me_ref, s32[2,128]{1,0:T(2,128)S(1)} %bitcast.16, f32[2,128]{1,0:T(2,128)S(1)} %bitcast.19, bf16[320,128]{1,0:T(8,128)(2,1)S(1)} %get-tuple-element.43.place_ref, bf16[80,768]{1,0:T(8,128)(2,1)S(1)} %get-tuple-element.57.refs_0_, ...), custom_call_target="tpu_custom_call" | custom-call | flops 125829120 | bytes 772100 | tf_op jit(solution)/shard_map/mix/pallas_call | solution.py:40
  61.7 5.7 %collective-permute-done.15.refs_2_ = bf16[80,768]{1,0:T(8,128)(2,1)S(1)} collective-permute-done((bf16[80,768]{1,0:T(8,128)(2,1)S(1)}, bf16[80,768]{1,0:T(8,128)(2,1)S(1)}, u32[]{:S(2)}, u32[]{:S(2)}) %collective-permute-start.15) | collective-permute-done | bytes 122912 | tf_op jit(solution)/shard_map/ppermute | solution.py:19
  67.4 1.0 %merge.1 = (bf16[128,768]{1,0:T(8,128)(2,1)}, f32[2,128]{1,0:T(2,128)}) custom-call(s32[1]{0:T(128)} %bitcast.me_ref, s32[2,128]{1,0:T(2,128)S(1)} %bitcast.17, f32[2,128]{1,0:T(2,128)S(1)} %bitcast.20, bf16[320,128]{1,0:T(8,128)(2,1)S(1)} %get-tuple-element.43.place_ref, bf16[80,768]{1,0:T(8,128)(2,1)S(1)} %get-tuple-element.69.refs_0_, ...), custom_call_target="tpu_custom_call" | custom-call | flops 62914560 | bytes 773124 | tf_op jit(solution)/shard_map/merge/pallas_call | solution.py:40
  (22 shorter events, 0.1 us)
Async XLA Ops:
  0.6 0.7 copy-start.4
  1.3 0.9 %copy-start.9 = (bf16[128,768]{1,0:T(8,128)(2,1)S(1)}, bf16[128,768]{1,0:T(8,128)(2,1)}, u32[]{:S(2)}) copy-start(bf16[128,768]{1,0:T(8,128)(2,1)} %tokens_ref.1) | copy-start | bytes 589828
  2.7 12.8 %collective-permute-start = (bf16[80,768]{1,0:T(8,128)(2,1)S(1)}, bf16[80,768]{1,0:T(8,128)(2,1)S(1)}, u32[]{:S(2)}, u32[]{:S(2)}) collective-permute-start(bf16[80,768]{1,0:T(8,128)(2,1)S(1)} %get-tuple-element.50), channel_id=1, source_target_pairs={{0,4},{4,0},{8,12},{12,8},{1,5},{5,1},{9,13},{13,9},{2,6},{6,2},{1... | collective-permute-start | bytes 368648 | tf_op jit(solution)/shard_map/ppermute | solution.py:19
  5.8 12.3 %collective-permute-start.1 = (bf16[80,768]{1,0:T(8,128)(2,1)S(1)}, bf16[80,768]{1,0:T(8,128)(2,1)S(1)}, u32[]{:S(2)}, u32[]{:S(2)}) collective-permute-start(bf16[80,768]{1,0:T(8,128)(2,1)S(1)} %get-tuple-element.51), channel_id=1, source_target_pairs={{0,8},{4,12},{8,0},{12,4},{1,9},{5,13},{9,1},{13,5},{2,10},{6,14},... | collective-permute-start | bytes 368648 | tf_op jit(solution)/shard_map/ppermute | solution.py:19
  8.3 9.7 %collective-permute-start.2 = (bf16[80,768]{1,0:T(8,128)(2,1)S(1)}, bf16[80,768]{1,0:T(8,128)(2,1)S(1)}, u32[]{:S(2)}, u32[]{:S(2)}) collective-permute-start(bf16[80,768]{1,0:T(8,128)(2,1)S(1)} %get-tuple-element.52), channel_id=1, source_target_pairs={{0,12},{4,8},{8,4},{12,0},{1,13},{5,9},{9,5},{13,1},{2,14},{6,10},... | collective-permute-start | bytes 368648 | tf_op jit(solution)/shard_map/ppermute | solution.py:19
  8.3 0.9 %copy-start.3 = (bf16[128,768]{1,0:T(8,128)(2,1)S(1)}, bf16[128,768]{1,0:T(8,128)(2,1)}, u32[]{:S(2)}) copy-start(bf16[128,768]{1,0:T(8,128)(2,1)} %cot_ref.1) | copy-start | bytes 589828
  9.3 0.7 copy-start.5
  10.0 0.7 copy-start.7
  10.9 1.3 %copy-start = (bf16[1,768,768]{2,1,0:T(8,128)(2,1)S(1)}, bf16[1,768,768]{2,1,0:T(8,128)(2,1)}, u32[]{:S(2)}) copy-start(bf16[1,768,768]{2,1,0:T(8,128)(2,1)} %param.11) | copy-start | bytes 3538948
  12.2 1.3 %copy-start.1 = (bf16[1,768,768]{2,1,0:T(8,128)(2,1)S(1)}, bf16[1,768,768]{2,1,0:T(8,128)(2,1)}, u32[]{:S(2)}) copy-start(bf16[1,768,768]{2,1,0:T(8,128)(2,1)} %param.12) | copy-start | bytes 3538948
  13.5 1.3 %copy-start.2 = (bf16[1,768,768]{2,1,0:T(8,128)(2,1)S(1)}, bf16[1,768,768]{2,1,0:T(8,128)(2,1)}, u32[]{:S(2)}) copy-start(bf16[1,768,768]{2,1,0:T(8,128)(2,1)} %param.13) | copy-start | bytes 3538948
  19.5 1.9 %collective-permute-start.3 = (bf16[160,1536]{1,0:T(8,128)(2,1)S(1)}, bf16[160,1536]{1,0:T(8,128)(2,1)S(1)}, u32[]{:S(2)}, u32[]{:S(2)}) collective-permute-start(bf16[160,1536]{1,0:T(8,128)(2,1)S(1)} %get-tuple-element.56), channel_id=1, source_target_pairs={{0,1},{1,0},{2,3},{3,2},{4,5},{5,4},{6,7},{7,6},{8,9},{9,8},{10,11... | collective-permute-start | bytes 1474568 | tf_op jit(solution)/shard_map/ppermute | solution.py:19
  21.6 16.5 %collective-permute-start.4 = (bf16[160,1536]{1,0:T(8,128)(2,1)S(1)}, bf16[160,1536]{1,0:T(8,128)(2,1)S(1)}, u32[]{:S(2)}, u32[]{:S(2)}) collective-permute-start(bf16[160,1536]{1,0:T(8,128)(2,1)S(1)} %add_convert_fusion.1), channel_id=1, source_target_pairs={{0,2},{1,3},{2,0},{3,1},{4,6},{5,7},{6,4},{7,5},{8,10},{9,11},{10,... | collective-permute-start | bytes 1474568 | tf_op jit(solution)/shard_map/ppermute | solution.py:19
  23.1 6.6 %collective-permute-start.9 = (bf16[80,768]{1,0:T(8,128)(2,1)S(1)}, bf16[80,768]{1,0:T(8,128)(2,1)S(1)}, u32[]{:S(2)}, u32[]{:S(2)}) collective-permute-start(bf16[80,768]{1,0:T(8,128)(2,1)S(1)} %get-tuple-element.63), channel_id=1, source_target_pairs={{0,4},{4,0},{8,12},{12,8},{1,5},{5,1},{9,13},{13,9},{2,6},{6,2},{1... | collective-permute-start | bytes 368648 | tf_op jit(solution)/shard_map/ppermute | solution.py:19
  25.0 12.3 %collective-permute-start.10 = (bf16[80,768]{1,0:T(8,128)(2,1)S(1)}, bf16[80,768]{1,0:T(8,128)(2,1)S(1)}, u32[]{:S(2)}, u32[]{:S(2)}) collective-permute-start(bf16[80,768]{1,0:T(8,128)(2,1)S(1)} %get-tuple-element.64), channel_id=1, source_target_pairs={{0,8},{4,12},{8,0},{12,4},{1,9},{5,13},{9,1},{13,5},{2,10},{6,14},... | collective-permute-start | bytes 368648 | tf_op jit(solution)/shard_map/ppermute | solution.py:19
  26.1 11.3 %collective-permute-start.11 = (bf16[80,768]{1,0:T(8,128)(2,1)S(1)}, bf16[80,768]{1,0:T(8,128)(2,1)S(1)}, u32[]{:S(2)}, u32[]{:S(2)}) collective-permute-start(bf16[80,768]{1,0:T(8,128)(2,1)S(1)} %get-tuple-element.65), channel_id=1, source_target_pairs={{0,12},{4,8},{8,4},{12,0},{1,13},{5,9},{9,5},{13,1},{2,14},{6,10},... | collective-permute-start | bytes 368648 | tf_op jit(solution)/shard_map/ppermute | solution.py:19
  37.9 1.6 %collective-permute-start.12 = (bf16[160,768]{1,0:T(8,128)(2,1)S(1)}, bf16[160,768]{1,0:T(8,128)(2,1)S(1)}, u32[]{:S(2)}, u32[]{:S(2)}) collective-permute-start(bf16[160,768]{1,0:T(8,128)(2,1)S(1)} %get-tuple-element.67), channel_id=1, source_target_pairs={{0,1},{1,0},{2,3},{3,2},{4,5},{5,4},{6,7},{7,6},{8,9},{9,8},{10,11... | collective-permute-start | bytes 737288 | tf_op jit(solution)/shard_map/ppermute | solution.py:19
  38.2 2.1 %collective-permute-start.5 = (bf16[160,1536]{1,0:T(8,128)(2,1)S(1)}, bf16[160,1536]{1,0:T(8,128)(2,1)S(1)}, u32[]{:S(2)}, u32[]{:S(2)}) collective-permute-start(bf16[160,1536]{1,0:T(8,128)(2,1)S(1)} %add_convert_fusion.refs_0_), channel_id=1, source_target_pairs={{0,1},{1,0},{2,3},{3,2},{4,5},{5,4},{6,7},{7,6},{8,9},{9,8},{10,11... | collective-permute-start | bytes 1474568 | tf_op jit(solution)/shard_map/ppermute | solution.py:19
  39.6 8.1 %collective-permute-start.13 = (bf16[160,768]{1,0:T(8,128)(2,1)S(1)}, bf16[160,768]{1,0:T(8,128)(2,1)S(1)}, u32[]{:S(2)}, u32[]{:S(2)}) collective-permute-start(bf16[160,768]{1,0:T(8,128)(2,1)S(1)} %add_convert_fusion.3), channel_id=1, source_target_pairs={{0,2},{1,3},{2,0},{3,1},{4,6},{5,7},{6,4},{7,5},{8,10},{9,11},{10,... | collective-permute-start | bytes 737288 | tf_op jit(solution)/shard_map/ppermute | solution.py:19
  41.0 15.1 %collective-permute-start.6 = (bf16[80,768]{1,0:T(8,128)(2,1)S(1)}, bf16[80,768]{1,0:T(8,128)(2,1)S(1)}, u32[]{:S(2)}, u32[]{:S(2)}) collective-permute-start(bf16[80,768]{1,0:T(8,128)(2,1)S(1)} %get-tuple-element.58), channel_id=1, source_target_pairs={{0,4},{4,0},{8,12},{12,8},{1,5},{5,1},{9,13},{13,9},{2,6},{6,2},{1... | collective-permute-start | bytes 368648 | tf_op jit(solution)/shard_map/ppermute | solution.py:19
  42.9 17.6 %collective-permute-start.7 = (bf16[80,768]{1,0:T(8,128)(2,1)S(1)}, bf16[80,768]{1,0:T(8,128)(2,1)S(1)}, u32[]{:S(2)}, u32[]{:S(2)}) collective-permute-start(bf16[80,768]{1,0:T(8,128)(2,1)S(1)} %get-tuple-element.59), channel_id=1, source_target_pairs={{0,8},{4,12},{8,0},{12,4},{1,9},{5,13},{9,1},{13,5},{2,10},{6,14},... | collective-permute-start | bytes 368648 | tf_op jit(solution)/shard_map/ppermute | solution.py:19
  44.0 16.6 %collective-permute-start.8 = (bf16[80,768]{1,0:T(8,128)(2,1)S(1)}, bf16[80,768]{1,0:T(8,128)(2,1)S(1)}, u32[]{:S(2)}, u32[]{:S(2)}) collective-permute-start(bf16[80,768]{1,0:T(8,128)(2,1)S(1)} %get-tuple-element.60), channel_id=1, source_target_pairs={{0,12},{4,8},{8,4},{12,0},{1,13},{5,9},{9,5},{13,1},{2,14},{6,10},... | collective-permute-start | bytes 368648 | tf_op jit(solution)/shard_map/ppermute | solution.py:19
  53.0 8.7 %collective-permute-start.14 = (bf16[80,768]{1,0:T(8,128)(2,1)S(1)}, bf16[80,768]{1,0:T(8,128)(2,1)S(1)}, u32[]{:S(2)}, u32[]{:S(2)}) collective-permute-start(bf16[80,768]{1,0:T(8,128)(2,1)S(1)} %get-tuple-element.70), channel_id=1, source_target_pairs={{0,4},{4,0},{8,12},{12,8},{1,5},{5,1},{9,13},{13,9},{2,6},{6,2},{1... | collective-permute-start | bytes 368648 | tf_op jit(solution)/shard_map/ppermute | solution.py:19
  55.0 12.4 %collective-permute-start.15 = (bf16[80,768]{1,0:T(8,128)(2,1)S(1)}, bf16[80,768]{1,0:T(8,128)(2,1)S(1)}, u32[]{:S(2)}, u32[]{:S(2)}) collective-permute-start(bf16[80,768]{1,0:T(8,128)(2,1)S(1)} %get-tuple-element.71), channel_id=1, source_target_pairs={{0,8},{4,12},{8,0},{12,4},{1,9},{5,13},{9,1},{13,5},{2,10},{6,14},... | collective-permute-start | bytes 368648 | tf_op jit(solution)/shard_map/ppermute | solution.py:19
  56.0 11.3 %collective-permute-start.16 = (bf16[80,768]{1,0:T(8,128)(2,1)S(1)}, bf16[80,768]{1,0:T(8,128)(2,1)S(1)}, u32[]{:S(2)}, u32[]{:S(2)}) collective-permute-start(bf16[80,768]{1,0:T(8,128)(2,1)S(1)} %get-tuple-element.72), channel_id=1, source_target_pairs={{0,12},{4,8},{8,4},{12,0},{1,13},{5,9},{9,5},{13,1},{2,14},{6,10},... | collective-permute-start | bytes 368648 | tf_op jit(solution)/shard_map/ppermute | solution.py:19
  57.5 3.1 %copy-start.6 = (s32[128,2]{0,1:T(2,128)S(1)}, s32[128,2]{0,1:T(2,128)}, u32[]{:S(2)}) copy-start(s32[128,2]{0,1:T(2,128)} %param.9) | copy-start | bytes 3076
  57.5 3.1 %copy-start.8 = (f32[128,2]{0,1:T(2,128)S(1)}, f32[128,2]{0,1:T(2,128)}, u32[]{:S(2)}) copy-start(f32[128,2]{0,1:T(2,128)} %param.10) | copy-start | bytes 3076

commit v4 on v3

--- a/solution.py
+++ b/solution.py
@@ -10,8 +10,8 @@
 BF = jnp.bfloat16
 F32 = jnp.float32
 VMEM_BYTES = 40 * 1024 * 1024
-DH_AFTER = True
-SYNC = (False, False, False, True)
+NEAR_PIECES, DH_PIECES, DX_FLOPS = 2, 3, 0
+NEAR_AFTER, DH_AFTER = True, True
 
 
 def swap(block, axis, offset):
@@ -104,45 +104,42 @@
         copy.wait()
 
 
-def hand_out(half, y, refs):
+def hand_out(half, y, start, lane, keep_ref, send_ref):
     rows = y.shape[0] // 2
-    width = y.shape[1]
-    lanes = pl.ds(half[1], width)
-    if len(refs) == 1:
-        refs[0][0, :, lanes] = y[:rows]
-        refs[0][1, :, lanes] = y[rows:]
-        return
+    target = (slice(start, start + rows), slice(lane, lane + y.shape[1]))
     for h in range(2):
 
-        @pl.when(half[0] == h)
+        @pl.when(half == h)
         def _():
-            refs[0][:, lanes] = y[h * rows : (h + 1) * rows]
-            refs[1][:, lanes] = y[(1 - h) * rows : (2 - h) * rows]
-
-
-def both_halves(half, refs, store_ref):
-    if len(refs) == 1:
-        return refs[0]
-    store_ref[half] = refs[0][...]
-    store_ref[1 - half] = refs[1][...]
-    return store_ref
+            keep_ref[target] = y[h * rows : (h + 1) * rows]
+            send_ref[target] = y[(1 - h) * rows : (2 - h) * rows]
 
 
 def stack(refs, part=slice(None)):
     return jnp.concatenate([r[part, :] for r in refs], axis=0)
 
 
-def up_kernel(peers, half_ref, *refs):
-    x_refs, (gate_ref, up_ref, *to_refs) = refs[:peers], refs[peers:]
+def up_kernel(near, half_ref, *refs):
+    x_refs, (gate_ref, up_ref, near_keep, near_send, far_keep, far_send) = refs[:-6], refs[-6:]
+    x_refs = x_refs[near:] + x_refs[:near]
+    half = half_ref[0]
     x = stack(x_refs)
+    rows = near * x_refs[0].shape[0]
     width = gate_ref.shape[1]
-    hand_out((half_ref[0], 0), dot(x, gate_ref[...]).astype(BF), to_refs)
-    hand_out((half_ref[0], width), dot(x, up_ref[...]).astype(BF), to_refs)
-
-
-def back_kernel(peers, half_ref, *refs):
-    c_refs, (down_ref, *to_refs) = refs[:peers], refs[peers:]
-    hand_out((half_ref[0], 0), dot_nt(stack(c_refs), down_ref[...]).astype(BF), to_refs)
+    for i, w_ref in enumerate((gate_ref, up_ref)):
+        y = dot(x, w_ref[...]).astype(BF)
+        hand_out(half, y[:rows], 0, i * width, near_keep, near_send)
+        hand_out(half, y[rows:], 0, i * width, far_keep, far_send)
+
+
+def back_kernel(near, half_ref, *refs):
+    c_refs, (down_ref, keep_ref, send_ref) = refs[:-3], refs[-3:]
+    c_refs = c_refs[near:] + c_refs[:near]
+    half = half_ref[0]
+    y = dot_nt(stack(c_refs), down_ref[...]).astype(BF)
+    rows = near * c_refs[0].shape[0]
+    hand_out(half, y[:rows], 0, 0, keep_ref, send_ref)
+    hand_out(half, y[rows:], rows // 2, 0, keep_ref, send_ref)
 
 
 def activate(g, u):
@@ -159,7 +156,7 @@
 
 
 def store_dx(cap, dx_ref, block, dots):
-    cp = dx_ref.shape[0]
+    cp = block.shape[0]
     lanes = 128 * (-(-cp // 128))
     row = lax.broadcasted_iota(jnp.int32, (cp, lanes), 0)
     eye = row == lax.broadcasted_iota(jnp.int32, (cp, lanes), 1)
@@ -174,73 +171,113 @@
     dx_ref[:, lanes:] = block[:, lanes:].astype(BF)
 
 
-def out_kernel(peers, waits, half_ref, down_ref, *refs):
-    from_refs, refs = refs[: 2 - waits], refs[2 - waits :]
-    out_refs, hidden_ref, sums_ref = refs[:peers], refs[peers], refs[-1]
+def out_kernel(near, half_ref, mine_ref, other_ref, down_ref, *refs):
+    out_refs, (hidden_ref, sums_ref) = refs[:near], refs[near:]
+    half = half_ref[0]
     width = down_ref.shape[0]
-    source_ref = both_halves(half_ref[0], from_refs, sums_ref)
-    rows = source_ref.shape[1]
+    sums_ref[half] = mine_ref[...]
+    sums_ref[1 - half] = other_ref[...]
+    rows = mine_ref.shape[0]
     for h in range(2):
-        g = source_ref[h, :, :width].astype(F32)
-        u = source_ref[h, :, width:].astype(F32)
+        g = sums_ref[h, :, :width].astype(F32)
+        u = sums_ref[h, :, width:].astype(F32)
         hidden_ref[h * rows : (h + 1) * rows, :] = activate(g, u)
     out = dot(hidden_ref[...], down_ref[...]).astype(BF)
     cp = out_refs[0].shape[0]
-    for j in range(peers):
+    for j in range(near):
         out_refs[j][...] = out[j * cp : (j + 1) * cp]
 
 
-def dx_kernel(peers, cap, half_ref, sums_ref, hidden_ref, gate_ref, up_ref, *refs):
-    from_refs = refs[: -peers - 4]
-    dx_refs, (dgate_ref, dup_ref, dh_ref, dot_ref) = refs[-peers - 4 : -4], refs[-4:]
-    width = gate_ref.shape[1]
-    source_ref = both_halves(half_ref[0], from_refs, dh_ref)
-    rows = source_ref.shape[1]
+def gather(half, refs, target_ref):
+    count = len(refs) // 2
+    wide = refs[0].shape[1]
+    for i in range(count):
+        target_ref[half, :, i * wide : (i + 1) * wide] = refs[i][...]
+        target_ref[1 - half, :, i * wide : (i + 1) * wide] = refs[count + i][...]
+
+
+def dx_rows(rows, width, source_ref, dh_ref, first, hidden_ref, dgate_ref, dup_ref, dot_ref):
     for h in range(2):
         part = slice(h * rows, (h + 1) * rows)
-        g = sums_ref[h, :, :width].astype(F32)
-        u = sums_ref[h, :, width:].astype(F32)
-        dh = source_ref[h].astype(F32)
+        g = source_ref[h, :, :width].astype(F32)
+        u = source_ref[h, :, width:].astype(F32)
+        dh = dh_ref[h, first : first + rows, :].astype(F32)
         dgate_ref[part, :], dup_ref[part, :] = derive(g, u, dh)
         dot_ref[part, :] = row_dots(hidden_ref[part, :], dh)
+
+
+def dx_kernel(near, cap, half_ref, far_ref, hidden_ref, gate_ref, up_ref, *refs):
+    dh_sums, refs = refs[: 2 * DH_PIECES], refs[2 * DH_PIECES :]
+    dx_refs, (dgate_ref, dup_ref, dh_ref, dot_ref) = refs[:near], refs[near:]
+    gather(half_ref[0], dh_sums, dh_ref)
+    rows = far_ref.shape[1]
+    dx_rows(rows, gate_ref.shape[1], far_ref, dh_ref, rows, hidden_ref, dgate_ref, dup_ref, dot_ref)
     dx = dot_nt(dgate_ref[...], gate_ref[...]) + dot_nt(dup_ref[...], up_ref[...])
     cp = dx_refs[0].shape[0]
-    for j in range(peers):
+    for j in range(near):
         part = slice(j * cp, (j + 1) * cp)
         store_dx(cap, dx_refs[j], dx[part], dot_ref[part, :])
 
 
+def near_kernel(near, cap, half_ref, dh_ref, gate_ref, up_ref, down_ref, *refs):
+    near_sums, refs = refs[: 2 * NEAR_PIECES], refs[2 * NEAR_PIECES :]
+    out_refs, dx_refs, refs = refs[:near], refs[near : 2 * near], refs[2 * near :]
+    hidden_ref, dgate_ref, dup_ref, near_ref, dot_ref = refs
+    gather(half_ref[0], near_sums, near_ref)
+    rows, width = near_ref.shape[1], gate_ref.shape[1]
+    for h in range(2):
+        g = near_ref[h, :, :width].astype(F32)
+        u = near_ref[h, :, width:].astype(F32)
+        hidden_ref[h * rows : (h + 1) * rows, :] = activate(g, u)
+    dx_rows(rows, width, near_ref, dh_ref, 0, hidden_ref, dgate_ref, dup_ref, dot_ref)
+    out = dot(hidden_ref[...], down_ref[...]).astype(BF)
+    dx = dot_nt(dgate_ref[...], gate_ref[...]) + dot_nt(dup_ref[...], up_ref[...])
+    cp = dx_refs[0].shape[0]
+    for j in range(near):
+        part = slice(j * cp, (j + 1) * cp)
+        out_refs[j][...] = out[part]
+        store_dx(cap, dx_refs[j], dx[part], dot_ref[part, :])
+
+
 def grad_kernel(peers, *refs):
     x_refs, c_refs = refs[:peers], refs[peers : 2 * peers]
-    hidden_ref, dgate_ref, dup_ref, gg_ref, gu_ref, gd_ref = refs[2 * peers :]
+    hidden_refs, dgate_refs, dup_refs = (refs[2 * peers + 2 * i :][:2] for i in range(3))
+    gg_ref, gu_ref, gd_ref = refs[2 * peers + 6 :]
     x = stack(x_refs)
-    gg_ref[...] = dot_tn(x, dgate_ref[...]).astype(BF)
-    gu_ref[...] = dot_tn(x, dup_ref[...]).astype(BF)
-    gd_ref[...] = dot_tn(hidden_ref[...], stack(c_refs)).astype(BF)
-
-
-def mix_kernel(peers, me_ref, routes_ref, gates_ref, place_ref, *refs):
-    out_refs, mixed_ref = refs[:peers], refs[peers]
-    me = me_ref[0]
+    gg_ref[...] = dot_tn(x, stack(dgate_refs)).astype(BF)
+    gu_ref[...] = dot_tn(x, stack(dup_refs)).astype(BF)
+    gd_ref[...] = dot_tn(stack(hidden_refs), stack(c_refs)).astype(BF)
+
+
+def weighted(peers, me, routes_ref, gates_ref, place_ref, out, first):
     routes, gates = routes_ref[...], gates_ref[...]
-    cp = out_refs[0].shape[0]
+    cp = place_ref.shape[0] // peers
     highs, lows = [], []
-    for j in range(peers):
+    for j in range(first, first + out.shape[0] // cp):
         place = place_ref[j * cp : (j + 1) * cp, :].astype(F32)
         gate = gate_row(routes, gates, me ^ j)
         high = gate.astype(BF).astype(F32)
         highs.append((place * high).astype(BF))
         lows.append((place * (gate - high)).astype(BF))
-    out = stack(out_refs)
-    mixed = dot_tn(jnp.concatenate(highs, axis=0), out) + dot_tn(jnp.concatenate(lows, axis=0), out)
-    mixed_ref[...] = mixed.astype(BF)
-
-
-def merge_kernel(peers, cap, me_ref, routes_ref, gates_ref, place_ref, *refs):
-    dx_refs, (grad_ref, gates_out_ref) = refs[:peers], refs[peers:]
+    return dot_tn(jnp.concatenate(highs, axis=0), out) + dot_tn(jnp.concatenate(lows, axis=0), out)
+
+
+def mix_kernel(peers, me_ref, routes_ref, gates_ref, place_ref, *refs):
+    out_refs, mixed_ref = refs[:-1], refs[-1]
+    near = peers // 2
+    mixed_ref[...] = weighted(
+        peers, me_ref[0], routes_ref, gates_ref, place_ref, stack(out_refs), near
+    )
+
+
+def merge_kernel(peers, cap, me_ref, routes_ref, gates_ref, place_ref, far_ref, *refs):
+    near = peers // 2
+    out_refs, dx_refs, (mixed_ref, grad_ref, gates_out_ref) = refs[:near], refs[near:-3], refs[-3:]
     me = me_ref[0]
     routes, gates = routes_ref[...], gates_ref[...]
     cp = dx_refs[0].shape[0]
+    mixed = weighted(peers, me, routes_ref, gates_ref, place_ref, stack(out_refs), 0)
+    mixed_ref[...] = (far_ref[...] + mixed).astype(BF)
     grad_ref[...] = dot_tn(place_ref[...], stack(dx_refs)).astype(BF)
     total = jnp.zeros(gates.shape, F32)
     base = cap // 16 * 16
@@ -261,31 +298,26 @@
     return lax.optimization_barrier((*first, *arrays))[len(first) :]
 
 
-def pairs_of(count):
-    return [[i, i + 1] for i in range(0, count, 2)]
-
-
-def reduced(parts, dp_count, first=()):
-    if len(parts) == 1:
-        arrived = lax.all_to_all(parts[0], "dp", 0, 0, axis_index_groups=pairs_of(dp_count))
-        total = added(arrived[0], arrived[1])
-    else:
-        total = added(parts[0], swap(parts[1], "dp", 1))
+def paired(keep, send):
+    return added(keep, swap(send, "dp", 1))
+
+
+def both(pieces):
+    return [*pieces, *(swap(piece, "dp", 1) for piece in pieces)]
+
+
+def reduced(total, dp_count, pieces=1, first=()):
     bit = 2
     while bit < dp_count:
         arrived = swap(total, "dp", bit)
         bit *= 2
         if first and bit >= dp_count:
             (arrived,) = after(first, (arrived,))
+        if bit >= dp_count:
+            wide = total.shape[1] // pieces
+            lanes = [slice(i * wide, (i + 1) * wide) for i in range(pieces)]
+            return [added(total[:, part], arrived[:, part]) for part in lanes]
         total = added(total, arrived)
-    return total
-
-
-def whole(total, dp_count, waits):
-    if waits:
-        twice = jnp.broadcast_to(total[None], (2, *total.shape))
-        return [lax.all_to_all(twice, "dp", 0, 0, axis_index_groups=pairs_of(dp_count))]
-    return [total, swap(total, "dp", 1)]
 
 
 def shards(tokens, cotangent, routes, route_gates, gate_weight, up_weight, down_weight):
@@ -334,66 +366,85 @@
     cs = [cs[0]] + [swap(cs[j], "expert", j) for j in range(1, peers)]
     work = 2 * rows * width * ff
 
-    def parts_of(waits, wide):
-        return [sds((2, rows, wide))] if waits else [sds((rows, wide))] * 2
-
-    up_parts = call(
-        functools.partial(up_kernel, peers),
+    near_keep, near_send, far_keep, far_send = call(
+        functools.partial(up_kernel, near),
         "up",
-        parts_of(SYNC[0], 2 * ff),
-        (half, *xs, gate_w, up_w),
+        [sds((rows // 2, 2 * ff))] * 4,
+        (half, *xs[near:], *xs[:near], gate_w, up_w),
         flops=4 * work,
     )
-    up_sum = reduced(up_parts, dp_count)
-    dh_parts = call(
-        functools.partial(back_kernel, peers),
+    far_total = paired(far_keep, far_send)
+    near_total = paired(near_keep, near_send)
+    cs = after((far_total, near_total), (*cs[near:], *cs[:near]))
+    cs = (*cs[near:], *cs[:near])
+    (far_sum,) = reduced(far_total, dp_count)
+    dh_keep, dh_send = call(
+        functools.partial(back_kernel, near),
         "back",
-        parts_of(SYNC[1], ff),
-        (half, *cs, down_w),
+        [sds((rows, ff))] * 2,
+        (half, *cs[near:], *cs[:near], down_w),
         flops=2 * work,
     )
-    up_both = whole(up_sum, dp_count, SYNC[2])
+    dh_total = paired(dh_keep, dh_send)
+    *outs, far_hidden, far_sums = call(
+        functools.partial(out_kernel, near),
+        "out",
+        [part] * near + [sds((rows, ff)), sds((2, rows // 2, 2 * ff))],
+        (half, far_sum, swap(far_sum, "dp", 1), down_w),
+        flops=work,
+    )
+    near_sum = reduced(near_total, dp_count, NEAR_PIECES, NEAR_AFTER and (outs[0],))
+    dh_sum = reduced(dh_total, dp_count, DH_PIECES, DH_AFTER and (outs[0],))
+    near_sums, dh_sums = both(near_sum), both(dh_sum)
+
+    *dxs, far_dgate, far_dup, dh = call(
+        functools.partial(dx_kernel, near, cap),
+        "dx",
+        [part] * near + [sds((rows, ff))] * 2 + [sds((2, rows, ff))],
+        (half, far_sums, far_hidden, gate_w, up_w, *dh_sums),
+        scratch=[pltpu.VMEM((rows, 1), F32)],
+        flops=DX_FLOPS * work,
+    )
+    dxs = [swap(dxs[j], "expert", near + j) for j in range(near)]
+    outs = [swap(outs[j], "expert", near + j) for j in range(near)]
+    (far_mixed,) = call(
+        functools.partial(mix_kernel, peers),
+        "mix",
+        [sds((count, width), F32)],
+        (me, routes_t, gates_t, place, *outs),
+        flops=DX_FLOPS * rows * count * width,
+    )
+    (dh,) = after((far_mixed,), (dh,))
     produced = call(
-        functools.partial(out_kernel, peers, SYNC[2]),
-        "out",
-        [part] * peers + [sds((2 * rows, ff))] + [sds((2, rows, 2 * ff))] * (not SYNC[2]),
-        (half, down_w, *up_both),
-        flops=2 * work,
-    )
-    outs, hidden = produced[:peers], produced[peers]
-    sums = up_both[0] if SYNC[2] else produced[-1]
-    dh_sum = reduced(dh_parts, dp_count, DH_AFTER and (outs[0],))
-    *dxs, dgate, dup = call(
-        functools.partial(dx_kernel, peers, cap),
-        "dx",
-        [part] * peers + [sds((2 * rows, ff))] * 2,
-        (half, sums, hidden, gate_w, up_w, *whole(dh_sum, dp_count, SYNC[3])),
-        scratch=[pltpu.VMEM((2, rows, ff), BF), pltpu.VMEM((2 * rows, 1), F32)],
-        flops=4 * work,
-    )
-    outs = [outs[0]] + [swap(outs[j], "expert", j) for j in range(1, peers)]
-    dxs = [dxs[0]] + [swap(dxs[j], "expert", j) for j in range(1, peers)]
+        functools.partial(near_kernel, near, cap),
+        "near",
+        [part] * (2 * near) + [sds((rows, ff))] * 3,
+        (half, dh, gate_w, up_w, down_w, *near_sums),
+        scratch=[pltpu.VMEM((2, rows // 2, 2 * ff), BF), pltpu.VMEM((rows, 1), F32)],
+        flops=DX_FLOPS * work,
+    )
+    near_outs, near_dxs, (near_hidden, near_dgate, near_dup) = (
+        produced[:near],
+        produced[near:peers],
+        produced[peers:],
+    )
+    near_outs = [near_outs[0]] + [swap(near_outs[j], "expert", j) for j in range(1, near)]
+    near_dxs = [near_dxs[0]] + [swap(near_dxs[j], "expert", j) for j in range(1, near)]
+
     grad_gate, grad_up, grad_down = call(
         functools.partial(grad_kernel, peers),
         "grads",
         [sds((width, ff))] * 2 + [sds((ff, width))],
-        (*xs, *cs, hidden, dgate, dup),
+        (*xs, *cs, near_hidden, far_hidden, near_dgate, far_dgate, near_dup, far_dup),
         scalars=0,
         flops=6 * work,
     )
-    (mixed,) = call(
-        functools.partial(mix_kernel, peers),
-        "mix",
-        [sds((count, width))],
-        (me, routes_t, gates_t, place, *outs),
-        flops=8 * rows * count * width,
-    )
-    grad_tokens, gates_grad = call(
+    mixed, grad_tokens, gates_grad = call(
         functools.partial(merge_kernel, peers, cap),
         "merge",
-        [sds((count, width)), sds((top, count), F32)],
-        (me, routes_t, gates_t, place, *dxs),
-        flops=4 * rows * count * width,
+        [sds((count, width))] * 2 + [sds((top, count), F32)],
+        (me, routes_t, gates_t, place, far_mixed, *near_outs, *near_dxs, *dxs),
+        flops=8 * rows * count * width,
     )
     return (mixed, grad_tokens, gates_grad.T, grad_gate[None], grad_up[None], grad_down[None])
 

time: 68.7 us -> 65.5 us (0.953)
  starting transfers between devices: 21.8 us -> 27.5 us
  waiting for transfers between devices: 23 us -> 18.3 us
  blocking collectives: 4.11 us -> 0 us
    ppermute x17 -> x24, starting transfers between devices: 21.8 us -> 27.5 us  [swap(): return lax.ppermute(block, axis, [(i, i ^ offset) for i in range(count)])]
    ppermute x17 -> x24, waiting for transfers between devices: 23 us -> 18.3 us  [swap(): return lax.ppermute(block, axis, [(i, i ^ offset) for i in range(count)])]
    all_to_all x1 -> x0, blocking collectives: 4.11 us -> none  [whole(): lax.all_to_all(twice, 'dp', 0, 0, axis_index_groups=pairs_of(dp_count))]
    pallas_call x10 -> x11, Pallas kernels: 10.6 us -> 10.5 us  [call(): pl.pallas_call(kernel, name=name, out_shape=outs, in_specs=[smem] * scala...]
  transfers between devices with their start and end apart: 17 -> 24, of which waited for: 7 -> 11; matrix products, arithmetic and copies ran while one was open for 0% -> 1% of each run, Pallas kernels for 11% -> 12%
where the time goes in v4:
time: 65.5 us; the launch traced here: 65.2 us
  starting transfers between devices  27.5 us (42%)
  waiting for transfers between devices  18.3 us (28%)
  Pallas kernels  10.5 us (16%)
  local copies, waits for them, and re-layouts  7.7 us (12%)
  between operations  0.82 us (1%)
    ppermute x24, starting transfers between devices, swap(): return lax.ppermute(block, axis, [(i, i ^ offset) for i in range(count)])  27.5 us
    ppermute x24, waiting for transfers between devices, swap(): return lax.ppermute(block, axis, [(i, i ^ offset) for i in range(count)])  18.3 us
    pallas_call x11, Pallas kernels, call(): pl.pallas_call(kernel, name=name, out_shape=outs, in_specs=[smem] * scala...  10.5 us
    unnamed x20, local copies, waits for them, and re-layouts  7.7 us
  transfers between devices with their start and end apart: 24, of which 11 were waited for; matrix products, arithmetic and copies ran while one was open for 1% of the time, Pallas kernels for 12%

profile of v4, /device:TPU:0, one launch (start us, length us, event | category | flops | bytes accessed | tf_op | source)
XLA Modules:
  0.0 65.2 jit_solution(17102669787518119094)
XLA Ops:
  0.6 0.7 %copy-done.4 = s32[128,2]{0,1:T(2,128)S(1)} copy-done((s32[128,2]{0,1:T(2,128)S(1)}, s32[128,2]{0,1:T(2,128)}, u32[]{:S(2)}) %copy-start.4) | copy-done | bytes 1048
  1.3 0.9 %copy-done.9 = bf16[128,768]{1,0:T(8,128)(2,1)S(1)} copy-done((bf16[128,768]{1,0:T(8,128)(2,1)S(1)}, bf16[128,768]{1,0:T(8,128)(2,1)}, u32[]{:S(2)}) %copy-start.9) | copy-done | bytes 196632
  2.2 0.4 pack.1
  2.7 4.1 %collective-permute-start = (bf16[80,768]{1,0:T(8,128)(2,1)S(1)}, bf16[80,768]{1,0:T(8,128)(2,1)S(1)}, u32[]{:S(2)}, u32[]{:S(2)}) collective-permute-start(bf16[80,768]{1,0:T(8,128)(2,1)S(1)} %get-tuple-element.57), channel_id=1, source_target_pairs={{0,8},{4,12},{8,0},{12,4},{1,9},{5,13},{9,1},{13,5},{2,10},{6,14},... | collective-permute-start | bytes 368648 | tf_op jit(solution)/shard_map/ppermute | solution.py:19
  6.8 1.3 %collective-permute-start.1 = (bf16[80,768]{1,0:T(8,128)(2,1)S(1)}, bf16[80,768]{1,0:T(8,128)(2,1)S(1)}, u32[]{:S(2)}, u32[]{:S(2)}) collective-permute-start(bf16[80,768]{1,0:T(8,128)(2,1)S(1)} %get-tuple-element.58), channel_id=1, source_target_pairs={{0,12},{4,8},{8,4},{12,0},{1,13},{5,9},{9,5},{13,1},{2,14},{6,10},... | collective-permute-start | bytes 368648 | tf_op jit(solution)/shard_map/ppermute | solution.py:19
  8.1 0.2 collective-permute-start.2
  8.3 0.9 %copy-done.3 = bf16[128,768]{1,0:T(8,128)(2,1)S(1)} copy-done((bf16[128,768]{1,0:T(8,128)(2,1)S(1)}, bf16[128,768]{1,0:T(8,128)(2,1)}, u32[]{:S(2)}) %copy-start.3) | copy-done | bytes 196632
  9.3 0.7 %copy-done.5 = s32[128,2]{0,1:T(2,128)S(1)} copy-done((s32[128,2]{0,1:T(2,128)S(1)}, s32[128,2]{0,1:T(2,128)}, u32[]{:S(2)}) %copy-start.5) | copy-done | bytes 1048
  10.0 0.7 %copy-done.7 = f32[128,2]{0,1:T(2,128)S(1)} copy-done((f32[128,2]{0,1:T(2,128)S(1)}, f32[128,2]{0,1:T(2,128)}, u32[]{:S(2)}) %copy-start.7) | copy-done | bytes 1048
  10.6 0.3 pack_cot.1
  10.9 1.3 %copy-done = bf16[1,768,768]{2,1,0:T(8,128)(2,1)S(1)} copy-done((bf16[1,768,768]{2,1,0:T(8,128)(2,1)S(1)}, bf16[1,768,768]{2,1,0:T(8,128)(2,1)}, u32[]{:S(2)}) %copy-start) | copy-done | bytes 1179672
  12.2 1.3 %copy-done.1 = bf16[1,768,768]{2,1,0:T(8,128)(2,1)S(1)} copy-done((bf16[1,768,768]{2,1,0:T(8,128)(2,1)S(1)}, bf16[1,768,768]{2,1,0:T(8,128)(2,1)}, u32[]{:S(2)}) %copy-start.1) | copy-done | bytes 1179672
  13.5 1.3 %copy-done.2 = bf16[1,768,768]{2,1,0:T(8,128)(2,1)S(1)} copy-done((bf16[1,768,768]{2,1,0:T(8,128)(2,1)S(1)}, bf16[1,768,768]{2,1,0:T(8,128)(2,1)}, u32[]{:S(2)}) %copy-start.2) | copy-done | bytes 1179672
  14.7 0.7 %load.1 = (bf16[768,768]{1,0:T(8,128)(2,1)S(1)}, bf16[768,768]{1,0:T(8,128)(2,1)S(1)}, bf16[768,768]{1,0:T(8,128)(2,1)S(1)}) custom-call(bf16[768,768]{1,0:T(8,128)(2,1)S(1)} %bitcast.11, bf16[768,768]{1,0:T(8,128)(2,1)S(1)} %bitcast.12, bf16[768,768]{1,0:T(8,128)(2,1)S(1)} %bitcast.13), custom_call_target="tpu_custom_call" | custom-call | bytes 7077888 | tf_op jit(solution)/shard_map/load/pallas_call | solution.py:40
  15.5 0.7 %collective-permute-done.refs_0_.refs_2_ = bf16[80,768]{1,0:T(8,128)(2,1)S(1)} collective-permute-done((bf16[80,768]{1,0:T(8,128)(2,1)S(1)}, bf16[80,768]{1,0:T(8,128)(2,1)S(1)}, u32[]{:S(2)}, u32[]{:S(2)}) %collective-permute-start) | collective-permute-done | bytes 122912 | tf_op jit(solution)/shard_map/ppermute | solution.py:19
  16.2 0.5 collective-permute-done.2.refs_3_.refs_1_
  16.8 1.4 %up.1 = (bf16[80,1536]{1,0:T(8,128)(2,1)S(1)}, bf16[80,1536]{1,0:T(8,128)(2,1)S(1)}, bf16[80,1536]{1,0:T(8,128)(2,1)S(1)}, bf16[80,1536]{1,0:T(8,128)(2,1)S(1)}) custom-call(s32[1]{0:T(128)} %bitcast.3.half_ref, bf16[80,768]{1,0:T(8,128)(2,1)S(1)} %collective-permute-done.refs_0_.refs_2_, bf16[80,768]{1,0:T(8,128)(2,1)S(1)} %collective-permute-done.1.refs_1_.refs_3_, ...), custom_call_target="tpu_custom_call" | custom-call | flops 754974720 | bytes 3833860 | tf_op jit(solution)/shard_map/up/pallas_call | solution.py:40
  18.3 4.0 %collective-permute-start.9 = (bf16[80,768]{1,0:T(8,128)(2,1)S(1)}, bf16[80,768]{1,0:T(8,128)(2,1)S(1)}, u32[]{:S(2)}, u32[]{:S(2)}) collective-permute-start(bf16[80,768]{1,0:T(8,128)(2,1)S(1)} %get-tuple-element.76), channel_id=1, source_target_pairs={{0,8},{4,12},{8,0},{12,4},{1,9},{5,13},{9,1},{13,5},{2,10},{6,14},... | collective-permute-start | bytes 368648 | tf_op jit(solution)/shard_map/ppermute | solution.py:19
  22.3 0.4 collective-permute-start.10
  22.7 0.2 collective-permute-start.11
  23.0 1.6 %collective-permute-start.4 = (bf16[80,1536]{1,0:T(8,128)(2,1)S(1)}, bf16[80,1536]{1,0:T(8,128)(2,1)S(1)}, u32[]{:S(2)}, u32[]{:S(2)}) collective-permute-start(bf16[80,1536]{1,0:T(8,128)(2,1)S(1)} %add_convert_fusion.3), channel_id=1, source_target_pairs={{0,2},{1,3},{2,0},{3,1},{4,6},{5,7},{6,4},{7,5},{8,10},{9,11},{10,... | collective-permute-start | bytes 737288 | tf_op jit(solution)/shard_map/ppermute | solution.py:19
  24.6 1.4 %collective-permute-start.17 = (bf16[80,1536]{1,0:T(8,128)(2,1)S(1)}, bf16[80,1536]{1,0:T(8,128)(2,1)S(1)}, u32[]{:S(2)}, u32[]{:S(2)}) collective-permute-start(bf16[80,1536]{1,0:T(8,128)(2,1)S(1)} %add_convert_fusion.1), channel_id=1, source_target_pairs={{0,2},{1,3},{2,0},{3,1},{4,6},{5,7},{6,4},{7,5},{8,10},{9,11},{10,... | collective-permute-start | bytes 737288 | tf_op jit(solution)/shard_map/ppermute | solution.py:19
  26.0 5.7 %collective-permute-done.9.refs_0_.refs_6_ = bf16[80,768]{1,0:T(8,128)(2,1)S(1)} collective-permute-done((bf16[80,768]{1,0:T(8,128)(2,1)S(1)}, bf16[80,768]{1,0:T(8,128)(2,1)S(1)}, u32[]{:S(2)}, u32[]{:S(2)}) %collective-permute-start.9) | collective-permute-done | bytes 122912 | tf_op jit(solution)/shard_map/ppermute | solution.py:19
  31.7 1.1 %collective-permute-done.11.refs_3_.refs_5_ = bf16[80,768]{1,0:T(8,128)(2,1)S(1)} collective-permute-done((bf16[80,768]{1,0:T(8,128)(2,1)S(1)}, bf16[80,768]{1,0:T(8,128)(2,1)S(1)}, u32[]{:S(2)}, u32[]{:S(2)}) %collective-permute-start.11) | collective-permute-done | bytes 122912 | tf_op jit(solution)/shard_map/ppermute | solution.py:19
  32.8 0.6 back.1
  33.6 0.6 collective-permute-start.5
  34.2 0.9 %collective-permute-done.12 = bf16[160,768]{1,0:T(8,128)(2,1)S(1)} collective-permute-done((bf16[160,768]{1,0:T(8,128)(2,1)S(1)}, bf16[160,768]{1,0:T(8,128)(2,1)S(1)}, u32[]{:S(2)}, u32[]{:S(2)}) %collective-permute-start.12) | collective-permute-done | bytes 245792 | tf_op jit(solution)/shard_map/ppermute | solution.py:19
  35.1 1.6 %collective-permute-start.13 = (bf16[160,768]{1,0:T(8,128)(2,1)S(1)}, bf16[160,768]{1,0:T(8,128)(2,1)S(1)}, u32[]{:S(2)}, u32[]{:S(2)}) collective-permute-start(bf16[160,768]{1,0:T(8,128)(2,1)S(1)} %add_convert_fusion), channel_id=1, source_target_pairs={{0,2},{1,3},{2,0},{3,1},{4,6},{5,7},{6,4},{7,5},{8,10},{9,11},{10,... | collective-permute-start | bytes 737288 | tf_op jit(solution)/shard_map/ppermute | solution.py:19
  36.7 0.4 out.1
  37.1 2.7 %collective-permute-start.6 = (bf16[80,768]{1,0:T(8,128)(2,1)S(1)}, bf16[80,768]{1,0:T(8,128)(2,1)S(1)}, u32[]{:S(2)}, u32[]{:S(2)}) collective-permute-start(bf16[80,768]{1,0:T(8,128)(2,1)S(1)} %get-tuple-element.70), channel_id=1, source_target_pairs={{0,8},{4,12},{8,0},{12,4},{1,9},{5,13},{9,1},{13,5},{2,10},{6,14},... | collective-permute-start | bytes 368648 | tf_op jit(solution)/shard_map/ppermute | solution.py:19
  39.8 1.6 %collective-permute-start.7 = (bf16[80,768]{1,0:T(8,128)(2,1)S(1)}, bf16[80,768]{1,0:T(8,128)(2,1)S(1)}, u32[]{:S(2)}, u32[]{:S(2)}) collective-permute-start(bf16[80,768]{1,0:T(8,128)(2,1)S(1)} %get-tuple-element.71), channel_id=1, source_target_pairs={{0,12},{4,8},{8,4},{12,0},{1,13},{5,9},{9,5},{13,1},{2,14},{6,10},... | collective-permute-start | bytes 368648 | tf_op jit(solution)/shard_map/ppermute | solution.py:19
  41.4 1.8 %collective-permute-done.13 = bf16[160,768]{1,0:T(8,128)(2,1)S(1)} collective-permute-done((bf16[160,768]{1,0:T(8,128)(2,1)S(1)}, bf16[160,768]{1,0:T(8,128)(2,1)S(1)}, u32[]{:S(2)}, u32[]{:S(2)}) %collective-permute-start.13) | collective-permute-done | bytes 245792 | tf_op jit(solution)/shard_map/ppermute | solution.py:19
  43.3 0.5 collective-permute-start.15
  44.0 0.6 collective-permute-done.16.refs_5_
  44.7 0.4 collective-permute-start.14
  45.1 0.9 %collective-permute-done.14.refs_3_ = bf16[160,256]{1,0:T(8,128)(2,1)S(1)} collective-permute-done((bf16[160,256]{1,0:T(8,128)(2,1)S(1)}, bf16[160,256]{1,0:T(8,128)(2,1)S(1)}, u32[]{:S(2)}, u32[]{:S(2)}) %collective-permute-start.14) | collective-permute-done | bytes 81952 | tf_op jit(solution)/shard_map/ppermute | solution.py:19
  46.0 1.0 %dx.1 = (bf16[80,768]{1,0:T(8,128)(2,1)S(1)}, bf16[80,768]{1,0:T(8,128)(2,1)S(1)}, bf16[160,768]{1,0:T(8,128)(2,1)S(1)}, bf16[160,768]{1,0:T(8,128)(2,1)S(1)}, bf16[2,160,768]{2,1,0:T(8,128)(2,1)S(1)}) custom-call(s32[1]{0:T(128)} %bitcast.3.half_ref, bf16[2,80,1536]{2,1,0:T(8,128)(2,1)S(1)} %get-tuple-element.72.far_ref, ...), custom_call_target="tpu_custom_call" | custom-call | bytes 4816900 | tf_op jit(solution)/shard_map/dx/pallas_call | solution.py:40
  47.0 2.7 %collective-permute-start.22 = (bf16[80,768]{1,0:T(8,128)(2,1)S(1)}, bf16[80,768]{1,0:T(8,128)(2,1)S(1)}, u32[]{:S(2)}, u32[]{:S(2)}) collective-permute-start(bf16[80,768]{1,0:T(8,128)(2,1)S(1)} %get-tuple-element.93), channel_id=1, source_target_pairs={{0,8},{4,12},{8,0},{12,4},{1,9},{5,13},{9,1},{13,5},{2,10},{6,14},... | collective-permute-start | bytes 368648 | tf_op jit(solution)/shard_map/ppermute | solution.py:19
  49.7 1.6 %collective-permute-start.23 = (bf16[80,768]{1,0:T(8,128)(2,1)S(1)}, bf16[80,768]{1,0:T(8,128)(2,1)S(1)}, u32[]{:S(2)}, u32[]{:S(2)}) collective-permute-start(bf16[80,768]{1,0:T(8,128)(2,1)S(1)} %get-tuple-element.94), channel_id=1, source_target_pairs={{0,12},{4,8},{8,4},{12,0},{1,13},{5,9},{9,5},{13,1},{2,14},{6,10},... | collective-permute-start | bytes 368648 | tf_op jit(solution)/shard_map/ppermute | solution.py:19
  51.3 0.3 mix.1.far_ref
  51.7 1.2 %near.1 = (bf16[80,768]{1,0:T(8,128)(2,1)S(1)}, bf16[80,768]{1,0:T(8,128)(2,1)S(1)}, bf16[80,768]{1,0:T(8,128)(2,1)S(1)}, bf16[80,768]{1,0:T(8,128)(2,1)S(1)}, b...) custom-call(s32[1]{0:T(128)} %bitcast.3.half_ref, ...), custom_call_target="tpu_custom_call" | custom-call | bytes 5750788 | tf_op jit(solution)/shard_map/near/pallas_call | solution.py:40
  52.8 1.8 %collective-permute-start.20 = (bf16[80,768]{1,0:T(8,128)(2,1)S(1)}, bf16[80,768]{1,0:T(8,128)(2,1)S(1)}, u32[]{:S(2)}, u32[]{:S(2)}) collective-permute-start(bf16[80,768]{1,0:T(8,128)(2,1)S(1)} %get-tuple-element.90), channel_id=1, source_target_pairs={{0,4},{4,0},{8,12},{12,8},{1,5},{5,1},{9,13},{13,9},{2,6},{6,2},{1... | collective-permute-start | bytes 368648 | tf_op jit(solution)/shard_map/ppermute | solution.py:19
  54.6 0.3 collective-permute-start.21
  54.9 3.1 %grads.1 = (bf16[768,768]{1,0:T(8,128)(2,1)}, bf16[768,768]{1,0:T(8,128)(2,1)}, bf16[768,768]{1,0:T(8,128)(2,1)}) custom-call(bf16[80,768]{1,0:T(8,128)(2,1)S(1)} %get-tuple-element.59.refs_2_.refs_0_, bf16[80,768]{1,0:T(8,128)(2,1)S(1)} %collective-permute-done.2.refs_3_.refs_1_, bf16[80,768]{1,0:T(8,128)(2,1)S(1)} %collective-permute-done.refs_0_.refs_2_, ...), custom_call_target="tpu_custom_call" | custom-call | flops 1132462080 | bytes 5996544 | tf_op jit(solution)/shard_map/grads/pallas_call | solution.py:40
  58.0 1.4 %collective-permute-done.22.refs_4_ = bf16[80,768]{1,0:T(8,128)(2,1)S(1)} collective-permute-done((bf16[80,768]{1,0:T(8,128)(2,1)S(1)}, bf16[80,768]{1,0:T(8,128)(2,1)S(1)}, u32[]{:S(2)}, u32[]{:S(2)}) %collective-permute-start.22) | collective-permute-done | bytes 122912 | tf_op jit(solution)/shard_map/ppermute | solution.py:19
  59.4 2.3 %collective-permute-done.20.refs_1_ = bf16[80,768]{1,0:T(8,128)(2,1)S(1)} collective-permute-done((bf16[80,768]{1,0:T(8,128)(2,1)S(1)}, bf16[80,768]{1,0:T(8,128)(2,1)S(1)}, u32[]{:S(2)}, u32[]{:S(2)}) %collective-permute-start.20) | collective-permute-done | bytes 122912 | tf_op jit(solution)/shard_map/ppermute | solution.py:19
  61.7 2.4 %collective-permute-done.21.refs_3_ = bf16[80,768]{1,0:T(8,128)(2,1)S(1)} collective-permute-done((bf16[80,768]{1,0:T(8,128)(2,1)S(1)}, bf16[80,768]{1,0:T(8,128)(2,1)S(1)}, u32[]{:S(2)}, u32[]{:S(2)}) %collective-permute-start.21) | collective-permute-done | bytes 122912 | tf_op jit(solution)/shard_map/ppermute | solution.py:19
  64.1 1.1 %merge.1 = (bf16[128,768]{1,0:T(8,128)(2,1)}, bf16[128,768]{1,0:T(8,128)(2,1)}, f32[2,128]{1,0:T(2,128)}) custom-call(s32[1]{0:T(128)} %bitcast.me_ref, s32[2,128]{1,0:T(2,128)S(1)} %bitcast.17, f32[2,128]{1,0:T(2,128)S(1)} %bitcast.20, bf16[320,128]{1,0:T(8,128)(2,1)S(1)} %get-tuple-element.56.place_ref, f32[128,768]{1,0:T(8,128)S(1)} %mix.1.far_ref, ...), custom_call_target="tpu_custom_call" | custom-call | flops 125829120 | bytes 1608708 | tf_op jit(solution)/shard_map/merge/pallas_call | solution.py:40
  (37 shorter events, 0.9 us)
Async XLA Ops:
  0.6 0.7 %copy-start.4 = (s32[128,2]{0,1:T(2,128)S(1)}, s32[128,2]{0,1:T(2,128)}, u32[]{:S(2)}) copy-start(s32[128,2]{0,1:T(2,128)} %param.9) | copy-start | bytes 3076
  1.3 0.9 %copy-start.9 = (bf16[128,768]{1,0:T(8,128)(2,1)S(1)}, bf16[128,768]{1,0:T(8,128)(2,1)}, u32[]{:S(2)}) copy-start(bf16[128,768]{1,0:T(8,128)(2,1)} %tokens_ref.1) | copy-start | bytes 589828
  2.7 13.6 %collective-permute-start = (bf16[80,768]{1,0:T(8,128)(2,1)S(1)}, bf16[80,768]{1,0:T(8,128)(2,1)S(1)}, u32[]{:S(2)}, u32[]{:S(2)}) collective-permute-start(bf16[80,768]{1,0:T(8,128)(2,1)S(1)} %get-tuple-element.57), channel_id=1, source_target_pairs={{0,8},{4,12},{8,0},{12,4},{1,9},{5,13},{9,1},{13,5},{2,10},{6,14},... | collective-permute-start | bytes 368648 | tf_op jit(solution)/shard_map/ppermute | solution.py:19
  6.8 9.5 %collective-permute-start.1 = (bf16[80,768]{1,0:T(8,128)(2,1)S(1)}, bf16[80,768]{1,0:T(8,128)(2,1)S(1)}, u32[]{:S(2)}, u32[]{:S(2)}) collective-permute-start(bf16[80,768]{1,0:T(8,128)(2,1)S(1)} %get-tuple-element.58), channel_id=1, source_target_pairs={{0,12},{4,8},{8,4},{12,0},{1,13},{5,9},{9,5},{13,1},{2,14},{6,10},... | collective-permute-start | bytes 368648 | tf_op jit(solution)/shard_map/ppermute | solution.py:19
  8.1 8.6 %collective-permute-start.2 = (bf16[80,768]{1,0:T(8,128)(2,1)S(1)}, bf16[80,768]{1,0:T(8,128)(2,1)S(1)}, u32[]{:S(2)}, u32[]{:S(2)}) collective-permute-start(bf16[80,768]{1,0:T(8,128)(2,1)S(1)} %get-tuple-element.60), channel_id=1, source_target_pairs={{0,4},{4,0},{8,12},{12,8},{1,5},{5,1},{9,13},{13,9},{2,6},{6,2},{1... | collective-permute-start | bytes 368648 | tf_op jit(solution)/shard_map/ppermute | solution.py:19
  8.3 0.9 %copy-start.3 = (bf16[128,768]{1,0:T(8,128)(2,1)S(1)}, bf16[128,768]{1,0:T(8,128)(2,1)}, u32[]{:S(2)}) copy-start(bf16[128,768]{1,0:T(8,128)(2,1)} %cot_ref.1) | copy-start | bytes 589828
  9.3 0.7 %copy-start.5 = (s32[128,2]{0,1:T(2,128)S(1)}, s32[128,2]{0,1:T(2,128)}, u32[]{:S(2)}) copy-start(s32[128,2]{0,1:T(2,128)} %param.9) | copy-start | bytes 3076
  10.0 0.7 %copy-start.7 = (f32[128,2]{0,1:T(2,128)S(1)}, f32[128,2]{0,1:T(2,128)}, u32[]{:S(2)}) copy-start(f32[128,2]{0,1:T(2,128)} %param.10) | copy-start | bytes 3076
  10.9 1.3 %copy-start = (bf16[1,768,768]{2,1,0:T(8,128)(2,1)S(1)}, bf16[1,768,768]{2,1,0:T(8,128)(2,1)}, u32[]{:S(2)}) copy-start(bf16[1,768,768]{2,1,0:T(8,128)(2,1)} %param.11) | copy-start | bytes 3538948
  12.2 1.3 %copy-start.1 = (bf16[1,768,768]{2,1,0:T(8,128)(2,1)S(1)}, bf16[1,768,768]{2,1,0:T(8,128)(2,1)}, u32[]{:S(2)}) copy-start(bf16[1,768,768]{2,1,0:T(8,128)(2,1)} %param.12) | copy-start | bytes 3538948
  13.5 1.3 %copy-start.2 = (bf16[1,768,768]{2,1,0:T(8,128)(2,1)S(1)}, bf16[1,768,768]{2,1,0:T(8,128)(2,1)}, u32[]{:S(2)}) copy-start(bf16[1,768,768]{2,1,0:T(8,128)(2,1)} %param.13) | copy-start | bytes 3538948
  18.2 4.7 %collective-permute-start.3 = (bf16[80,1536]{1,0:T(8,128)(2,1)S(1)}, bf16[80,1536]{1,0:T(8,128)(2,1)S(1)}, u32[]{:S(2)}, u32[]{:S(2)}) collective-permute-start(bf16[80,1536]{1,0:T(8,128)(2,1)S(1)} %get-tuple-element.68), channel_id=1, source_target_pairs={{0,1},{1,0},{2,3},{3,2},{4,5},{5,4},{6,7},{7,6},{8,9},{9,8},{10,11... | collective-permute-start | bytes 737288 | tf_op jit(solution)/shard_map/ppermute | solution.py:19
  18.3 13.5 %collective-permute-start.9 = (bf16[80,768]{1,0:T(8,128)(2,1)S(1)}, bf16[80,768]{1,0:T(8,128)(2,1)S(1)}, u32[]{:S(2)}, u32[]{:S(2)}) collective-permute-start(bf16[80,768]{1,0:T(8,128)(2,1)S(1)} %get-tuple-element.76), channel_id=1, source_target_pairs={{0,8},{4,12},{8,0},{12,4},{1,9},{5,13},{9,1},{13,5},{2,10},{6,14},... | collective-permute-start | bytes 368648 | tf_op jit(solution)/shard_map/ppermute | solution.py:19
  22.3 9.5 %collective-permute-start.10 = (bf16[80,768]{1,0:T(8,128)(2,1)S(1)}, bf16[80,768]{1,0:T(8,128)(2,1)S(1)}, u32[]{:S(2)}, u32[]{:S(2)}) collective-permute-start(bf16[80,768]{1,0:T(8,128)(2,1)S(1)} %get-tuple-element.77), channel_id=1, source_target_pairs={{0,12},{4,8},{8,4},{12,0},{1,13},{5,9},{9,5},{13,1},{2,14},{6,10},... | collective-permute-start | bytes 368648 | tf_op jit(solution)/shard_map/ppermute | solution.py:19
  22.7 10.1 %collective-permute-start.11 = (bf16[80,768]{1,0:T(8,128)(2,1)S(1)}, bf16[80,768]{1,0:T(8,128)(2,1)S(1)}, u32[]{:S(2)}, u32[]{:S(2)}) collective-permute-start(bf16[80,768]{1,0:T(8,128)(2,1)S(1)} %get-tuple-element.78), channel_id=1, source_target_pairs={{0,4},{4,0},{8,12},{12,8},{1,5},{5,1},{9,13},{13,9},{2,6},{6,2},{1... | collective-permute-start | bytes 368648 | tf_op jit(solution)/shard_map/ppermute | solution.py:19
  22.9 1.6 %collective-permute-start.8 = (bf16[80,1536]{1,0:T(8,128)(2,1)S(1)}, bf16[80,1536]{1,0:T(8,128)(2,1)S(1)}, u32[]{:S(2)}, u32[]{:S(2)}) collective-permute-start(bf16[80,1536]{1,0:T(8,128)(2,1)S(1)} %get-tuple-element.75), channel_id=1, source_target_pairs={{0,1},{1,0},{2,3},{3,2},{4,5},{5,4},{6,7},{7,6},{8,9},{9,8},{10,11... | collective-permute-start | bytes 737288 | tf_op jit(solution)/shard_map/ppermute | solution.py:19
  23.0 10.6 %collective-permute-start.4 = (bf16[80,1536]{1,0:T(8,128)(2,1)S(1)}, bf16[80,1536]{1,0:T(8,128)(2,1)S(1)}, u32[]{:S(2)}, u32[]{:S(2)}) collective-permute-start(bf16[80,1536]{1,0:T(8,128)(2,1)S(1)} %add_convert_fusion.3), channel_id=1, source_target_pairs={{0,2},{1,3},{2,0},{3,1},{4,6},{5,7},{6,4},{7,5},{8,10},{9,11},{10,... | collective-permute-start | bytes 737288 | tf_op jit(solution)/shard_map/ppermute | solution.py:19
  24.6 15.2 %collective-permute-start.17 = (bf16[80,1536]{1,0:T(8,128)(2,1)S(1)}, bf16[80,1536]{1,0:T(8,128)(2,1)S(1)}, u32[]{:S(2)}, u32[]{:S(2)}) collective-permute-start(bf16[80,1536]{1,0:T(8,128)(2,1)S(1)} %add_convert_fusion.1), channel_id=1, source_target_pairs={{0,2},{1,3},{2,0},{3,1},{4,6},{5,7},{6,4},{7,5},{8,10},{9,11},{10,... | collective-permute-start | bytes 737288 | tf_op jit(solution)/shard_map/ppermute | solution.py:19
  33.5 1.6 %collective-permute-start.12 = (bf16[160,768]{1,0:T(8,128)(2,1)S(1)}, bf16[160,768]{1,0:T(8,128)(2,1)S(1)}, u32[]{:S(2)}, u32[]{:S(2)}) collective-permute-start(bf16[160,768]{1,0:T(8,128)(2,1)S(1)} %get-tuple-element.84), channel_id=1, source_target_pairs={{0,1},{1,0},{2,3},{3,2},{4,5},{5,4},{6,7},{7,6},{8,9},{9,8},{10,11... | collective-permute-start | bytes 737288 | tf_op jit(solution)/shard_map/ppermute | solution.py:19
  33.6 3.1 %collective-permute-start.5 = (bf16[80,1536]{1,0:T(8,128)(2,1)S(1)}, bf16[80,1536]{1,0:T(8,128)(2,1)S(1)}, u32[]{:S(2)}, u32[]{:S(2)}) collective-permute-start(bf16[80,1536]{1,0:T(8,128)(2,1)S(1)} %add_convert_fusion.2.mine_ref), channel_id=1, source_target_pairs={{0,1},{1,0},{2,3},{3,2},{4,5},{5,4},{6,7},{7,6},{8,9},{9,8},{10,11... | collective-permute-start | bytes 737288 | tf_op jit(solution)/shard_map/ppermute | solution.py:19
  35.1 8.1 %collective-permute-start.13 = (bf16[160,768]{1,0:T(8,128)(2,1)S(1)}, bf16[160,768]{1,0:T(8,128)(2,1)S(1)}, u32[]{:S(2)}, u32[]{:S(2)}) collective-permute-start(bf16[160,768]{1,0:T(8,128)(2,1)S(1)} %add_convert_fusion), channel_id=1, source_target_pairs={{0,2},{1,3},{2,0},{3,1},{4,6},{5,7},{6,4},{7,5},{8,10},{9,11},{10,... | collective-permute-start | bytes 737288 | tf_op jit(solution)/shard_map/ppermute | solution.py:19
  37.1 14.2 %collective-permute-start.6 = (bf16[80,768]{1,0:T(8,128)(2,1)S(1)}, bf16[80,768]{1,0:T(8,128)(2,1)S(1)}, u32[]{:S(2)}, u32[]{:S(2)}) collective-permute-start(bf16[80,768]{1,0:T(8,128)(2,1)S(1)} %get-tuple-element.70), channel_id=1, source_target_pairs={{0,8},{4,12},{8,0},{12,4},{1,9},{5,13},{9,1},{13,5},{2,10},{6,14},... | collective-permute-start | bytes 368648 | tf_op jit(solution)/shard_map/ppermute | solution.py:19
  39.8 9.9 %collective-permute-start.7 = (bf16[80,768]{1,0:T(8,128)(2,1)S(1)}, bf16[80,768]{1,0:T(8,128)(2,1)S(1)}, u32[]{:S(2)}, u32[]{:S(2)}) collective-permute-start(bf16[80,768]{1,0:T(8,128)(2,1)S(1)} %get-tuple-element.71), channel_id=1, source_target_pairs={{0,12},{4,8},{8,4},{12,0},{1,13},{5,9},{9,5},{13,1},{2,14},{6,10},... | collective-permute-start | bytes 368648 | tf_op jit(solution)/shard_map/ppermute | solution.py:19
  43.2 1.3 %collective-permute-start.16 = (bf16[160,256]{1,0:T(8,128)(2,1)S(1)}, bf16[160,256]{1,0:T(8,128)(2,1)S(1)}, u32[]{:S(2)}, u32[]{:S(2)}) collective-permute-start(bf16[160,256]{1,0:T(8,128)(2,1)S(1)} %get-tuple-element.108.refs_2_), channel_id=1, source_target_pairs={{0,1},{1,0},{2,3},{3,2},{4,5},{5,4},{6,7},{7,6},{8,9},{9,8},{10,11... | collective-permute-start | bytes 245768 | tf_op jit(solution)/shard_map/ppermute | solution.py:19
  43.3 1.4 %collective-permute-start.15 = (bf16[160,256]{1,0:T(8,128)(2,1)S(1)}, bf16[160,256]{1,0:T(8,128)(2,1)S(1)}, u32[]{:S(2)}, u32[]{:S(2)}) collective-permute-start(bf16[160,256]{1,0:T(8,128)(2,1)S(1)} %get-tuple-element.109.refs_1_), channel_id=1, source_target_pairs={{0,1},{1,0},{2,3},{3,2},{4,5},{5,4},{6,7},{7,6},{8,9},{9,8},{10,11... | collective-permute-start | bytes 245768 | tf_op jit(solution)/shard_map/ppermute | solution.py:19
  43.9 7.8 %collective-permute-start.19 = (bf16[80,768]{1,0:T(8,128)(2,1)S(1)}, bf16[80,768]{1,0:T(8,128)(2,1)S(1)}, u32[]{:S(2)}, u32[]{:S(2)}) collective-permute-start(bf16[80,768]{1,0:T(8,128)(2,1)S(1)} %get-tuple-element.106.refs_1_), channel_id=1, source_target_pairs={{0,1},{1,0},{2,3},{3,2},{4,5},{5,4},{6,7},{7,6},{8,9},{9,8},{10,11... | collective-permute-start | bytes 368648 | tf_op jit(solution)/shard_map/ppermute | solution.py:19
  44.6 7.1 %collective-permute-start.18 = (bf16[80,768]{1,0:T(8,128)(2,1)S(1)}, bf16[80,768]{1,0:T(8,128)(2,1)S(1)}, u32[]{:S(2)}, u32[]{:S(2)}) collective-permute-start(bf16[80,768]{1,0:T(8,128)(2,1)S(1)} %get-tuple-element.107.refs_0_), channel_id=1, source_target_pairs={{0,1},{1,0},{2,3},{3,2},{4,5},{5,4},{6,7},{7,6},{8,9},{9,8},{10,11... | collective-permute-start | bytes 368648 | tf_op jit(solution)/shard_map/ppermute | solution.py:19
  44.7 1.3 %collective-permute-start.14 = (bf16[160,256]{1,0:T(8,128)(2,1)S(1)}, bf16[160,256]{1,0:T(8,128)(2,1)S(1)}, u32[]{:S(2)}, u32[]{:S(2)}) collective-permute-start(bf16[160,256]{1,0:T(8,128)(2,1)S(1)} %get-tuple-element.110.refs_0_), channel_id=1, source_target_pairs={{0,1},{1,0},{2,3},{3,2},{4,5},{5,4},{6,7},{7,6},{8,9},{9,8},{10,11... | collective-permute-start | bytes 245768 | tf_op jit(solution)/shard_map/ppermute | solution.py:19
  46.0 5.3 %copy-start.6 = (s32[128,2]{0,1:T(2,128)S(1)}, s32[128,2]{0,1:T(2,128)}, u32[]{:S(2)}) copy-start(s32[128,2]{0,1:T(2,128)} %param.9) | copy-start | bytes 3076
  46.0 5.3 %copy-start.8 = (f32[128,2]{0,1:T(2,128)S(1)}, f32[128,2]{0,1:T(2,128)}, u32[]{:S(2)}) copy-start(f32[128,2]{0,1:T(2,128)} %param.10) | copy-start | bytes 3076
  47.0 12.4 %collective-permute-start.22 = (bf16[80,768]{1,0:T(8,128)(2,1)S(1)}, bf16[80,768]{1,0:T(8,128)(2,1)S(1)}, u32[]{:S(2)}, u32[]{:S(2)}) collective-permute-start(bf16[80,768]{1,0:T(8,128)(2,1)S(1)} %get-tuple-element.93), channel_id=1, source_target_pairs={{0,8},{4,12},{8,0},{12,4},{1,9},{5,13},{9,1},{13,5},{2,10},{6,14},... | collective-permute-start | bytes 368648 | tf_op jit(solution)/shard_map/ppermute | solution.py:19
  49.7 9.7 %collective-permute-start.23 = (bf16[80,768]{1,0:T(8,128)(2,1)S(1)}, bf16[80,768]{1,0:T(8,128)(2,1)S(1)}, u32[]{:S(2)}, u32[]{:S(2)}) collective-permute-start(bf16[80,768]{1,0:T(8,128)(2,1)S(1)} %get-tuple-element.94), channel_id=1, source_target_pairs={{0,12},{4,8},{8,4},{12,0},{1,13},{5,9},{9,5},{13,1},{2,14},{6,10},... | collective-permute-start | bytes 368648 | tf_op jit(solution)/shard_map/ppermute | solution.py:19
  52.8 8.8 %collective-permute-start.20 = (bf16[80,768]{1,0:T(8,128)(2,1)S(1)}, bf16[80,768]{1,0:T(8,128)(2,1)S(1)}, u32[]{:S(2)}, u32[]{:S(2)}) collective-permute-start(bf16[80,768]{1,0:T(8,128)(2,1)S(1)} %get-tuple-element.90), channel_id=1, source_target_pairs={{0,4},{4,0},{8,12},{12,8},{1,5},{5,1},{9,13},{13,9},{2,6},{6,2},{1... | collective-permute-start | bytes 368648 | tf_op jit(solution)/shard_map/ppermute | solution.py:19
  54.6 9.5 %collective-permute-start.21 = (bf16[80,768]{1,0:T(8,128)(2,1)S(1)}, bf16[80,768]{1,0:T(8,128)(2,1)S(1)}, u32[]{:S(2)}, u32[]{:S(2)}) collective-permute-start(bf16[80,768]{1,0:T(8,128)(2,1)S(1)} %get-tuple-element.92), channel_id=1, source_target_pairs={{0,4},{4,0},{8,12},{12,8},{1,5},{5,1},{9,13},{13,9},{2,6},{6,2},{1... | collective-permute-start | bytes 368648 | tf_op jit(solution)/shard_map/ppermute | solution.py:19

commit v5 on v4

--- a/solution.py
+++ b/solution.py
@@ -270,7 +270,12 @@
     )
 
 
-def merge_kernel(peers, cap, me_ref, routes_ref, gates_ref, place_ref, far_ref, *refs):
+def far_kernel(place_ref, *refs):
+    dx_refs, grad_ref = refs[:-1], refs[-1]
+    grad_ref[...] = dot_tn(place_ref[place_ref.shape[0] // 2 :, :], stack(dx_refs))
+
+
+def merge_kernel(peers, cap, me_ref, routes_ref, gates_ref, place_ref, far_ref, far_grad_ref, *refs):
     near = peers // 2
     out_refs, dx_refs, (mixed_ref, grad_ref, gates_out_ref) = refs[:near], refs[near:-3], refs[-3:]
     me = me_ref[0]
@@ -278,7 +283,8 @@
     cp = dx_refs[0].shape[0]
     mixed = weighted(peers, me, routes_ref, gates_ref, place_ref, stack(out_refs), 0)
     mixed_ref[...] = (far_ref[...] + mixed).astype(BF)
-    grad_ref[...] = dot_tn(place_ref[...], stack(dx_refs)).astype(BF)
+    near_dx = dot_tn(place_ref[: near * cp, :], stack(dx_refs[:near]))
+    grad_ref[...] = (far_grad_ref[...] + near_dx).astype(BF)
     total = jnp.zeros(gates.shape, F32)
     base = cap // 16 * 16
     at = cap - base
@@ -439,11 +445,19 @@
         scalars=0,
         flops=6 * work,
     )
+    (far_grad,) = call(
+        far_kernel,
+        "far",
+        [sds((count, width), F32)],
+        (place, *dxs),
+        scalars=0,
+        flops=0,
+    )
     mixed, grad_tokens, gates_grad = call(
         functools.partial(merge_kernel, peers, cap),
         "merge",
         [sds((count, width))] * 2 + [sds((top, count), F32)],
-        (me, routes_t, gates_t, place, far_mixed, *near_outs, *near_dxs, *dxs),
+        (me, routes_t, gates_t, place, far_mixed, far_grad, *near_outs, *near_dxs, *dxs),
         flops=8 * rows * count * width,
     )
     return (mixed, grad_tokens, gates_grad.T, grad_gate[None], grad_up[None], grad_down[None])

time: 65.5 us -> 65.5 us (level)
    pallas_call x11 -> x12, Pallas kernels: 10.5 us -> 10.8 us  [call(): pl.pallas_call(kernel, name=name, out_shape=outs, in_specs=[smem] * scala...]
where the time goes in v5:
time: 65.5 us; the launch traced here: 65.2 us
  starting transfers between devices  27.5 us (42%)
  waiting for transfers between devices  18 us (27%)
  Pallas kernels  10.8 us (16%)
  local copies, waits for them, and re-layouts  7.7 us (12%)
  between operations  0.83 us (1%)
    ppermute x24, starting transfers between devices, swap(): return lax.ppermute(block, axis, [(i, i ^ offset) for i in range(count)])  27.5 us
    ppermute x24, waiting for transfers between devices, swap(): return lax.ppermute(block, axis, [(i, i ^ offset) for i in range(count)])  18 us
    pallas_call x12, Pallas kernels, call(): pl.pallas_call(kernel, name=name, out_shape=outs, in_specs=[smem] * scala...  10.8 us
    unnamed x20, local copies, waits for them, and re-layouts  7.7 us
  transfers between devices with their start and end apart: 24, of which 11 were waited for; matrix products, arithmetic and copies ran while one was open for 1% of the time, Pallas kernels for 12%

profile of v5, /device:TPU:0, one launch (start us, length us, event | category | flops | bytes accessed | tf_op | source)
XLA Modules:
  0.0 65.2 jit_solution(10361827033911032480)
XLA Ops:
  0.6 0.7 %copy-done.4 = s32[128,2]{0,1:T(2,128)S(1)} copy-done((s32[128,2]{0,1:T(2,128)S(1)}, s32[128,2]{0,1:T(2,128)}, u32[]{:S(2)}) %copy-start.4) | copy-done | bytes 1048
  1.3 0.9 %copy-done.9 = bf16[128,768]{1,0:T(8,128)(2,1)S(1)} copy-done((bf16[128,768]{1,0:T(8,128)(2,1)S(1)}, bf16[128,768]{1,0:T(8,128)(2,1)}, u32[]{:S(2)}) %copy-start.9) | copy-done | bytes 196632
  2.2 0.4 pack.1
  2.7 4.1 %collective-permute-start = (bf16[80,768]{1,0:T(8,128)(2,1)S(1)}, bf16[80,768]{1,0:T(8,128)(2,1)S(1)}, u32[]{:S(2)}, u32[]{:S(2)}) collective-permute-start(bf16[80,768]{1,0:T(8,128)(2,1)S(1)} %get-tuple-element.57), channel_id=1, source_target_pairs={{0,8},{4,12},{8,0},{12,4},{1,9},{5,13},{9,1},{13,5},{2,10},{6,14},... | collective-permute-start | bytes 368648 | tf_op jit(solution)/shard_map/ppermute | solution.py:19
  6.8 1.3 %collective-permute-start.1 = (bf16[80,768]{1,0:T(8,128)(2,1)S(1)}, bf16[80,768]{1,0:T(8,128)(2,1)S(1)}, u32[]{:S(2)}, u32[]{:S(2)}) collective-permute-start(bf16[80,768]{1,0:T(8,128)(2,1)S(1)} %get-tuple-element.58), channel_id=1, source_target_pairs={{0,12},{4,8},{8,4},{12,0},{1,13},{5,9},{9,5},{13,1},{2,14},{6,10},... | collective-permute-start | bytes 368648 | tf_op jit(solution)/shard_map/ppermute | solution.py:19
  8.1 0.2 collective-permute-start.2
  8.3 0.9 %copy-done.3 = bf16[128,768]{1,0:T(8,128)(2,1)S(1)} copy-done((bf16[128,768]{1,0:T(8,128)(2,1)S(1)}, bf16[128,768]{1,0:T(8,128)(2,1)}, u32[]{:S(2)}) %copy-start.3) | copy-done | bytes 196632
  9.3 0.7 %copy-done.5 = s32[128,2]{0,1:T(2,128)S(1)} copy-done((s32[128,2]{0,1:T(2,128)S(1)}, s32[128,2]{0,1:T(2,128)}, u32[]{:S(2)}) %copy-start.5) | copy-done | bytes 1048
  10.0 0.7 %copy-done.7 = f32[128,2]{0,1:T(2,128)S(1)} copy-done((f32[128,2]{0,1:T(2,128)S(1)}, f32[128,2]{0,1:T(2,128)}, u32[]{:S(2)}) %copy-start.7) | copy-done | bytes 1048
  10.6 0.3 pack_cot.1
  10.9 1.3 %copy-done = bf16[1,768,768]{2,1,0:T(8,128)(2,1)S(1)} copy-done((bf16[1,768,768]{2,1,0:T(8,128)(2,1)S(1)}, bf16[1,768,768]{2,1,0:T(8,128)(2,1)}, u32[]{:S(2)}) %copy-start) | copy-done | bytes 1179672
  12.2 1.3 %copy-done.1 = bf16[1,768,768]{2,1,0:T(8,128)(2,1)S(1)} copy-done((bf16[1,768,768]{2,1,0:T(8,128)(2,1)S(1)}, bf16[1,768,768]{2,1,0:T(8,128)(2,1)}, u32[]{:S(2)}) %copy-start.1) | copy-done | bytes 1179672
  13.5 1.3 %copy-done.2 = bf16[1,768,768]{2,1,0:T(8,128)(2,1)S(1)} copy-done((bf16[1,768,768]{2,1,0:T(8,128)(2,1)S(1)}, bf16[1,768,768]{2,1,0:T(8,128)(2,1)}, u32[]{:S(2)}) %copy-start.2) | copy-done | bytes 1179672
  14.7 0.7 %load.1 = (bf16[768,768]{1,0:T(8,128)(2,1)S(1)}, bf16[768,768]{1,0:T(8,128)(2,1)S(1)}, bf16[768,768]{1,0:T(8,128)(2,1)S(1)}) custom-call(bf16[768,768]{1,0:T(8,128)(2,1)S(1)} %bitcast.11, bf16[768,768]{1,0:T(8,128)(2,1)S(1)} %bitcast.12, bf16[768,768]{1,0:T(8,128)(2,1)S(1)} %bitcast.13), custom_call_target="tpu_custom_call" | custom-call | bytes 7077888 | tf_op jit(solution)/shard_map/load/pallas_call | solution.py:40
  15.5 0.7 %collective-permute-done.refs_0_.refs_2_ = bf16[80,768]{1,0:T(8,128)(2,1)S(1)} collective-permute-done((bf16[80,768]{1,0:T(8,128)(2,1)S(1)}, bf16[80,768]{1,0:T(8,128)(2,1)S(1)}, u32[]{:S(2)}, u32[]{:S(2)}) %collective-permute-start) | collective-permute-done | bytes 122912 | tf_op jit(solution)/shard_map/ppermute | solution.py:19
  16.2 0.5 collective-permute-done.2.refs_3_.refs_1_
  16.8 1.4 %up.1 = (bf16[80,1536]{1,0:T(8,128)(2,1)S(1)}, bf16[80,1536]{1,0:T(8,128)(2,1)S(1)}, bf16[80,1536]{1,0:T(8,128)(2,1)S(1)}, bf16[80,1536]{1,0:T(8,128)(2,1)S(1)}) custom-call(s32[1]{0:T(128)} %bitcast.3.half_ref, bf16[80,768]{1,0:T(8,128)(2,1)S(1)} %collective-permute-done.refs_0_.refs_2_, bf16[80,768]{1,0:T(8,128)(2,1)S(1)} %collective-permute-done.1.refs_1_.refs_3_, ...), custom_call_target="tpu_custom_call" | custom-call | flops 754974720 | bytes 3833860 | tf_op jit(solution)/shard_map/up/pallas_call | solution.py:40
  18.3 4.0 %collective-permute-start.9 = (bf16[80,768]{1,0:T(8,128)(2,1)S(1)}, bf16[80,768]{1,0:T(8,128)(2,1)S(1)}, u32[]{:S(2)}, u32[]{:S(2)}) collective-permute-start(bf16[80,768]{1,0:T(8,128)(2,1)S(1)} %get-tuple-element.76), channel_id=1, source_target_pairs={{0,8},{4,12},{8,0},{12,4},{1,9},{5,13},{9,1},{13,5},{2,10},{6,14},... | collective-permute-start | bytes 368648 | tf_op jit(solution)/shard_map/ppermute | solution.py:19
  22.3 0.4 collective-permute-start.10
  23.0 1.6 %collective-permute-start.4 = (bf16[80,1536]{1,0:T(8,128)(2,1)S(1)}, bf16[80,1536]{1,0:T(8,128)(2,1)S(1)}, u32[]{:S(2)}, u32[]{:S(2)}) collective-permute-start(bf16[80,1536]{1,0:T(8,128)(2,1)S(1)} %add_convert_fusion.3), channel_id=1, source_target_pairs={{0,2},{1,3},{2,0},{3,1},{4,6},{5,7},{6,4},{7,5},{8,10},{9,11},{10,... | collective-permute-start | bytes 737288 | tf_op jit(solution)/shard_map/ppermute | solution.py:19
  24.6 1.4 %collective-permute-start.19 = (bf16[80,1536]{1,0:T(8,128)(2,1)S(1)}, bf16[80,1536]{1,0:T(8,128)(2,1)S(1)}, u32[]{:S(2)}, u32[]{:S(2)}) collective-permute-start(bf16[80,1536]{1,0:T(8,128)(2,1)S(1)} %add_convert_fusion.1), channel_id=1, source_target_pairs={{0,2},{1,3},{2,0},{3,1},{4,6},{5,7},{6,4},{7,5},{8,10},{9,11},{10,... | collective-permute-start | bytes 737288 | tf_op jit(solution)/shard_map/ppermute | solution.py:19
  26.0 5.7 %collective-permute-done.9.refs_0_.refs_6_ = bf16[80,768]{1,0:T(8,128)(2,1)S(1)} collective-permute-done((bf16[80,768]{1,0:T(8,128)(2,1)S(1)}, bf16[80,768]{1,0:T(8,128)(2,1)S(1)}, u32[]{:S(2)}, u32[]{:S(2)}) %collective-permute-start.9) | collective-permute-done | bytes 122912 | tf_op jit(solution)/shard_map/ppermute | solution.py:19
  31.7 1.1 %collective-permute-done.11.refs_3_.refs_5_ = bf16[80,768]{1,0:T(8,128)(2,1)S(1)} collective-permute-done((bf16[80,768]{1,0:T(8,128)(2,1)S(1)}, bf16[80,768]{1,0:T(8,128)(2,1)S(1)}, u32[]{:S(2)}, u32[]{:S(2)}) %collective-permute-start.11) | collective-permute-done | bytes 122912 | tf_op jit(solution)/shard_map/ppermute | solution.py:19
  32.8 0.6 back.1
  33.6 0.6 collective-permute-start.5
  34.2 0.9 %collective-permute-done.12 = bf16[160,768]{1,0:T(8,128)(2,1)S(1)} collective-permute-done((bf16[160,768]{1,0:T(8,128)(2,1)S(1)}, bf16[160,768]{1,0:T(8,128)(2,1)S(1)}, u32[]{:S(2)}, u32[]{:S(2)}) %collective-permute-start.12) | collective-permute-done | bytes 245792 | tf_op jit(solution)/shard_map/ppermute | solution.py:19
  35.1 1.6 %collective-permute-start.13 = (bf16[160,768]{1,0:T(8,128)(2,1)S(1)}, bf16[160,768]{1,0:T(8,128)(2,1)S(1)}, u32[]{:S(2)}, u32[]{:S(2)}) collective-permute-start(bf16[160,768]{1,0:T(8,128)(2,1)S(1)} %add_convert_fusion), channel_id=1, source_target_pairs={{0,2},{1,3},{2,0},{3,1},{4,6},{5,7},{6,4},{7,5},{8,10},{9,11},{10,... | collective-permute-start | bytes 737288 | tf_op jit(solution)/shard_map/ppermute | solution.py:19
  36.7 0.4 out.1
  37.1 2.7 %collective-permute-start.6 = (bf16[80,768]{1,0:T(8,128)(2,1)S(1)}, bf16[80,768]{1,0:T(8,128)(2,1)S(1)}, u32[]{:S(2)}, u32[]{:S(2)}) collective-permute-start(bf16[80,768]{1,0:T(8,128)(2,1)S(1)} %get-tuple-element.70), channel_id=1, source_target_pairs={{0,8},{4,12},{8,0},{12,4},{1,9},{5,13},{9,1},{13,5},{2,10},{6,14},... | collective-permute-start | bytes 368648 | tf_op jit(solution)/shard_map/ppermute | solution.py:19
  39.8 1.6 %collective-permute-start.7 = (bf16[80,768]{1,0:T(8,128)(2,1)S(1)}, bf16[80,768]{1,0:T(8,128)(2,1)S(1)}, u32[]{:S(2)}, u32[]{:S(2)}) collective-permute-start(bf16[80,768]{1,0:T(8,128)(2,1)S(1)} %get-tuple-element.71), channel_id=1, source_target_pairs={{0,12},{4,8},{8,4},{12,0},{1,13},{5,9},{9,5},{13,1},{2,14},{6,10},... | collective-permute-start | bytes 368648 | tf_op jit(solution)/shard_map/ppermute | solution.py:19
  41.4 1.8 %collective-permute-done.13 = bf16[160,768]{1,0:T(8,128)(2,1)S(1)} collective-permute-done((bf16[160,768]{1,0:T(8,128)(2,1)S(1)}, bf16[160,768]{1,0:T(8,128)(2,1)S(1)}, u32[]{:S(2)}, u32[]{:S(2)}) %collective-permute-start.13) | collective-permute-done | bytes 245792 | tf_op jit(solution)/shard_map/ppermute | solution.py:19
  43.3 0.5 collective-permute-start.15
  44.0 0.6 collective-permute-done.16.refs_5_
  44.7 0.4 collective-permute-start.14
  45.1 0.9 %collective-permute-done.14.refs_3_ = bf16[160,256]{1,0:T(8,128)(2,1)S(1)} collective-permute-done((bf16[160,256]{1,0:T(8,128)(2,1)S(1)}, bf16[160,256]{1,0:T(8,128)(2,1)S(1)}, u32[]{:S(2)}, u32[]{:S(2)}) %collective-permute-start.14) | collective-permute-done | bytes 81952 | tf_op jit(solution)/shard_map/ppermute | solution.py:19
  46.0 1.0 %dx.1 = (bf16[80,768]{1,0:T(8,128)(2,1)S(1)}, bf16[80,768]{1,0:T(8,128)(2,1)S(1)}, bf16[160,768]{1,0:T(8,128)(2,1)S(1)}, bf16[160,768]{1,0:T(8,128)(2,1)S(1)}, bf16[2,160,768]{2,1,0:T(8,128)(2,1)S(1)}) custom-call(s32[1]{0:T(128)} %bitcast.3.half_ref, bf16[2,80,1536]{2,1,0:T(8,128)(2,1)S(1)} %get-tuple-element.72.far_ref, ...), custom_call_target="tpu_custom_call" | custom-call | bytes 4816900 | tf_op jit(solution)/shard_map/dx/pallas_call | solution.py:40
  47.0 2.7 %collective-permute-start.17 = (bf16[80,768]{1,0:T(8,128)(2,1)S(1)}, bf16[80,768]{1,0:T(8,128)(2,1)S(1)}, u32[]{:S(2)}, u32[]{:S(2)}) collective-permute-start(bf16[80,768]{1,0:T(8,128)(2,1)S(1)} %get-tuple-element.86), channel_id=1, source_target_pairs={{0,8},{4,12},{8,0},{12,4},{1,9},{5,13},{9,1},{13,5},{2,10},{6,14},... | collective-permute-start | bytes 368648 | tf_op jit(solution)/shard_map/ppermute | solution.py:19
  49.7 1.6 %collective-permute-start.18 = (bf16[80,768]{1,0:T(8,128)(2,1)S(1)}, bf16[80,768]{1,0:T(8,128)(2,1)S(1)}, u32[]{:S(2)}, u32[]{:S(2)}) collective-permute-start(bf16[80,768]{1,0:T(8,128)(2,1)S(1)} %get-tuple-element.87), channel_id=1, source_target_pairs={{0,12},{4,8},{8,4},{12,0},{1,13},{5,9},{9,5},{13,1},{2,14},{6,10},... | collective-permute-start | bytes 368648 | tf_op jit(solution)/shard_map/ppermute | solution.py:19
  51.3 0.3 mix.1.far_ref
  51.7 1.2 %near.1 = (bf16[80,768]{1,0:T(8,128)(2,1)S(1)}, bf16[80,768]{1,0:T(8,128)(2,1)S(1)}, bf16[80,768]{1,0:T(8,128)(2,1)S(1)}, bf16[80,768]{1,0:T(8,128)(2,1)S(1)}, b...) custom-call(s32[1]{0:T(128)} %bitcast.3.half_ref, ...), custom_call_target="tpu_custom_call" | custom-call | bytes 5750788 | tf_op jit(solution)/shard_map/near/pallas_call | solution.py:40
  52.8 1.8 %collective-permute-start.22 = (bf16[80,768]{1,0:T(8,128)(2,1)S(1)}, bf16[80,768]{1,0:T(8,128)(2,1)S(1)}, u32[]{:S(2)}, u32[]{:S(2)}) collective-permute-start(bf16[80,768]{1,0:T(8,128)(2,1)S(1)} %get-tuple-element.92), channel_id=1, source_target_pairs={{0,4},{4,0},{8,12},{12,8},{1,5},{5,1},{9,13},{13,9},{2,6},{6,2},{1... | collective-permute-start | bytes 368648 | tf_op jit(solution)/shard_map/ppermute | solution.py:19
  54.6 0.3 collective-permute-start.23
  54.9 3.1 %grads.1 = (bf16[768,768]{1,0:T(8,128)(2,1)}, bf16[768,768]{1,0:T(8,128)(2,1)}, bf16[768,768]{1,0:T(8,128)(2,1)}) custom-call(bf16[80,768]{1,0:T(8,128)(2,1)S(1)} %get-tuple-element.59.refs_2_.refs_0_, bf16[80,768]{1,0:T(8,128)(2,1)S(1)} %collective-permute-done.2.refs_3_.refs_1_, bf16[80,768]{1,0:T(8,128)(2,1)S(1)} %collective-permute-done.refs_0_.refs_2_, ...), custom_call_target="tpu_custom_call" | custom-call | flops 1132462080 | bytes 5996544 | tf_op jit(solution)/shard_map/grads/pallas_call | solution.py:40
  58.0 1.4 %collective-permute-done.17.refs_0_.refs_4_ = bf16[80,768]{1,0:T(8,128)(2,1)S(1)} collective-permute-done((bf16[80,768]{1,0:T(8,128)(2,1)S(1)}, bf16[80,768]{1,0:T(8,128)(2,1)S(1)}, u32[]{:S(2)}, u32[]{:S(2)}) %collective-permute-start.17) | collective-permute-done | bytes 122912 | tf_op jit(solution)/shard_map/ppermute | solution.py:19
  59.4 0.2 far.1.far_grad_ref
  59.7 2.0 %collective-permute-done.22.refs_1_ = bf16[80,768]{1,0:T(8,128)(2,1)S(1)} collective-permute-done((bf16[80,768]{1,0:T(8,128)(2,1)S(1)}, bf16[80,768]{1,0:T(8,128)(2,1)S(1)}, u32[]{:S(2)}, u32[]{:S(2)}) %collective-permute-start.22) | collective-permute-done | bytes 122912 | tf_op jit(solution)/shard_map/ppermute | solution.py:19
  61.7 2.4 %collective-permute-done.23.refs_3_ = bf16[80,768]{1,0:T(8,128)(2,1)S(1)} collective-permute-done((bf16[80,768]{1,0:T(8,128)(2,1)S(1)}, bf16[80,768]{1,0:T(8,128)(2,1)S(1)}, u32[]{:S(2)}, u32[]{:S(2)}) %collective-permute-start.23) | collective-permute-done | bytes 122912 | tf_op jit(solution)/shard_map/ppermute | solution.py:19
  64.1 1.1 %merge.1 = (bf16[128,768]{1,0:T(8,128)(2,1)}, bf16[128,768]{1,0:T(8,128)(2,1)}, f32[2,128]{1,0:T(2,128)}) custom-call(s32[1]{0:T(128)} %bitcast.me_ref, s32[2,128]{1,0:T(2,128)S(1)} %bitcast.17, f32[2,128]{1,0:T(2,128)S(1)} %bitcast.20, bf16[320,128]{1,0:T(8,128)(2,1)S(1)} %get-tuple-element.56.place_ref, f32[128,768]{1,0:T(8,128)S(1)} %mix.1.far_ref, ...), custom_call_target="tpu_custom_call" | custom-call | flops 125829120 | bytes 2001924 | tf_op jit(solution)/shard_map/merge/pallas_call | solution.py:40
  (38 shorter events, 1.1 us)
Async XLA Ops:
  0.6 0.7 %copy-start.4 = (s32[128,2]{0,1:T(2,128)S(1)}, s32[128,2]{0,1:T(2,128)}, u32[]{:S(2)}) copy-start(s32[128,2]{0,1:T(2,128)} %param.9) | copy-start | bytes 3076
  1.3 0.9 %copy-start.9 = (bf16[128,768]{1,0:T(8,128)(2,1)S(1)}, bf16[128,768]{1,0:T(8,128)(2,1)}, u32[]{:S(2)}) copy-start(bf16[128,768]{1,0:T(8,128)(2,1)} %tokens_ref.1) | copy-start | bytes 589828
  2.7 13.6 %collective-permute-start = (bf16[80,768]{1,0:T(8,128)(2,1)S(1)}, bf16[80,768]{1,0:T(8,128)(2,1)S(1)}, u32[]{:S(2)}, u32[]{:S(2)}) collective-permute-start(bf16[80,768]{1,0:T(8,128)(2,1)S(1)} %get-tuple-element.57), channel_id=1, source_target_pairs={{0,8},{4,12},{8,0},{12,4},{1,9},{5,13},{9,1},{13,5},{2,10},{6,14},... | collective-permute-start | bytes 368648 | tf_op jit(solution)/shard_map/ppermute | solution.py:19
  6.8 9.5 %collective-permute-start.1 = (bf16[80,768]{1,0:T(8,128)(2,1)S(1)}, bf16[80,768]{1,0:T(8,128)(2,1)S(1)}, u32[]{:S(2)}, u32[]{:S(2)}) collective-permute-start(bf16[80,768]{1,0:T(8,128)(2,1)S(1)} %get-tuple-element.58), channel_id=1, source_target_pairs={{0,12},{4,8},{8,4},{12,0},{1,13},{5,9},{9,5},{13,1},{2,14},{6,10},... | collective-permute-start | bytes 368648 | tf_op jit(solution)/shard_map/ppermute | solution.py:19
  8.1 8.6 %collective-permute-start.2 = (bf16[80,768]{1,0:T(8,128)(2,1)S(1)}, bf16[80,768]{1,0:T(8,128)(2,1)S(1)}, u32[]{:S(2)}, u32[]{:S(2)}) collective-permute-start(bf16[80,768]{1,0:T(8,128)(2,1)S(1)} %get-tuple-element.60), channel_id=1, source_target_pairs={{0,4},{4,0},{8,12},{12,8},{1,5},{5,1},{9,13},{13,9},{2,6},{6,2},{1... | collective-permute-start | bytes 368648 | tf_op jit(solution)/shard_map/ppermute | solution.py:19
  8.3 0.9 %copy-start.3 = (bf16[128,768]{1,0:T(8,128)(2,1)S(1)}, bf16[128,768]{1,0:T(8,128)(2,1)}, u32[]{:S(2)}) copy-start(bf16[128,768]{1,0:T(8,128)(2,1)} %cot_ref.1) | copy-start | bytes 589828
  9.3 0.7 %copy-start.5 = (s32[128,2]{0,1:T(2,128)S(1)}, s32[128,2]{0,1:T(2,128)}, u32[]{:S(2)}) copy-start(s32[128,2]{0,1:T(2,128)} %param.9) | copy-start | bytes 3076
  10.0 0.7 %copy-start.7 = (f32[128,2]{0,1:T(2,128)S(1)}, f32[128,2]{0,1:T(2,128)}, u32[]{:S(2)}) copy-start(f32[128,2]{0,1:T(2,128)} %param.10) | copy-start | bytes 3076
  10.9 1.3 %copy-start = (bf16[1,768,768]{2,1,0:T(8,128)(2,1)S(1)}, bf16[1,768,768]{2,1,0:T(8,128)(2,1)}, u32[]{:S(2)}) copy-start(bf16[1,768,768]{2,1,0:T(8,128)(2,1)} %param.11) | copy-start | bytes 3538948
  12.2 1.3 %copy-start.1 = (bf16[1,768,768]{2,1,0:T(8,128)(2,1)S(1)}, bf16[1,768,768]{2,1,0:T(8,128)(2,1)}, u32[]{:S(2)}) copy-start(bf16[1,768,768]{2,1,0:T(8,128)(2,1)} %param.12) | copy-start | bytes 3538948
  13.5 1.3 %copy-start.2 = (bf16[1,768,768]{2,1,0:T(8,128)(2,1)S(1)}, bf16[1,768,768]{2,1,0:T(8,128)(2,1)}, u32[]{:S(2)}) copy-start(bf16[1,768,768]{2,1,0:T(8,128)(2,1)} %param.13) | copy-start | bytes 3538948
  18.2 4.7 %collective-permute-start.3 = (bf16[80,1536]{1,0:T(8,128)(2,1)S(1)}, bf16[80,1536]{1,0:T(8,128)(2,1)S(1)}, u32[]{:S(2)}, u32[]{:S(2)}) collective-permute-start(bf16[80,1536]{1,0:T(8,128)(2,1)S(1)} %get-tuple-element.68), channel_id=1, source_target_pairs={{0,1},{1,0},{2,3},{3,2},{4,5},{5,4},{6,7},{7,6},{8,9},{9,8},{10,11... | collective-permute-start | bytes 737288 | tf_op jit(solution)/shard_map/ppermute | solution.py:19
  18.3 13.5 %collective-permute-start.9 = (bf16[80,768]{1,0:T(8,128)(2,1)S(1)}, bf16[80,768]{1,0:T(8,128)(2,1)S(1)}, u32[]{:S(2)}, u32[]{:S(2)}) collective-permute-start(bf16[80,768]{1,0:T(8,128)(2,1)S(1)} %get-tuple-element.76), channel_id=1, source_target_pairs={{0,8},{4,12},{8,0},{12,4},{1,9},{5,13},{9,1},{13,5},{2,10},{6,14},... | collective-permute-start | bytes 368648 | tf_op jit(solution)/shard_map/ppermute | solution.py:19
  22.3 9.5 %collective-permute-start.10 = (bf16[80,768]{1,0:T(8,128)(2,1)S(1)}, bf16[80,768]{1,0:T(8,128)(2,1)S(1)}, u32[]{:S(2)}, u32[]{:S(2)}) collective-permute-start(bf16[80,768]{1,0:T(8,128)(2,1)S(1)} %get-tuple-element.77), channel_id=1, source_target_pairs={{0,12},{4,8},{8,4},{12,0},{1,13},{5,9},{9,5},{13,1},{2,14},{6,10},... | collective-permute-start | bytes 368648 | tf_op jit(solution)/shard_map/ppermute | solution.py:19
  22.7 10.1 %collective-permute-start.11 = (bf16[80,768]{1,0:T(8,128)(2,1)S(1)}, bf16[80,768]{1,0:T(8,128)(2,1)S(1)}, u32[]{:S(2)}, u32[]{:S(2)}) collective-permute-start(bf16[80,768]{1,0:T(8,128)(2,1)S(1)} %get-tuple-element.78), channel_id=1, source_target_pairs={{0,4},{4,0},{8,12},{12,8},{1,5},{5,1},{9,13},{13,9},{2,6},{6,2},{1... | collective-permute-start | bytes 368648 | tf_op jit(solution)/shard_map/ppermute | solution.py:19
  22.9 1.6 %collective-permute-start.8 = (bf16[80,1536]{1,0:T(8,128)(2,1)S(1)}, bf16[80,1536]{1,0:T(8,128)(2,1)S(1)}, u32[]{:S(2)}, u32[]{:S(2)}) collective-permute-start(bf16[80,1536]{1,0:T(8,128)(2,1)S(1)} %get-tuple-element.75), channel_id=1, source_target_pairs={{0,1},{1,0},{2,3},{3,2},{4,5},{5,4},{6,7},{7,6},{8,9},{9,8},{10,11... | collective-permute-start | bytes 737288 | tf_op jit(solution)/shard_map/ppermute | solution.py:19
  23.0 10.6 %collective-permute-start.4 = (bf16[80,1536]{1,0:T(8,128)(2,1)S(1)}, bf16[80,1536]{1,0:T(8,128)(2,1)S(1)}, u32[]{:S(2)}, u32[]{:S(2)}) collective-permute-start(bf16[80,1536]{1,0:T(8,128)(2,1)S(1)} %add_convert_fusion.3), channel_id=1, source_target_pairs={{0,2},{1,3},{2,0},{3,1},{4,6},{5,7},{6,4},{7,5},{8,10},{9,11},{10,... | collective-permute-start | bytes 737288 | tf_op jit(solution)/shard_map/ppermute | solution.py:19
  24.6 15.2 %collective-permute-start.19 = (bf16[80,1536]{1,0:T(8,128)(2,1)S(1)}, bf16[80,1536]{1,0:T(8,128)(2,1)S(1)}, u32[]{:S(2)}, u32[]{:S(2)}) collective-permute-start(bf16[80,1536]{1,0:T(8,128)(2,1)S(1)} %add_convert_fusion.1), channel_id=1, source_target_pairs={{0,2},{1,3},{2,0},{3,1},{4,6},{5,7},{6,4},{7,5},{8,10},{9,11},{10,... | collective-permute-start | bytes 737288 | tf_op jit(solution)/shard_map/ppermute | solution.py:19
  33.5 1.6 %collective-permute-start.12 = (bf16[160,768]{1,0:T(8,128)(2,1)S(1)}, bf16[160,768]{1,0:T(8,128)(2,1)S(1)}, u32[]{:S(2)}, u32[]{:S(2)}) collective-permute-start(bf16[160,768]{1,0:T(8,128)(2,1)S(1)} %get-tuple-element.84), channel_id=1, source_target_pairs={{0,1},{1,0},{2,3},{3,2},{4,5},{5,4},{6,7},{7,6},{8,9},{9,8},{10,11... | collective-permute-start | bytes 737288 | tf_op jit(solution)/shard_map/ppermute | solution.py:19
  33.6 3.1 %collective-permute-start.5 = (bf16[80,1536]{1,0:T(8,128)(2,1)S(1)}, bf16[80,1536]{1,0:T(8,128)(2,1)S(1)}, u32[]{:S(2)}, u32[]{:S(2)}) collective-permute-start(bf16[80,1536]{1,0:T(8,128)(2,1)S(1)} %add_convert_fusion.2.mine_ref), channel_id=1, source_target_pairs={{0,1},{1,0},{2,3},{3,2},{4,5},{5,4},{6,7},{7,6},{8,9},{9,8},{10,11... | collective-permute-start | bytes 737288 | tf_op jit(solution)/shard_map/ppermute | solution.py:19
  35.1 8.1 %collective-permute-start.13 = (bf16[160,768]{1,0:T(8,128)(2,1)S(1)}, bf16[160,768]{1,0:T(8,128)(2,1)S(1)}, u32[]{:S(2)}, u32[]{:S(2)}) collective-permute-start(bf16[160,768]{1,0:T(8,128)(2,1)S(1)} %add_convert_fusion), channel_id=1, source_target_pairs={{0,2},{1,3},{2,0},{3,1},{4,6},{5,7},{6,4},{7,5},{8,10},{9,11},{10,... | collective-permute-start | bytes 737288 | tf_op jit(solution)/shard_map/ppermute | solution.py:19
  37.1 14.2 %collective-permute-start.6 = (bf16[80,768]{1,0:T(8,128)(2,1)S(1)}, bf16[80,768]{1,0:T(8,128)(2,1)S(1)}, u32[]{:S(2)}, u32[]{:S(2)}) collective-permute-start(bf16[80,768]{1,0:T(8,128)(2,1)S(1)} %get-tuple-element.70), channel_id=1, source_target_pairs={{0,8},{4,12},{8,0},{12,4},{1,9},{5,13},{9,1},{13,5},{2,10},{6,14},... | collective-permute-start | bytes 368648 | tf_op jit(solution)/shard_map/ppermute | solution.py:19
  39.8 9.9 %collective-permute-start.7 = (bf16[80,768]{1,0:T(8,128)(2,1)S(1)}, bf16[80,768]{1,0:T(8,128)(2,1)S(1)}, u32[]{:S(2)}, u32[]{:S(2)}) collective-permute-start(bf16[80,768]{1,0:T(8,128)(2,1)S(1)} %get-tuple-element.71), channel_id=1, source_target_pairs={{0,12},{4,8},{8,4},{12,0},{1,13},{5,9},{9,5},{13,1},{2,14},{6,10},... | collective-permute-start | bytes 368648 | tf_op jit(solution)/shard_map/ppermute | solution.py:19
  43.2 1.3 %collective-permute-start.16 = (bf16[160,256]{1,0:T(8,128)(2,1)S(1)}, bf16[160,256]{1,0:T(8,128)(2,1)S(1)}, u32[]{:S(2)}, u32[]{:S(2)}) collective-permute-start(bf16[160,256]{1,0:T(8,128)(2,1)S(1)} %get-tuple-element.108.refs_2_), channel_id=1, source_target_pairs={{0,1},{1,0},{2,3},{3,2},{4,5},{5,4},{6,7},{7,6},{8,9},{9,8},{10,11... | collective-permute-start | bytes 245768 | tf_op jit(solution)/shard_map/ppermute | solution.py:19
  43.3 1.4 %collective-permute-start.15 = (bf16[160,256]{1,0:T(8,128)(2,1)S(1)}, bf16[160,256]{1,0:T(8,128)(2,1)S(1)}, u32[]{:S(2)}, u32[]{:S(2)}) collective-permute-start(bf16[160,256]{1,0:T(8,128)(2,1)S(1)} %get-tuple-element.109.refs_1_), channel_id=1, source_target_pairs={{0,1},{1,0},{2,3},{3,2},{4,5},{5,4},{6,7},{7,6},{8,9},{9,8},{10,11... | collective-permute-start | bytes 245768 | tf_op jit(solution)/shard_map/ppermute | solution.py:19
  43.9 7.8 %collective-permute-start.21 = (bf16[80,768]{1,0:T(8,128)(2,1)S(1)}, bf16[80,768]{1,0:T(8,128)(2,1)S(1)}, u32[]{:S(2)}, u32[]{:S(2)}) collective-permute-start(bf16[80,768]{1,0:T(8,128)(2,1)S(1)} %get-tuple-element.106.refs_1_), channel_id=1, source_target_pairs={{0,1},{1,0},{2,3},{3,2},{4,5},{5,4},{6,7},{7,6},{8,9},{9,8},{10,11... | collective-permute-start | bytes 368648 | tf_op jit(solution)/shard_map/ppermute | solution.py:19
  44.6 7.1 %collective-permute-start.20 = (bf16[80,768]{1,0:T(8,128)(2,1)S(1)}, bf16[80,768]{1,0:T(8,128)(2,1)S(1)}, u32[]{:S(2)}, u32[]{:S(2)}) collective-permute-start(bf16[80,768]{1,0:T(8,128)(2,1)S(1)} %get-tuple-element.107.refs_0_), channel_id=1, source_target_pairs={{0,1},{1,0},{2,3},{3,2},{4,5},{5,4},{6,7},{7,6},{8,9},{9,8},{10,11... | collective-permute-start | bytes 368648 | tf_op jit(solution)/shard_map/ppermute | solution.py:19
  44.7 1.3 %collective-permute-start.14 = (bf16[160,256]{1,0:T(8,128)(2,1)S(1)}, bf16[160,256]{1,0:T(8,128)(2,1)S(1)}, u32[]{:S(2)}, u32[]{:S(2)}) collective-permute-start(bf16[160,256]{1,0:T(8,128)(2,1)S(1)} %get-tuple-element.110.refs_0_), channel_id=1, source_target_pairs={{0,1},{1,0},{2,3},{3,2},{4,5},{5,4},{6,7},{7,6},{8,9},{9,8},{10,11... | collective-permute-start | bytes 245768 | tf_op jit(solution)/shard_map/ppermute | solution.py:19
  46.0 5.3 %copy-start.6 = (s32[128,2]{0,1:T(2,128)S(1)}, s32[128,2]{0,1:T(2,128)}, u32[]{:S(2)}) copy-start(s32[128,2]{0,1:T(2,128)} %param.9) | copy-start | bytes 3076
  46.0 5.3 %copy-start.8 = (f32[128,2]{0,1:T(2,128)S(1)}, f32[128,2]{0,1:T(2,128)}, u32[]{:S(2)}) copy-start(f32[128,2]{0,1:T(2,128)} %param.10) | copy-start | bytes 3076
  47.0 12.4 %collective-permute-start.17 = (bf16[80,768]{1,0:T(8,128)(2,1)S(1)}, bf16[80,768]{1,0:T(8,128)(2,1)S(1)}, u32[]{:S(2)}, u32[]{:S(2)}) collective-permute-start(bf16[80,768]{1,0:T(8,128)(2,1)S(1)} %get-tuple-element.86), channel_id=1, source_target_pairs={{0,8},{4,12},{8,0},{12,4},{1,9},{5,13},{9,1},{13,5},{2,10},{6,14},... | collective-permute-start | bytes 368648 | tf_op jit(solution)/shard_map/ppermute | solution.py:19
  49.7 9.7 %collective-permute-start.18 = (bf16[80,768]{1,0:T(8,128)(2,1)S(1)}, bf16[80,768]{1,0:T(8,128)(2,1)S(1)}, u32[]{:S(2)}, u32[]{:S(2)}) collective-permute-start(bf16[80,768]{1,0:T(8,128)(2,1)S(1)} %get-tuple-element.87), channel_id=1, source_target_pairs={{0,12},{4,8},{8,4},{12,0},{1,13},{5,9},{9,5},{13,1},{2,14},{6,10},... | collective-permute-start | bytes 368648 | tf_op jit(solution)/shard_map/ppermute | solution.py:19
  52.8 8.8 %collective-permute-start.22 = (bf16[80,768]{1,0:T(8,128)(2,1)S(1)}, bf16[80,768]{1,0:T(8,128)(2,1)S(1)}, u32[]{:S(2)}, u32[]{:S(2)}) collective-permute-start(bf16[80,768]{1,0:T(8,128)(2,1)S(1)} %get-tuple-element.92), channel_id=1, source_target_pairs={{0,4},{4,0},{8,12},{12,8},{1,5},{5,1},{9,13},{13,9},{2,6},{6,2},{1... | collective-permute-start | bytes 368648 | tf_op jit(solution)/shard_map/ppermute | solution.py:19
  54.6 9.5 %collective-permute-start.23 = (bf16[80,768]{1,0:T(8,128)(2,1)S(1)}, bf16[80,768]{1,0:T(8,128)(2,1)S(1)}, u32[]{:S(2)}, u32[]{:S(2)}) collective-permute-start(bf16[80,768]{1,0:T(8,128)(2,1)S(1)} %get-tuple-element.94), channel_id=1, source_target_pairs={{0,4},{4,0},{8,12},{12,8},{1,5},{5,1},{9,13},{13,9},{2,6},{6,2},{1... | collective-permute-start | bytes 368648 | tf_op jit(solution)/shard_map/ppermute | solution.py:19
